TPU v7x, 256 devices: a whole 4x4x8 slice. The times are simulated.
256 devices in a mesh: island: 4 (over y_hi, core), fsdp: 64 (over z, x, y_lo).
Axes of the slice: x: 4, y: 4 (y_hi: 2, y_lo: 2; y = y_hi * 2 + y_lo), z: 8, core: 2. Of those that a mesh axis runs over, the one named last changes fastest.
Arguments:
- tokens: bfloat16 [4, 16384, 8192], P('island', 'fsdp'), may hold values from -6 to 6
- cotangent: bfloat16 [4, 16384, 512], P('island', 'fsdp'), may hold values from -6 to 6
- key_weight: bfloat16 [4, 8192, 512], P('island', 'fsdp'), may hold values from -0.0625 to 0.0625
- quant_codes: int32 [4, 1024, 8192], P('island', 'fsdp'), may hold values from 0 to 15
- zero_points: int32 [4, 1024, 64], P('island', 'fsdp'), may hold values from 0 to 15
- minima: float32 [4, 1024, 64], P('island', 'fsdp'), may hold values from -0.5 to 0.5
- quant_steps: float32 [4, 1024, 64], P('island', 'fsdp'), may hold values from 0.01 to 0.1
- momentum: float32 [1024, 8192], P('fsdp'), may hold values from -4 to 4
- params: float32 [1024, 8192], P('fsdp'), may hold values from -6 to 6
Outputs:
- projected: bfloat16 [4, 16384, 512], P('island', 'fsdp')
- token_grad: bfloat16 [4, 16384, 8192], P('island', 'fsdp')
- weight_grad: float32 [4, 8192, 512], P('island', 'fsdp')
- new_momentum: float32 [1024, 8192], P('fsdp')
- new_params: float32 [1024, 8192], P('fsdp')
All inputs are finite; a program needn't handle non-finite values.
Results may differ from a plain program's by a relative error of at most 0.0054.
Values may be sent and summed in bfloat16 or wider, within the bound.
No kernel may reach another device: no remote copies, remote signals or barrier semaphores. Data moves between devices by JAX's collectives and lax.ppermute only.
A program may use at most 128 MiB of HBM per device.

v0:
```python
import math

import jax
import jax.numpy as jnp
from jax import lax
from jax.sharding import PartitionSpec as P

GROUP = 128


def dequantize(quant_codes, zero_points, minima, quant_steps):
    shape = quant_codes.shape
    grouped = quant_codes.reshape(shape[:-1] + (shape[-1] // GROUP, GROUP))
    offset = (grouped - zero_points[..., None]).astype(jnp.float32)
    values = quant_steps[..., None] * offset + minima[..., None]
    return values.reshape(shape)


def local(
    tokens, cotangent, key_weight, quant_codes, zero_points, minima, quant_steps, momentum, params
):
    inputs = tokens[0]
    cot_rows = cotangent[0]
    weight = key_weight[0]
    island_tok = inputs.shape[0] * lax.axis_size("fsdp")
    scaling = 1.0 / math.sqrt(island_tok)
    piece = lax.all_gather(weight, "fsdp", axis=0, tiled=True)
    columns = inputs
    keys_acc = jnp.dot(columns, piece, preferred_element_type=jnp.float32)
    back_part = lax.dot_general(
        cot_rows, piece, (((1,), (1,)), ((), ())), preferred_element_type=jnp.float32
    )
    back_acc = back_part.astype(jnp.bfloat16)
    projected = keys_acc.astype(jnp.bfloat16)
    columns = inputs
    grad = lax.psum_scatter(
        lax.dot_general(
            columns, cot_rows, (((0,), (0,)), ((), ())), preferred_element_type=jnp.float32
        ),
        "fsdp",
        scatter_dimension=0,
        tiled=True,
    )
    weight_grad = grad * scaling
    values = dequantize(quant_codes[0], zero_points[0], minima[0], quant_steps[0])
    replicas = lax.axis_size("island")
    summed = lax.psum(values.astype(jnp.bfloat16), "island").astype(jnp.float32)
    delta = summed / replicas
    new_momentum = 0.9 * momentum + delta
    new_params = params - 0.7 * (delta + 0.9 * new_momentum)
    return (projected[None], back_acc[None], weight_grad[None], new_momentum, new_params)


def solution(mesh):
    placed = (
        P("island", "fsdp", None),
        P("island", "fsdp", None),
        P("island", "fsdp", None),
        P("island", "fsdp", None),
        P("island", "fsdp", None),
        P("island", "fsdp", None),
        P("island", "fsdp", None),
        P("fsdp", None),
        P("fsdp", None),
    )
    return jax.shard_map(
        local,
        mesh=mesh,
        in_specs=placed,
        out_specs=(
            P("island", "fsdp", None),
            P("island", "fsdp", None),
            P("island", "fsdp", None),
            P("fsdp", None),
            P("fsdp", None),
        ),
        check_vma=False,
    )
```

profile of v0, /device:TPU:16, one launch (start us, length us, event | category | flops | bytes accessed | tf_op | source)
XLA Modules:
  0.0 713.3 jit_solution(9034087799165758792)
XLA Ops:
  8.0 0.0 copy-start
  8.0 0.0 all-reduce.2.cloned.1.call-start
  8.1 0.9 add.24
  9.0 0.9 sub.17
  9.9 0.9 mul.35
  10.8 2.6 fusion.17
  13.4 0.0 all-reduce.2.cloned.1.call-update
  13.4 0.0 all-gather.3.cloned.1.call-start
  13.5 0.5 all-gather.3.cloned.1.call-update
  14.0 0.0 reduce-scatter.2.cloned.1.call-start
  14.0 0.0 copy-done
  14.1 10.3 %fusion.4 = f32[8192,512]{1,0:T(8,128)} fusion(bf16[1,256,8192]{2,1,0:T(8,128)(2,1)} %param.9, bf16[1,256,512]{2,1,0:T(8,128)(2,1)S(1)} %copy-done), kind=kOutput, calls=%fused_computation.5 | convolution fusion | flops 2147483648 | bytes 21233664 | tf_op jit(solution)/shard_map/dot_general | solution.py:37
  24.4 0.0 copy-start.3
  24.4 0.0 copy-start.4
  24.4 0.0 reduce-scatter.2.cloned.1.call-update
  24.4 40.3 %all-reduce.2.cloned.1.call-done = bf16[16,8192]{1,0:T(8,128)(2,1)} async-done(((bf16[16,8192]{1,0:T(8,128)(2,1)}), bf16[16,8192]{1,0:T(8,128)(2,1)}) %all-reduce.2.cloned.1.call-update) | async-done | bytes 262160 | tf_op jit(solution)/shard_map/psum | solution.py:47
  64.7 0.0 copy-done.3
  64.7 0.0 copy-done.4
  64.7 2.1 multiply_subtract_fusion
  66.7 266.0 %all-gather.3.cloned.1.call-done = bf16[1,8192,512]{2,1,0:T(8,128)(2,1)} async-done(((bf16[1,128,512]{2,1,0:T(8,128)(2,1)}), bf16[1,8192,512]{2,1,0:T(8,128)(2,1)}) %all-gather.3.cloned.1.call-update) | async-done | bytes 8388624 | tf_op jit(solution)/shard_map/all_gather | solution.py:27
  332.7 0.0 copy-start.1
  332.7 0.0 copy-start.2
  332.7 7.9 %fusion = bf16[1,256,8192]{2,1,0:T(8,128)(2,1)} fusion(bf16[1,8192,512]{2,1,0:T(8,128)(2,1)} %all-gather.3.cloned.1.call-done, bf16[1,256,512]{2,1,0:T(8,128)(2,1)S(1)} %copy-done), kind=kOutput, calls=%fused_computation.1 | convolution fusion | flops 2149580800 | bytes 12845056 | tf_op jit(solution)/shard_map/dot_general | solution.py:30
  340.6 0.0 copy-done.1
  340.6 0.0 copy-done.2
  340.6 3.0 fusion.12
  343.7 360.5 %reduce-scatter.2.cloned.1.call-done = f32[128,512]{1,0:T(8,128)} async-done(((f32[8192,512]{1,0:T(8,128)}), f32[128,512]{1,0:T(8,128)}) %reduce-scatter.2.cloned.1.call-update) | async-done | bytes 262160 | tf_op jit(solution)/shard_map/reduce_scatter | solution.py:36
  704.2 1.7 multiply_bitcast_fusion
Async XLA Ops:
  8.0 6.0 copy-start
  8.0 56.6 %all-reduce.2.cloned.1.call-start = ((), (), s32[]{:S(2)}) async-start(), calls=%async_computation.2 | async-start | bytes 524288 | tf_op jit(solution)/shard_map/psum | solution.py:47
  13.4 319.3 %all-gather.3.cloned.1.call-start = ((), (), s32[]{:S(2)}) async-start(), calls=%async_computation.3 | async-start | bytes 8519680 | tf_op jit(solution)/shard_map/all_gather | solution.py:27
  14.0 690.2 %reduce-scatter.2.cloned.1.call-start = ((), (), s32[]{:S(2)}) async-start(), calls=%async_computation.1 | async-start | bytes 17039360 | tf_op jit(solution)/shard_map/reduce_scatter | solution.py:36
  24.4 40.3 %copy-start.3 = (f32[16,8192]{1,0:T(8,128)S(1)}, f32[16,8192]{1,0:T(8,128)}, u32[]{:S(2)}) copy-start(f32[16,8192]{1,0:T(8,128)} %param.17) | copy-start | bytes 1572868
  24.4 40.3 %copy-start.4 = (f32[16,8192]{1,0:T(8,128)S(1)}, f32[16,8192]{1,0:T(8,128)}, u32[]{:S(2)}) copy-start(f32[16,8192]{1,0:T(8,128)} %param.16) | copy-start | bytes 1572868
  332.7 7.9 %copy-start.1 = (bf16[1,8192,512]{2,1,0:T(8,128)(2,1)S(1)}, bf16[1,8192,512]{2,1,0:T(8,128)(2,1)}, u32[]{:S(2)}) copy-start(bf16[1,8192,512]{2,1,0:T(8,128)(2,1)} %all-gather.3.cloned.1.call-done) | copy-start | bytes 25165828
  332.7 7.9 %copy-start.2 = (bf16[1,256,8192]{2,1,0:T(8,128)(2,1)S(1)}, bf16[1,256,8192]{2,1,0:T(8,128)(2,1)}, u32[]{:S(2)}) copy-start(bf16[1,256,8192]{2,1,0:T(8,128)(2,1)} %param.9) | copy-start | bytes 12582916
Sparse Core Ops, SparseCore 0:
  13.5 51.0 all-reduce.1
Sparse Core Ops, SparseCore 1:
  15.7 317.0 all-gather.2
  335.1 369.0 reduce-scatter.1
where the time goes:
time: 714 us; the launch traced here: 713 us
  waiting for transfers between devices  667 us (93%)
  matrix products  21.3 us (3%)
  between operations  15.5 us (2%)
    reduce_scatter x1, waiting for transfers between devices, local(): lax.psum_scatter(lax.dot_general(columns, cot_rows, (((0,), (0,)), ((), (...  361 us
    all_gather x1, waiting for transfers between devices, local(): piece = lax.all_gather(weight, 'fsdp', axis=0, tiled=True)  266 us
    psum x1, waiting for transfers between devices, local(): summed = lax.psum(values.astype(jnp.bfloat16), 'island').astype(jnp.float32)  40.3 us
  transfers between devices with their start and end apart: 3, of which 3 were waited for; matrix products, arithmetic and copies ran while one was open for 3% of the time, Pallas kernels for 0%

commit v1 on v0

v1 whole, which is shorter than its diff:
```python
import math

import jax
import jax.numpy as jnp
from jax import lax
from jax.experimental import pallas as pl
from jax.experimental.pallas import tpu as pltpu
from jax.sharding import Mesh
from jax.sharding import PartitionSpec as P

GROUP = 128
Z, X, Y = 8, 4, 2
WEIGHT_SPLIT = 256
GRAD_SPLIT = 384
F32, BF16 = jnp.float32, jnp.bfloat16
VMEM_LIMIT = 56 * 1024 * 1024


def dequantize(quant_codes, zero_points, minima, quant_steps):
    shape = quant_codes.shape
    grouped = quant_codes.reshape(shape[:-1] + (shape[-1] // GROUP, GROUP))
    offset = (grouped - zero_points[..., None]).astype(F32)
    values = quant_steps[..., None] * offset + minima[..., None]
    return values.reshape(shape)


def shift(block, axis, by):
    size = lax.axis_size(axis)
    return lax.ppermute(block, axis, [(i, (i + by) % size) for i in range(size)])


def after(value, *earlier):
    return lax.optimization_barrier((value, *earlier))[0]


def outer_values(quant_codes, zero_points, minima, quant_steps):
    values = dequantize(quant_codes, zero_points, minima, quant_steps).astype(BF16)
    core = shift(values, "c", 1)
    far = shift(values, "yh", 1)
    far_core = lax.ppermute(values, ("yh", "c"), [(i, 3 - i) for i in range(4)])
    return values, core, far, far_core


def outer_step(exchanged, momentum, params):
    values, core, far, far_core = (v.astype(F32) for v in exchanged)
    delta = ((values + core) + (far + far_core)) / 4
    new_momentum = 0.9 * momentum + delta
    new_params = params - 0.7 * (delta + 0.9 * new_momentum)
    return new_momentum, new_params


def grad_kernel(
    place, tokens, cot, grad_a, keep, send, columns, cot_rows, cot_turned, a, kept, sent, sems
):
    part = kept.shape[3]
    load = pltpu.make_async_copy(cot, cot_rows, sems.at[0, Z])
    load.start()
    loads = []
    for j in range(Z):
        width = columns.shape[2]
        at = pl.multiple_of(lax.rem(place[0] + j, Z) * width, width)
        loads.append(
            pltpu.make_async_copy(tokens.at[:, pl.ds(at, width)], columns.at[j], sems.at[0, j])
        )
        loads[j].start()
    load.wait()
    cot_turned[...] = cot_rows[...].T
    first = place[2] == 0
    stores = []
    for j in range(Z):
        loads[j].wait()
        for k in range(X):
            grad = jnp.dot(
                cot_turned[...],
                columns[j, :, k * Y * part : (k + 1) * Y * part],
                preferred_element_type=F32,
            ).astype(BF16)
            a[j, k] = grad[:GRAD_SPLIT]
            lower, upper = grad[GRAD_SPLIT:, :part], grad[GRAD_SPLIT:, part:]
            kept[j, k] = jnp.where(first, lower, upper)
            sent[j, k] = jnp.where(first, upper, lower)
        own = lax.rem(place[0] + j, Z)
        for i, (buffer, out, to) in enumerate(((a, grad_a, j), (kept, keep, own), (sent, send, own))):
            store = pltpu.make_async_copy(buffer.at[j], out.at[:, to], sems.at[1 + i, j])
            store.start()
            stores.append(store)
    for store in stores:
        store.wait()


def gradients(place, tokens, cot, part):
    rows, width = tokens.shape
    heads = cot.shape[1]
    anywhere = pl.BlockSpec(memory_space=pl.ANY)
    shapes = [(GRAD_SPLIT, Y * part), (heads - GRAD_SPLIT, part), (heads - GRAD_SPLIT, part)]
    return pl.pallas_call(
        grad_kernel,
        in_specs=[pl.BlockSpec(memory_space=pltpu.SMEM), anywhere, anywhere],
        out_specs=[anywhere] * 3,
        out_shape=[jax.ShapeDtypeStruct((X, Z) + shape, BF16) for shape in shapes],
        scratch_shapes=[
            pltpu.VMEM((Z, rows, width // Z), BF16),
            pltpu.VMEM((rows, heads), BF16),
            pltpu.VMEM((heads, rows), BF16),
        ]
        + [pltpu.VMEM((Z, X) + shape, BF16) for shape in shapes]
        + [pltpu.SemaphoreType.DMA((4, Z + 1))],
        compiler_params=pltpu.CompilerParams(vmem_limit_bytes=VMEM_LIMIT),
        cost_estimate=pl.CostEstimate(
            flops=2 * rows * width * heads,
            bytes_accessed=2 * width * (rows + heads),
            transcendentals=0,
        ),
    )(place, tokens, cot)


def product_kernel(place, tokens, cot, weight_a, weight_c, other_c, keys, back, total):
    j = pl.program_id(0)
    part = weight_c.shape[2]
    first = place[2] == 0
    added = None
    for k in range(X):
        columns = slice(k * Y * part, (k + 1) * Y * part)
        at = lax.rem(k - place[1] + X, X)
        mine, theirs = weight_c[0, at], other_c[0, at]
        right = jnp.concatenate(
            [jnp.where(first, mine, theirs), jnp.where(first, theirs, mine)], axis=0
        )
        weight = jnp.concatenate([weight_a[0, at], right], axis=1)
        product = jnp.dot(tokens[:, columns], weight, preferred_element_type=F32)
        added = product if added is None else added + product
        back[:, columns] = lax.dot_general(
            cot[...], weight, (((1,), (1,)), ((), ())), preferred_element_type=F32
        ).astype(BF16)

    @pl.when(j == 0)
    def _():
        total[...] = added

    @pl.when(j > 0)
    def _():
        total[...] += added

    @pl.when(j == Z - 1)
    def _():
        keys[...] = total[...].astype(BF16)


def products(place, tokens, cot, weight_a, weight_c, other_c):
    rows, width = tokens.shape
    heads = cot.shape[1]
    part = weight_c.shape[2]
    by_z = lambda j, place: (j, 0, 0, 0)
    return pl.pallas_call(
        product_kernel,
        grid_spec=pltpu.PrefetchScalarGridSpec(
            num_scalar_prefetch=1,
            grid=(Z,),
            in_specs=[
                pl.BlockSpec((rows, width // Z), lambda j, place: (0, j)),
                pl.BlockSpec((rows, heads), lambda j, place: (0, 0)),
                pl.BlockSpec((1, X, Y * part, WEIGHT_SPLIT), by_z),
                pl.BlockSpec((1, X, part, heads - WEIGHT_SPLIT), by_z),
                pl.BlockSpec((1, X, part, heads - WEIGHT_SPLIT), by_z),
            ],
            out_specs=[
                pl.BlockSpec((rows, heads), lambda j, place: (0, 0)),
                pl.BlockSpec((rows, width // Z), lambda j, place: (0, j)),
            ],
            scratch_shapes=[pltpu.VMEM((rows, heads), F32)],
        ),
        out_shape=[
            jax.ShapeDtypeStruct((rows, heads), BF16),
            jax.ShapeDtypeStruct((rows, width), BF16),
        ],
        compiler_params=pltpu.CompilerParams(vmem_limit_bytes=VMEM_LIMIT),
        cost_estimate=pl.CostEstimate(
            flops=4 * rows * width * heads,
            bytes_accessed=4 * width * (rows + heads // 2),
            transcendentals=0,
        ),
    )(place, tokens, cot, weight_a, weight_c, other_c)


def gather_x(block):
    return jnp.stack([block] + [shift(block, "x", -k) for k in range(1, X)])


def local(
    tokens, cotangent, key_weight, quant_codes, zero_points, minima, quant_steps, momentum, params
):
    tokens, cot, weight = tokens[0], cotangent[0], key_weight[0]
    rows, width = tokens.shape
    part = weight.shape[0]
    scaling = 1.0 / math.sqrt(rows * Z * X * Y)
    z, x, y = lax.axis_index("z"), lax.axis_index("x"), lax.axis_index("yl")
    place = jnp.stack([z, x, y]).astype(jnp.int32)

    lower = weight[:, :WEIGHT_SPLIT]
    upper = shift(lower, "yl", 1)
    weight_c = gather_x(weight[:, WEIGHT_SPLIT:])
    weight_c, upper = lax.optimization_barrier((weight_c, upper))
    place = after(place, weight_c)
    weight_c = lax.all_gather(weight_c, "z")
    grad_a, keep, send = gradients(place, tokens, cot, part)

    grad_a = lax.psum_scatter(grad_a, "x", scatter_dimension=0, tiled=True)[0]
    got = shift(send, "yl", 1)
    upper = after(upper, send)
    weight_a = jnp.concatenate(
        [jnp.where(y == 0, lower, upper), jnp.where(y == 0, upper, lower)], axis=0
    )
    weight_a = gather_x(weight_a)

    got = after(got, weight_a)
    grad_c = (keep.astype(F32) + got.astype(F32)).astype(BF16)
    grad_c_x = lax.psum_scatter(grad_c, "x", scatter_dimension=0, tiled=True)[0]

    weight_c = after(weight_c, grad_c)
    weight_a = lax.all_gather(after(weight_a, weight_c), "z")
    other_c = shift(weight_c, "yl", 1)

    quant_codes = after(quant_codes[0], weight_c)
    exchanged = outer_values(quant_codes, zero_points[0], minima[0], quant_steps[0])
    new_momentum, new_params = outer_step(exchanged, momentum, params)

    grad_a = after(grad_a, new_params)
    half = GRAD_SPLIT // 2
    at = grad_a.astype(F32)
    up, down = shift(grad_a[4][:half], "z", 1), shift(grad_a[4][half:], "z", -1)
    up = jnp.concatenate([at[3][:half] + up.astype(F32), at[3][half:]]).astype(BF16)
    down = jnp.concatenate([at[5][:half], at[5][half:] + down.astype(F32)]).astype(BF16)
    up, down = shift(up, "z", 1), shift(down, "z", -1)
    up, down = (at[2] + up.astype(F32)).astype(BF16), (at[6] + down.astype(F32)).astype(BF16)
    grad_c = lax.all_to_all(after(grad_c_x, up), "z", 0, 0, tiled=True)
    up, down = shift(up, "z", 1), shift(down, "z", -1)
    up, down = (at[1] + up.astype(F32)).astype(BF16), (at[7] + down.astype(F32)).astype(BF16)
    keys, back = products(place, tokens, cot, weight_a, weight_c, other_c)
    up, down = after(up, keys, grad_c), after(down, keys, grad_c)
    up, down = shift(up, "z", 1), shift(down, "z", -1)
    grad_a = at[0] + (up.astype(F32) + down.astype(F32))
    lower, upper = grad_a[:, :part], grad_a[:, part:]
    theirs = jnp.where(y == 0, upper, lower).astype(BF16)
    mine = jnp.where(y == 0, lower, upper)
    grad_a = mine + shift(theirs, "yl", 1).astype(F32)
    grad_c = jnp.sum(grad_c.astype(F32), axis=0)
    weight_grad = jnp.concatenate([grad_a, grad_c]).T * scaling

    return keys[None], back[None], weight_grad[None], new_momentum, new_params


def solution(mesh):
    fine = Mesh(mesh.devices.reshape(2, 2, Z, X, Y), ("yh", "c", "z", "x", "yl"))
    island, fsdp = ("yh", "c"), ("z", "x", "yl")
    whole = P(island, fsdp, None)
    return jax.shard_map(
        local,
        mesh=fine,
        in_specs=(whole,) * 7 + (P(fsdp, None),) * 2,
        out_specs=(whole,) * 3 + (P(fsdp, None),) * 2,
        check_vma=False,
    )
```

time: 714 us -> 169 us (0.24)
  waiting for transfers between devices: 667 us -> 81.7 us
  starting transfers between devices: 0.12 us -> 36.8 us
  matrix products: 21.3 us -> 0 us
  Pallas kernels: 0 us -> 18.8 us
    reduce_scatter x1 -> x2, waiting for transfers between devices: 361 us -> 24.1 us  [the longest x1 18.8 us: local(): grad_a = lax.psum_scatter(grad_a, 'x', scatter_dimension=0, tiled=True)[0]]
    all_gather x1 -> x2, waiting for transfers between devices: 266 us -> 10 us  [the longest x1 10 us: local(): weight_c = lax.all_gather(weight_c, 'z')]
    ppermute x0 -> x21, waiting for transfers between devices: none -> 47.6 us  [the longest x20 47.6 us: shift(): lax.ppermute(block, axis, [(i, (i + by) % size) for i in range(size)])]
    psum x1 -> x0, waiting for transfers between devices: 40.3 us -> none  [local(): summed = lax.psum(values.astype(jnp.bfloat16), 'island').astype(jnp.float32)]
    ppermute x0 -> x21, starting transfers between devices: none -> 29.6 us  [the longest x20 29.6 us: shift(): lax.ppermute(block, axis, [(i, (i + by) % size) for i in range(size)])]
    dot_general x3 -> x0, matrix products: 21.3 us -> none  [the longest x1 10.3 us: local(): lax.dot_general(columns, cot_rows, (((0,), (0,)), ((), ())), preferred_el...]
    pallas_call x0 -> x2, Pallas kernels: none -> 18.8 us  [the longest x1 12.2 us: products(): pl.pallas_call(product_kernel, grid_spec=pltpu.PrefetchScalarGridSpec(num...]
  transfers between devices with their start and end apart: 3 -> 26, of which waited for: 3 -> 15; matrix products, arithmetic and copies ran while one was open for 3% -> 8% of each run, Pallas kernels for 0% -> 11%
where the time goes in v1:
time: 169 us
  waiting for transfers between devices  81.7 us (48%)
  starting transfers between devices  36.8 us (22%)
  Pallas kernels  18.8 us (11%)
  between operations  15.7 us (9%)
  other arithmetic  12.5 us (7%)
  local copies, waits for them, and re-layouts  3.39 us (2%)
    ppermute x20, waiting for transfers between devices, shift(): lax.ppermute(block, axis, [(i, (i + by) % size) for i in range(size)])  47.6 us
    ppermute x20, starting transfers between devices, shift(): lax.ppermute(block, axis, [(i, (i + by) % size) for i in range(size)])  29.6 us
    reduce_scatter x1, waiting for transfers between devices, local(): grad_a = lax.psum_scatter(grad_a, 'x', scatter_dimension=0, tiled=True)[0]  18.8 us
    pallas_call x1, Pallas kernels, products(): pl.pallas_call(product_kernel, grid_spec=pltpu.PrefetchScalarGridSpec(num...  12.2 us
    all_gather x1, waiting for transfers between devices, local(): weight_c = lax.all_gather(weight_c, 'z')  10 us
    all_to_all x1, starting transfers between devices, local(): grad_c = lax.all_to_all(after(grad_c_x, up), 'z', 0, 0, tiled=True)  7.01 us
    pallas_call x1, Pallas kernels, gradients(): pl.pallas_call(grad_kernel, in_specs=[pl.BlockSpec(memory_space=pltpu.SME...  6.54 us
    reduce_scatter x1, waiting for transfers between devices, local(): grad_c_x = lax.psum_scatter(grad_c, 'x', scatter_dimension=0, tiled=True)[0]  5.29 us
  transfers between devices with their start and end apart: 26, of which 15 were waited for; matrix products, arithmetic and copies ran while one was open for 8% of the time, Pallas kernels for 11%

profile of v1, /device:TPU:16, one launch (start us, length us, event | category | flops | bytes accessed | tf_op | source)
XLA Modules:
  0.0 168.9 jit_solution(15894325084153257968)
XLA Ops:
  8.0 0.0 all-gather.5.cloned.1.call-start
  8.0 0.9 fusion.18
  8.9 2.8 %collective-permute-start = (bf16[128,256]{1,0:T(8,128)(2,1)S(1)}, bf16[128,256]{1,0:T(8,128)(2,1)S(1)}, u32[]{:S(2)}, u32[]{:S(2)}) collective-permute-start(bf16[128,256]{1,0:T(8,128)(2,1)S(1)} %get-tuple-element.65), channel_id=1, source_target_pairs={{0,6},{2,0},{4,2},{6,4},{1,7},{3,1},{5,3},{7,5},{8,14},{10,8},{12,... | collective-permute-start | bytes 196616 | tf_op jit(solution)/shard_map/ppermute | solution.py:29
  11.8 0.8 collective-permute-start.1
  12.6 0.9 collective-permute-start.2
  13.5 1.3 collective-permute-start.3
  14.7 2.8 %collective-permute-done.1 = bf16[128,256]{1,0:T(8,128)(2,1)S(1)} collective-permute-done((bf16[128,256]{1,0:T(8,128)(2,1)S(1)}, bf16[128,256]{1,0:T(8,128)(2,1)S(1)}, u32[]{:S(2)}, u32[]{:S(2)}) %collective-permute-start.1) | collective-permute-done | bytes 65568 | tf_op jit(solution)/shard_map/ppermute | solution.py:29
  17.6 0.7 collective-permute-done.2
  18.2 0.7 pad_maximum_fusion.1
  19.0 0.0 all-gather.5.cloned.1.call-update
  19.0 0.0 reduce-scatter.3.cloned.1.call-start
  19.1 0.6 pad_add_fusion.place
  19.6 6.5 %shard_map.128 = (bf16[4,8,384,256]{3,2,1,0:T(8,128)(2,1)}, bf16[4,8,128,128]{3,2,1,0:T(8,128)(2,1)}, bf16[4,8,128,128]{3,2,1,0:T(8,128)(2,1)}) custom-call(s32[3]{0:T(128)} %pad_add_fusion.place, bf16[256,8192]{1,0:T(8,128)(2,1)} %bitcast.113, bf16[256,512]{1,0:T(8,128)(2,1)} %bitcast.116), custom_call_target="tpu_custom_call" | custom-call | flops 2147483648 | bytes 12582912 | tf_op jit(solution)/shard_map/pallas_call | solution.py:96
  26.2 0.0 reduce-scatter.3.cloned.1.call-update
  26.2 0.0 reduce-scatter.5.cloned.1.call-start
  26.3 1.4 collective-permute-start.7
  27.7 1.2 collective-permute-start.4
  28.9 1.5 collective-permute-start.5
  30.4 0.1 collective-permute-start.6
  30.5 2.2 %collective-permute-done.4 = bf16[256,256]{1,0:T(8,128)(2,1)S(1)} collective-permute-done((bf16[256,256]{1,0:T(8,128)(2,1)S(1)}, bf16[256,256]{1,0:T(8,128)(2,1)S(1)}, u32[]{:S(2)}, u32[]{:S(2)}) %collective-permute-start.4) | collective-permute-done | bytes 131104 | tf_op jit(solution)/shard_map/ppermute | solution.py:29
  32.7 2.6 %collective-permute-done.5 = bf16[256,256]{1,0:T(8,128)(2,1)S(1)} collective-permute-done((bf16[256,256]{1,0:T(8,128)(2,1)S(1)}, bf16[256,256]{1,0:T(8,128)(2,1)S(1)}, u32[]{:S(2)}, u32[]{:S(2)}) %collective-permute-start.5) | collective-permute-done | bytes 131104 | tf_op jit(solution)/shard_map/ppermute | solution.py:29
  35.4 1.4 collective-permute-done.6
  36.7 0.9 pad_maximum_fusion
  37.6 12.4 %collective-permute-done.7 = bf16[4,8,128,128]{3,2,1,0:T(8,128)(2,1)S(1)} collective-permute-done((bf16[4,8,128,128]{3,2,1,0:T(8,128)(2,1)}, bf16[4,8,128,128]{3,2,1,0:T(8,128)(2,1)S(1)}, u32[]{:S(2)}, u32[]{:S(2)}) %collective-permute-start.7) | collective-permute-done | bytes 1048608 | tf_op jit(solution)/shard_map/ppermute | solution.py:29
  50.0 1.3 add_convert_fusion
  51.4 0.0 reduce-scatter.5.cloned.1.call-update
  51.4 0.0 all-gather.7.cloned.1.call-start
  51.5 10.0 %all-gather.5.cloned.1.call-done = bf16[32,128,256]{2,1,0:T(8,128)(2,1)} async-done(((bf16[4,128,256]{2,1,0:T(8,128)(2,1)}), bf16[32,128,256]{2,1,0:T(8,128)(2,1)}) %all-gather.5.cloned.1.call-update) | async-done | bytes 2097168 | tf_op jit(solution)/shard_map/all_gather | solution.py:204
  61.5 0.0 all-gather.7.cloned.1.call-update
  61.5 0.2 mul.35
  61.7 0.2 sub.17
  61.9 0.2 add.64
  62.1 0.9 fusion
  63.0 0.6 collective-permute-start.10
  63.6 3.1 %collective-permute-start.9 = (bf16[16,8192]{1,0:T(8,128)(2,1)S(1)}, bf16[16,8192]{1,0:T(8,128)(2,1)S(1)}, u32[]{:S(2)}, u32[]{:S(2)}) collective-permute-start(bf16[16,8192]{1,0:T(8,128)(2,1)S(1)} %fusion), channel_id=1, source_target_pairs={{0,64},{64,0},{1,65},{65,1},{2,66},{66,2},{3,67},{67,3},{4,68},{68... | collective-permute-start | bytes 786440 | tf_op jit(solution)/shard_map/ppermute | solution.py:29
  66.8 1.2 collective-permute-start.8
  68.0 5.8 %collective-permute-done.10 = bf16[16,8192]{1,0:T(8,128)(2,1)S(1)} collective-permute-done((bf16[16,8192]{1,0:T(8,128)(2,1)S(1)}, bf16[16,8192]{1,0:T(8,128)(2,1)S(1)}, u32[]{:S(2)}, u32[]{:S(2)}) %collective-permute-start.10) | collective-permute-done | bytes 262176 | tf_op jit(solution)/shard_map/ppermute | solution.py:29
  73.8 1.2 multiply_subtract_fusion
  75.0 18.8 %reduce-scatter.3.cloned.1.call-done = bf16[1,8,384,256]{3,2,1,0:T(8,128)(2,1)} async-done(((bf16[4,8,384,256]{3,2,1,0:T(8,128)(2,1)}), bf16[1,8,384,256]{3,2,1,0:T(8,128)(2,1)}) %reduce-scatter.3.cloned.1.call-update) | async-done | bytes 1572880 | tf_op jit(solution)/shard_map/reduce_scatter | solution.py:207
  93.8 1.1 slice_bitcast_fusion.8
  94.9 1.6 collective-permute-start.12
  96.5 1.9 %collective-permute-start.16 = (bf16[192,256]{1,0:T(8,128)(2,1)S(1)}, bf16[192,256]{1,0:T(8,128)(2,1)S(1)}, u32[]{:S(2)}, u32[]{:S(2)}) collective-permute-start(bf16[192,256]{1,0:T(8,128)(2,1)S(1)} %get-tuple-element.56), channel_id=1, source_target_pairs={{0,56},{8,0},{16,8},{24,16},{32,24},{40,32},{48,40},{56,48},{1,57}... | collective-permute-start | bytes 294920 | tf_op jit(solution)/shard_map/ppermute | solution.py:29
  98.4 1.7 %convert_element_type.87 = f32[8,384,256]{2,1,0:T(8,128)S(1)} convert(bf16[8,384,256]{2,1,0:T(8,128)(2,1)} %bitcast.96) | non-fusion elementwise | flops 786432 | bytes 4718592 | tf_op jit(solution)/shard_map/convert_element_type | solution.py:229
  100.1 3.6 %collective-permute-done.12 = bf16[192,256]{1,0:T(8,128)(2,1)S(1)} collective-permute-done((bf16[192,256]{1,0:T(8,128)(2,1)S(1)}, bf16[192,256]{1,0:T(8,128)(2,1)S(1)}, u32[]{:S(2)}, u32[]{:S(2)}) %collective-permute-start.12) | collective-permute-done | bytes 98336 | tf_op jit(solution)/shard_map/ppermute | solution.py:29
  103.7 0.1 collective-permute-done.16
  103.8 0.1 fusion.14
  103.8 1.6 collective-permute-start.13
  105.5 0.7 pad_maximum_fusion.3
  106.2 1.7 collective-permute-start.17
  107.8 8.7 %collective-permute-done.13 = bf16[384,256]{1,0:T(8,128)(2,1)S(1)} collective-permute-done((bf16[384,256]{1,0:T(8,128)(2,1)S(1)}, bf16[384,256]{1,0:T(8,128)(2,1)S(1)}, u32[]{:S(2)}, u32[]{:S(2)}) %collective-permute-start.13) | collective-permute-done | bytes 196640 | tf_op jit(solution)/shard_map/ppermute | solution.py:29
  116.5 0.7 fusion.8
  117.2 0.1 collective-permute-start.14
  117.4 5.3 %reduce-scatter.5.cloned.1.call-done = bf16[1,8,128,128]{3,2,1,0:T(8,128)(2,1)} async-done(((bf16[4,8,128,128]{3,2,1,0:T(8,128)(2,1)}), bf16[1,8,128,128]{3,2,1,0:T(8,128)(2,1)}) %reduce-scatter.5.cloned.1.call-update) | async-done | bytes 262160 | tf_op jit(solution)/shard_map/reduce_scatter | solution.py:217
  122.6 7.0 %all-to-all-start = ((bf16[8,128,128]{2,1,0:T(8,128)(2,1)}), bf16[8,128,128]{2,1,0:T(8,128)(2,1)S(1)}, u32[]{:S(2)}, u32[]{:S(2)}) async-start(bf16[8,128,128]{2,1,0:T(8,128)(2,1)} %bitcast.103), calls=%async_computation.2 | async-start | bytes 524288 | tf_op jit(solution)/shard_map/all_to_all | solution.py:235
  129.7 1.8 %fusion.10 = (bf16[384,256]{1,0:T(8,128)(2,1)}, bf16[384,256]{1,0:T(8,128)(2,1)}) fusion(f32[8,384,256]{2,1,0:T(8,128)S(1)} %convert_element_type.87, bf16[384,256]{1,0:T(8,128)(2,1)} %collective-permute-done.14, bf16[384,256]{1,0:T(8,128)(2,1)} %collective-permute-done.17), kind=kLoop, calls=%fused_computation.22 | loop fusion | flops 589824 | bytes 1572864 | tf_op jit(solution)/shard_map/convert_element_type | solution.py:237
  131.5 3.2 %collective-permute-start.18 = (bf16[384,256]{1,0:T(8,128)(2,1)}, bf16[384,256]{1,0:T(8,128)(2,1)}, u32[]{:S(2)}, u32[]{:S(2)}) collective-permute-start(bf16[384,256]{1,0:T(8,128)(2,1)} %get-tuple-element.52), channel_id=1, source_target_pairs={{0,56},{8,0},{16,8},{24,16},{32,24},{40,32},{48,40},{56,48},{1,57}... | collective-permute-start | bytes 589832 | tf_op jit(solution)/shard_map/ppermute | solution.py:29
  134.8 12.2 %shard_map.129 = (bf16[256,512]{1,0:T(8,128)(2,1)}, bf16[256,8192]{1,0:T(8,128)(2,1)}) custom-call(s32[3]{0:T(128)} %pad_add_fusion.place, bf16[256,8192]{1,0:T(8,128)(2,1)} %bitcast.114, bf16[256,512]{1,0:T(8,128)(2,1)} %bitcast.117, bf16[8,4,256,256]{3,2,1,0:T(8,128)(2,1)} %bitcast.115, bf16[8,4,128,256]{3,2,1,0:T(8,128)(2,1)} %bitcast.14.weight_c, ...), custom_call_target="tpu_custom_call" | custom-call | flops 4294967296 | bytes 16777216 | tf_op jit(solution)/shard_map/pallas_call | solution.py:154
  147.0 1.7 fusion.6
  148.7 3.2 %collective-permute-start.19 = (bf16[384,256]{1,0:T(8,128)(2,1)}, bf16[384,256]{1,0:T(8,128)(2,1)S(1)}, u32[]{:S(2)}, u32[]{:S(2)}) collective-permute-start(bf16[384,256]{1,0:T(8,128)(2,1)} %fusion.6), channel_id=1, source_target_pairs={{0,56},{8,0},{16,8},{24,16},{32,24},{40,32},{48,40},{56,48},{1,57}... | collective-permute-start | bytes 589832 | tf_op jit(solution)/shard_map/ppermute | solution.py:29
  151.9 3.9 %collective-permute-done.15 = bf16[384,256]{1,0:T(8,128)(2,1)S(1)} collective-permute-done((bf16[384,256]{1,0:T(8,128)(2,1)}, bf16[384,256]{1,0:T(8,128)(2,1)S(1)}, u32[]{:S(2)}, u32[]{:S(2)}) %collective-permute-start.15) | collective-permute-done | bytes 196640 | tf_op jit(solution)/shard_map/ppermute | solution.py:29
  155.8 0.1 fusion.11
  155.9 1.3 collective-permute-start.20
  157.2 3.4 %collective-permute-done.20 = bf16[384,128]{1,0:T(8,128)(2,1)S(1)} collective-permute-done((bf16[384,128]{1,0:T(8,128)(2,1)S(1)}, bf16[384,128]{1,0:T(8,128)(2,1)S(1)}, u32[]{:S(2)}, u32[]{:S(2)}) %collective-permute-start.20) | collective-permute-done | bytes 98336 | tf_op jit(solution)/shard_map/ppermute | solution.py:29
  160.6 0.8 copy.15
  (36 shorter events, 0.2 us)
Async XLA Ops:
  8.0 53.5 %all-gather.5.cloned.1.call-start = ((), (), s32[]{:S(2)}) async-start(), calls=%async_computation.5 | async-start | bytes 2359296 | tf_op jit(solution)/shard_map/all_gather | solution.py:204
  8.9 5.8 %collective-permute-start = (bf16[128,256]{1,0:T(8,128)(2,1)S(1)}, bf16[128,256]{1,0:T(8,128)(2,1)S(1)}, u32[]{:S(2)}, u32[]{:S(2)}) collective-permute-start(bf16[128,256]{1,0:T(8,128)(2,1)S(1)} %get-tuple-element.65), channel_id=1, source_target_pairs={{0,6},{2,0},{4,2},{6,4},{1,7},{3,1},{5,3},{7,5},{8,14},{10,8},{12,... | collective-permute-start | bytes 196616 | tf_op jit(solution)/shard_map/ppermute | solution.py:29
  11.8 5.8 %collective-permute-start.1 = (bf16[128,256]{1,0:T(8,128)(2,1)S(1)}, bf16[128,256]{1,0:T(8,128)(2,1)S(1)}, u32[]{:S(2)}, u32[]{:S(2)}) collective-permute-start(bf16[128,256]{1,0:T(8,128)(2,1)S(1)} %get-tuple-element.65), channel_id=1, source_target_pairs={{0,4},{2,6},{4,0},{6,2},{1,5},{3,7},{5,1},{7,3},{8,12},{10,14},{12... | collective-permute-start | bytes 196616 | tf_op jit(solution)/shard_map/ppermute | solution.py:29
  12.6 5.7 %collective-permute-start.2 = (bf16[128,256]{1,0:T(8,128)(2,1)S(1)}, bf16[128,256]{1,0:T(8,128)(2,1)S(1)}, u32[]{:S(2)}, u32[]{:S(2)}) collective-permute-start(bf16[128,256]{1,0:T(8,128)(2,1)S(1)} %get-tuple-element.65), channel_id=1, source_target_pairs={{0,2},{2,4},{4,6},{6,0},{1,3},{3,5},{5,7},{7,1},{8,10},{10,12},{12... | collective-permute-start | bytes 196616 | tf_op jit(solution)/shard_map/ppermute | solution.py:29
  13.5 5.5 %collective-permute-start.3 = (bf16[128,256]{1,0:T(8,128)(2,1)S(1)}, bf16[128,256]{1,0:T(8,128)(2,1)S(1)}, u32[]{:S(2)}, u32[]{:S(2)}) collective-permute-start(bf16[128,256]{1,0:T(8,128)(2,1)S(1)} %get-tuple-element.63), channel_id=1, source_target_pairs={{0,1},{1,0},{2,3},{3,2},{4,5},{5,4},{6,7},{7,6},{8,9},{9,8},{10,11... | collective-permute-start | bytes 196616 | tf_op jit(solution)/shard_map/ppermute | solution.py:29
  19.0 74.8 %reduce-scatter.3.cloned.1.call-start = ((), (), s32[]{:S(2)}) async-start(), calls=%async_computation.3 | async-start | bytes 7864320 | tf_op jit(solution)/shard_map/reduce_scatter | solution.py:207
  26.2 1.5 copy-start.4
  26.2 23.9 %copy-start = (bf16[4,8,128,128]{3,2,1,0:T(8,128)(2,1)S(1)}, bf16[4,8,128,128]{3,2,1,0:T(8,128)(2,1)}, u32[]{:S(2)}) copy-start(bf16[4,8,128,128]{3,2,1,0:T(8,128)(2,1)} %get-tuple-element.27) | copy-start | bytes 3145732
  26.2 96.4 %reduce-scatter.5.cloned.1.call-start = ((), (), s32[]{:S(2)}) async-start(), calls=%async_computation.4 | async-start | bytes 1310720 | tf_op jit(solution)/shard_map/reduce_scatter | solution.py:217
  26.3 23.8 %collective-permute-start.7 = (bf16[4,8,128,128]{3,2,1,0:T(8,128)(2,1)}, bf16[4,8,128,128]{3,2,1,0:T(8,128)(2,1)S(1)}, u32[]{:S(2)}, u32[]{:S(2)}) collective-permute-start(bf16[4,8,128,128]{3,2,1,0:T(8,128)(2,1)} %get-tuple-element.25), channel_id=1, source_target_pairs={{0,1},{1,0},{2,3},{3,2},{4,5},{5,4},{6,7},{7,6},{8,9},{9,8},{10,11... | collective-permute-start | bytes 3145736 | tf_op jit(solution)/shard_map/ppermute | solution.py:29
  27.7 33.9 %copy-start.5 = (f32[1,16,64]{2,1,0:T(8,128)S(1)}, f32[1,16,64]{2,1,0:T(8,128)}, u32[]{:S(2)}) copy-start(f32[1,16,64]{2,1,0:T(8,128)} %param.15) | copy-start | bytes 12292
  27.7 5.0 %collective-permute-start.4 = (bf16[256,256]{1,0:T(8,128)(2,1)S(1)}, bf16[256,256]{1,0:T(8,128)(2,1)S(1)}, u32[]{:S(2)}, u32[]{:S(2)}) collective-permute-start(bf16[256,256]{1,0:T(8,128)(2,1)S(1)} %get-tuple-element.62), channel_id=1, source_target_pairs={{0,6},{2,0},{4,2},{6,4},{1,7},{3,1},{5,3},{7,5},{8,14},{10,8},{12,... | collective-permute-start | bytes 393224 | tf_op jit(solution)/shard_map/ppermute | solution.py:29
  28.9 6.5 %collective-permute-start.5 = (bf16[256,256]{1,0:T(8,128)(2,1)S(1)}, bf16[256,256]{1,0:T(8,128)(2,1)S(1)}, u32[]{:S(2)}, u32[]{:S(2)}) collective-permute-start(bf16[256,256]{1,0:T(8,128)(2,1)S(1)} %get-tuple-element.62), channel_id=1, source_target_pairs={{0,4},{2,6},{4,0},{6,2},{1,5},{3,7},{5,1},{7,3},{8,12},{10,14},{12... | collective-permute-start | bytes 393224 | tf_op jit(solution)/shard_map/ppermute | solution.py:29
  30.4 6.4 %collective-permute-start.6 = (bf16[256,256]{1,0:T(8,128)(2,1)S(1)}, bf16[256,256]{1,0:T(8,128)(2,1)S(1)}, u32[]{:S(2)}, u32[]{:S(2)}) collective-permute-start(bf16[256,256]{1,0:T(8,128)(2,1)S(1)} %get-tuple-element.62), channel_id=1, source_target_pairs={{0,2},{2,4},{4,6},{6,0},{1,3},{3,5},{5,7},{7,1},{8,10},{10,12},{12... | collective-permute-start | bytes 393224 | tf_op jit(solution)/shard_map/ppermute | solution.py:29
  36.7 25.0 %copy-start.6 = (s32[1,16,64]{2,1,0:T(8,128)S(1)}, s32[1,16,64]{2,1,0:T(8,128)}, u32[]{:S(2)}) copy-start(s32[1,16,64]{2,1,0:T(8,128)} %param.13) | copy-start | bytes 12292
  37.6 24.3 %copy-start.7 = (f32[1,16,64]{2,1,0:T(8,128)S(1)}, f32[1,16,64]{2,1,0:T(8,128)}, u32[]{:S(2)}) copy-start(f32[1,16,64]{2,1,0:T(8,128)} %param.14) | copy-start | bytes 12292
  50.0 12.1 %copy-start.1 = (s32[1,16,8192]{2,1,0:T(8,128)S(1)}, s32[1,16,8192]{2,1,0:T(8,128)}, u32[]{:S(2)}) copy-start(s32[1,16,8192]{2,1,0:T(8,128)} %param.12) | copy-start | bytes 1572868
  51.4 22.4 %copy-start.2 = (f32[16,8192]{1,0:T(8,128)S(1)}, f32[16,8192]{1,0:T(8,128)}, u32[]{:S(2)}) copy-start(f32[16,8192]{1,0:T(8,128)} %param.17) | copy-start | bytes 1572868
  51.4 22.4 %copy-start.3 = (f32[16,8192]{1,0:T(8,128)S(1)}, f32[16,8192]{1,0:T(8,128)}, u32[]{:S(2)}) copy-start(f32[16,8192]{1,0:T(8,128)} %param.16) | copy-start | bytes 1572868
  51.4 83.3 %all-gather.7.cloned.1.call-start = ((), (), s32[]{:S(2)}) async-start(), calls=%async_computation.6 | async-start | bytes 4718592 | tf_op jit(solution)/shard_map/all_gather | solution.py:220
  63.0 10.8 %collective-permute-start.10 = (bf16[16,8192]{1,0:T(8,128)(2,1)S(1)}, bf16[16,8192]{1,0:T(8,128)(2,1)S(1)}, u32[]{:S(2)}, u32[]{:S(2)}) collective-permute-start(bf16[16,8192]{1,0:T(8,128)(2,1)S(1)} %fusion), channel_id=1, source_target_pairs={{0,128},{128,0},{1,129},{129,1},{2,130},{130,2},{3,131},{131,3},{4... | collective-permute-start | bytes 786440 | tf_op jit(solution)/shard_map/ppermute | solution.py:29
  63.6 10.2 %collective-permute-start.11 = (bf16[16,8192]{1,0:T(8,128)(2,1)S(1)}, bf16[16,8192]{1,0:T(8,128)(2,1)S(1)}, u32[]{:S(2)}, u32[]{:S(2)}) collective-permute-start(bf16[16,8192]{1,0:T(8,128)(2,1)S(1)} %fusion), channel_id=1, source_target_pairs={{0,192},{64,128},{128,64},{192,0},{1,193},{65,129},{129,65},{193,1... | collective-permute-start | bytes 786440 | tf_op jit(solution)/shard_map/ppermute | solution.py:40
  63.6 10.2 %collective-permute-start.9 = (bf16[16,8192]{1,0:T(8,128)(2,1)S(1)}, bf16[16,8192]{1,0:T(8,128)(2,1)S(1)}, u32[]{:S(2)}, u32[]{:S(2)}) collective-permute-start(bf16[16,8192]{1,0:T(8,128)(2,1)S(1)} %fusion), channel_id=1, source_target_pairs={{0,64},{64,0},{1,65},{65,1},{2,66},{66,2},{3,67},{67,3},{4,68},{68... | collective-permute-start | bytes 786440 | tf_op jit(solution)/shard_map/ppermute | solution.py:29
  66.8 68.0 %collective-permute-start.8 = (bf16[8,4,128,256]{3,2,1,0:T(8,128)(2,1)}, bf16[8,4,128,256]{3,2,1,0:T(8,128)(2,1)}, u32[]{:S(2)}, u32[]{:S(2)}) collective-permute-start(bf16[8,4,128,256]{3,2,1,0:T(8,128)(2,1)} %bitcast.14.weight_c), channel_id=1, source_target_pairs={{0,1},{1,0},{2,3},{3,2},{4,5},{5,4},{6,7},{7,6},{8,9},{9,8},{10,11... | collective-permute-start | bytes 6291464 | tf_op jit(solution)/shard_map/ppermute | solution.py:29
  94.9 8.8 %collective-permute-start.12 = (bf16[192,256]{1,0:T(8,128)(2,1)S(1)}, bf16[192,256]{1,0:T(8,128)(2,1)S(1)}, u32[]{:S(2)}, u32[]{:S(2)}) collective-permute-start(bf16[192,256]{1,0:T(8,128)(2,1)S(1)} %get-tuple-element.58), channel_id=1, source_target_pairs={{0,8},{8,16},{16,24},{24,32},{32,40},{40,48},{48,56},{56,0},{1,9},... | collective-permute-start | bytes 294920 | tf_op jit(solution)/shard_map/ppermute | solution.py:29
  96.5 7.3 %collective-permute-start.16 = (bf16[192,256]{1,0:T(8,128)(2,1)S(1)}, bf16[192,256]{1,0:T(8,128)(2,1)S(1)}, u32[]{:S(2)}, u32[]{:S(2)}) collective-permute-start(bf16[192,256]{1,0:T(8,128)(2,1)S(1)} %get-tuple-element.56), channel_id=1, source_target_pairs={{0,56},{8,0},{16,8},{24,16},{32,24},{40,32},{48,40},{56,48},{1,57}... | collective-permute-start | bytes 294920 | tf_op jit(solution)/shard_map/ppermute | solution.py:29
  103.8 12.7 %collective-permute-start.13 = (bf16[384,256]{1,0:T(8,128)(2,1)S(1)}, bf16[384,256]{1,0:T(8,128)(2,1)S(1)}, u32[]{:S(2)}, u32[]{:S(2)}) collective-permute-start(bf16[384,256]{1,0:T(8,128)(2,1)S(1)} %pad_maximum_fusion.2), channel_id=1, source_target_pairs={{0,8},{8,16},{16,24},{24,32},{32,40},{40,48},{48,56},{56,0},{1,9},... | collective-permute-start | bytes 589832 | tf_op jit(solution)/shard_map/ppermute | solution.py:29
  106.2 23.5 %collective-permute-start.17 = (bf16[384,256]{1,0:T(8,128)(2,1)}, bf16[384,256]{1,0:T(8,128)(2,1)}, u32[]{:S(2)}, u32[]{:S(2)}) collective-permute-start(bf16[384,256]{1,0:T(8,128)(2,1)} %pad_maximum_fusion.3), channel_id=1, source_target_pairs={{0,56},{8,0},{16,8},{24,16},{32,24},{40,32},{48,40},{56,48},{1,57}... | collective-permute-start | bytes 589832 | tf_op jit(solution)/shard_map/ppermute | solution.py:29
  117.2 12.4 %collective-permute-start.14 = (bf16[384,256]{1,0:T(8,128)(2,1)}, bf16[384,256]{1,0:T(8,128)(2,1)}, u32[]{:S(2)}, u32[]{:S(2)}) collective-permute-start(bf16[384,256]{1,0:T(8,128)(2,1)} %fusion.8), channel_id=1, source_target_pairs={{0,8},{8,16},{16,24},{24,32},{32,40},{40,48},{48,56},{56,0},{1,9},... | collective-permute-start | bytes 589832 | tf_op jit(solution)/shard_map/ppermute | solution.py:29
  122.6 26.0 %all-to-all-start = ((bf16[8,128,128]{2,1,0:T(8,128)(2,1)}), bf16[8,128,128]{2,1,0:T(8,128)(2,1)S(1)}, u32[]{:S(2)}, u32[]{:S(2)}) async-start(bf16[8,128,128]{2,1,0:T(8,128)(2,1)} %bitcast.103), calls=%async_computation.2 | async-start | bytes 524288 | tf_op jit(solution)/shard_map/all_to_all | solution.py:235
  131.5 15.5 %collective-permute-start.18 = (bf16[384,256]{1,0:T(8,128)(2,1)}, bf16[384,256]{1,0:T(8,128)(2,1)}, u32[]{:S(2)}, u32[]{:S(2)}) collective-permute-start(bf16[384,256]{1,0:T(8,128)(2,1)} %get-tuple-element.52), channel_id=1, source_target_pairs={{0,56},{8,0},{16,8},{24,16},{32,24},{40,32},{48,40},{56,48},{1,57}... | collective-permute-start | bytes 589832 | tf_op jit(solution)/shard_map/ppermute | solution.py:29
  148.7 7.1 %collective-permute-start.15 = (bf16[384,256]{1,0:T(8,128)(2,1)}, bf16[384,256]{1,0:T(8,128)(2,1)S(1)}, u32[]{:S(2)}, u32[]{:S(2)}) collective-permute-start(bf16[384,256]{1,0:T(8,128)(2,1)} %get-tuple-element.37), channel_id=1, source_target_pairs={{0,8},{8,16},{16,24},{24,32},{32,40},{40,48},{48,56},{56,0},{1,9},... | collective-permute-start | bytes 589832 | tf_op jit(solution)/shard_map/ppermute | solution.py:29
  148.7 7.1 %collective-permute-start.19 = (bf16[384,256]{1,0:T(8,128)(2,1)}, bf16[384,256]{1,0:T(8,128)(2,1)S(1)}, u32[]{:S(2)}, u32[]{:S(2)}) collective-permute-start(bf16[384,256]{1,0:T(8,128)(2,1)} %fusion.6), channel_id=1, source_target_pairs={{0,56},{8,0},{16,8},{24,16},{32,24},{40,32},{48,40},{56,48},{1,57}... | collective-permute-start | bytes 589832 | tf_op jit(solution)/shard_map/ppermute | solution.py:29
  155.9 4.7 %collective-permute-start.20 = (bf16[384,128]{1,0:T(8,128)(2,1)S(1)}, bf16[384,128]{1,0:T(8,128)(2,1)S(1)}, u32[]{:S(2)}, u32[]{:S(2)}) collective-permute-start(bf16[384,128]{1,0:T(8,128)(2,1)S(1)} %select_convert_fusion), channel_id=1, source_target_pairs={{0,1},{1,0},{2,3},{3,2},{4,5},{5,4},{6,7},{7,6},{8,9},{9,8},{10,11... | collective-permute-start | bytes 294920 | tf_op jit(solution)/shard_map/ppermute | solution.py:29
Sparse Core Ops, SparseCore 0:
  19.1 42.3 all-gather.4
  63.3 61.4 all-gather.6
Sparse Core Ops, SparseCore 1:
  26.3 67.4 reduce-scatter.2
  96.8 25.8 reduce-scatter.4

commit v2 on v1

--- a/solution.py
+++ b/solution.py
@@ -11,7 +11,7 @@
 GROUP = 128
 Z, X, Y = 8, 4, 2
 WEIGHT_SPLIT = 256
-GRAD_SPLIT = 384
+GRAD_SPLIT = 320
 F32, BF16 = jnp.float32, jnp.bfloat16
 VMEM_LIMIT = 56 * 1024 * 1024
 
@@ -230,22 +230,25 @@
     up, down = shift(grad_a[4][:half], "z", 1), shift(grad_a[4][half:], "z", -1)
     up = jnp.concatenate([at[3][:half] + up.astype(F32), at[3][half:]]).astype(BF16)
     down = jnp.concatenate([at[5][:half], at[5][half:] + down.astype(F32)]).astype(BF16)
+    up, down = lax.optimization_barrier((up, down))
     up, down = shift(up, "z", 1), shift(down, "z", -1)
     up, down = (at[2] + up.astype(F32)).astype(BF16), (at[6] + down.astype(F32)).astype(BF16)
-    grad_c = lax.all_to_all(after(grad_c_x, up), "z", 0, 0, tiled=True)
+    up, down = lax.optimization_barrier((up, down))
     up, down = shift(up, "z", 1), shift(down, "z", -1)
     up, down = (at[1] + up.astype(F32)).astype(BF16), (at[7] + down.astype(F32)).astype(BF16)
-    keys, back = products(place, tokens, cot, weight_a, weight_c, other_c)
-    up, down = after(up, keys, grad_c), after(down, keys, grad_c)
+    up, down = lax.optimization_barrier((up, down))
+    grad_c = lax.all_to_all(after(grad_c_x, up, other_c), "z", 0, 0, tiled=True)
     up, down = shift(up, "z", 1), shift(down, "z", -1)
     grad_a = at[0] + (up.astype(F32) + down.astype(F32))
     lower, upper = grad_a[:, :part], grad_a[:, part:]
     theirs = jnp.where(y == 0, upper, lower).astype(BF16)
     mine = jnp.where(y == 0, lower, upper)
+    weight_a = after(weight_a, theirs)
     grad_a = mine + shift(theirs, "yl", 1).astype(F32)
     grad_c = jnp.sum(grad_c.astype(F32), axis=0)
     weight_grad = jnp.concatenate([grad_a, grad_c]).T * scaling
 
+    keys, back = products(place, tokens, cot, weight_a, weight_c, other_c)
     return keys[None], back[None], weight_grad[None], new_momentum, new_params
 
 

time: 169 us -> 158 us (0.935)
  waiting for transfers between devices: 81.7 us -> 71.3 us
  other arithmetic: 12.5 us -> 8.96 us
    reduce_scatter x1, waiting for transfers between devices: 18.8 us -> 6.31 us  [local(): grad_a = lax.psum_scatter(grad_a, 'x', scatter_dimension=0, tiled=True)[0]]
    ppermute x20, waiting for transfers between devices: 47.6 us -> 57.9 us  [shift(): lax.ppermute(block, axis, [(i, (i + by) % size) for i in range(size)])]
    all_gather x1, waiting for transfers between devices: 10 us -> 0.02 us  [local(): weight_c = lax.all_gather(weight_c, 'z')]
    reduce_scatter x1, waiting for transfers between devices: 5.29 us -> 0.01 us  [local(): grad_c_x = lax.psum_scatter(grad_c, 'x', scatter_dimension=0, tiled=True)[0]]
    ppermute x1, waiting for transfers between devices: 0.01 us -> 5.25 us  [outer_values(): far_core = lax.ppermute(values, ('yh', 'c'), [(i, 3 - i) for i in range(4)])]
    convert_element_type x2 -> x1, other arithmetic: 2.57 us -> 0.09 us  [local(): (at[6] + down.astype(F32)).astype(BF16)]
  transfers between devices with their start and end apart: 26 -> 26, of which waited for: 15 -> 16; matrix products, arithmetic and copies ran while one was open for 8% -> 7% of each run, Pallas kernels for 11% -> 12%
where the time goes in v2:
time: 158 us; the launch traced here: 156 us
  waiting for transfers between devices  71.3 us (45%)
  starting transfers between devices  38.3 us (24%)
  Pallas kernels  18.8 us (12%)
  between operations  15.7 us (10%)
  other arithmetic  8.96 us (6%)
  local copies, waits for them, and re-layouts  3.36 us (2%)
    ppermute x20, waiting for transfers between devices, shift(): lax.ppermute(block, axis, [(i, (i + by) % size) for i in range(size)])  57.9 us
    ppermute x20, starting transfers between devices, shift(): lax.ppermute(block, axis, [(i, (i + by) % size) for i in range(size)])  29.5 us
    pallas_call x1, Pallas kernels, products(): pl.pallas_call(product_kernel, grid_spec=pltpu.PrefetchScalarGridSpec(num...  12.2 us
    all_to_all x1, starting transfers between devices, local(): grad_c = lax.all_to_all(after(grad_c_x, up, other_c), 'z', 0, 0, tiled=True)  8.46 us
    pallas_call x1, Pallas kernels, gradients(): pl.pallas_call(grad_kernel, in_specs=[pl.BlockSpec(memory_space=pltpu.SME...  6.55 us
    reduce_scatter x1, waiting for transfers between devices, local(): grad_a = lax.psum_scatter(grad_a, 'x', scatter_dimension=0, tiled=True)[0]  6.31 us
    ppermute x1, waiting for transfers between devices, outer_values(): far_core = lax.ppermute(values, ('yh', 'c'), [(i, 3 - i) for i in range(4)])  5.25 us
  transfers between devices with their start and end apart: 26, of which 16 were waited for; matrix products, arithmetic and copies ran while one was open for 7% of the time, Pallas kernels for 12%

profile of v2, /device:TPU:16, one launch (start us, length us, event | category | flops | bytes accessed | tf_op | source)
XLA Modules:
  0.0 156.4 jit_solution(16678979125592690336)
XLA Ops:
  8.0 0.0 all-gather.5.cloned.1.call-start
  8.0 0.9 fusion.18
  8.9 2.8 %collective-permute-start = (bf16[128,256]{1,0:T(8,128)(2,1)S(1)}, bf16[128,256]{1,0:T(8,128)(2,1)S(1)}, u32[]{:S(2)}, u32[]{:S(2)}) collective-permute-start(bf16[128,256]{1,0:T(8,128)(2,1)S(1)} %get-tuple-element.77), channel_id=1, source_target_pairs={{0,6},{2,0},{4,2},{6,4},{1,7},{3,1},{5,3},{7,5},{8,14},{10,8},{12,... | collective-permute-start | bytes 196616 | tf_op jit(solution)/shard_map/ppermute | solution.py:29
  11.8 0.8 collective-permute-start.1
  12.6 0.9 collective-permute-start.2
  13.5 1.3 collective-permute-start.3
  14.7 2.8 %collective-permute-done.1 = bf16[128,256]{1,0:T(8,128)(2,1)S(1)} collective-permute-done((bf16[128,256]{1,0:T(8,128)(2,1)S(1)}, bf16[128,256]{1,0:T(8,128)(2,1)S(1)}, u32[]{:S(2)}, u32[]{:S(2)}) %collective-permute-start.1) | collective-permute-done | bytes 65568 | tf_op jit(solution)/shard_map/ppermute | solution.py:29
  17.6 0.7 collective-permute-done.2
  18.2 0.7 pad_maximum_fusion.1
  19.0 0.0 reduce-scatter.3.cloned.1.call-start
  19.1 0.7 pad_add_fusion.place
  19.7 6.5 %shard_map.128 = (bf16[4,8,320,256]{3,2,1,0:T(8,128)(2,1)}, bf16[4,8,192,128]{3,2,1,0:T(8,128)(2,1)}, bf16[4,8,192,128]{3,2,1,0:T(8,128)(2,1)}) custom-call(s32[3]{0:T(128)} %pad_add_fusion.place, bf16[256,8192]{1,0:T(8,128)(2,1)} %bitcast.113, bf16[256,512]{1,0:T(8,128)(2,1)} %bitcast.116), custom_call_target="tpu_custom_call" | custom-call | flops 2147483648 | bytes 12582912 | tf_op jit(solution)/shard_map/pallas_call | solution.py:96
  26.3 0.0 reduce-scatter.3.cloned.1.call-update
  26.3 0.0 reduce-scatter.5.cloned.1.call-start
  26.4 1.4 collective-permute-start.7
  27.8 1.2 collective-permute-start.4
  29.0 1.5 collective-permute-start.5
  30.5 0.1 collective-permute-start.6
  30.6 2.2 %collective-permute-done.4 = bf16[256,256]{1,0:T(8,128)(2,1)S(1)} collective-permute-done((bf16[256,256]{1,0:T(8,128)(2,1)S(1)}, bf16[256,256]{1,0:T(8,128)(2,1)S(1)}, u32[]{:S(2)}, u32[]{:S(2)}) %collective-permute-start.4) | collective-permute-done | bytes 131104 | tf_op jit(solution)/shard_map/ppermute | solution.py:29
  32.8 2.6 %collective-permute-done.5 = bf16[256,256]{1,0:T(8,128)(2,1)S(1)} collective-permute-done((bf16[256,256]{1,0:T(8,128)(2,1)S(1)}, bf16[256,256]{1,0:T(8,128)(2,1)S(1)}, u32[]{:S(2)}, u32[]{:S(2)}) %collective-permute-start.5) | collective-permute-done | bytes 131104 | tf_op jit(solution)/shard_map/ppermute | solution.py:29
  35.4 1.4 collective-permute-done.6
  36.8 0.9 pad_maximum_fusion
  37.7 23.7 %collective-permute-done.7 = bf16[4,8,192,128]{3,2,1,0:T(8,128)(2,1)S(1)} collective-permute-done((bf16[4,8,192,128]{3,2,1,0:T(8,128)(2,1)}, bf16[4,8,192,128]{3,2,1,0:T(8,128)(2,1)S(1)}, u32[]{:S(2)}, u32[]{:S(2)}) %collective-permute-start.7) | collective-permute-done | bytes 1572896 | tf_op jit(solution)/shard_map/ppermute | solution.py:29
  61.4 1.7 %add_convert_fusion = bf16[4,8,192,128]{3,2,1,0:T(8,128)(2,1)} fusion(bf16[4,8,192,128]{3,2,1,0:T(8,128)(2,1)S(1)} %collective-permute-done.7, bf16[4,8,192,128]{3,2,1,0:T(8,128)(2,1)S(1)} %copy-done), kind=kLoop, calls=%fused_computation | loop fusion | flops 3145728 | bytes 4718592 | tf_op jit(solution)/shard_map/convert_element_type | solution.py:216
  63.1 0.0 all-gather.7.cloned.1.call-start
  63.2 0.7 all-gather.7.cloned.1.call-update
  63.9 0.2 mul.35
  64.1 0.2 sub.17
  64.3 0.2 add.64
  64.5 0.9 fusion
  65.4 0.1 collective-permute-start.10
  65.5 0.4 collective-permute-start.8
  65.9 3.2 %collective-permute-start.9 = (bf16[16,8192]{1,0:T(8,128)(2,1)S(1)}, bf16[16,8192]{1,0:T(8,128)(2,1)S(1)}, u32[]{:S(2)}, u32[]{:S(2)}) collective-permute-start(bf16[16,8192]{1,0:T(8,128)(2,1)S(1)} %fusion), channel_id=1, source_target_pairs={{0,128},{128,0},{1,129},{129,1},{2,130},{130,2},{3,131},{131,3},{4... | collective-permute-start | bytes 786440 | tf_op jit(solution)/shard_map/ppermute | solution.py:29
  69.1 1.3 collective-permute-start.19
  70.4 5.2 %collective-permute-done.10 = bf16[16,8192]{1,0:T(8,128)(2,1)S(1)} collective-permute-done((bf16[16,8192]{1,0:T(8,128)(2,1)S(1)}, bf16[16,8192]{1,0:T(8,128)(2,1)S(1)}, u32[]{:S(2)}, u32[]{:S(2)}) %collective-permute-start.10) | collective-permute-done | bytes 262176 | tf_op jit(solution)/shard_map/ppermute | solution.py:40
  75.7 2.1 %collective-permute-done.9 = bf16[16,8192]{1,0:T(8,128)(2,1)S(1)} collective-permute-done((bf16[16,8192]{1,0:T(8,128)(2,1)S(1)}, bf16[16,8192]{1,0:T(8,128)(2,1)S(1)}, u32[]{:S(2)}, u32[]{:S(2)}) %collective-permute-start.9) | collective-permute-done | bytes 262176 | tf_op jit(solution)/shard_map/ppermute | solution.py:29
  77.8 1.2 multiply_subtract_fusion
  79.0 6.3 %reduce-scatter.3.cloned.1.call-done = bf16[1,8,320,256]{3,2,1,0:T(8,128)(2,1)} async-done(((bf16[4,8,320,256]{3,2,1,0:T(8,128)(2,1)}), bf16[1,8,320,256]{3,2,1,0:T(8,128)(2,1)}) %reduce-scatter.3.cloned.1.call-update) | async-done | bytes 1310736 | tf_op jit(solution)/shard_map/reduce_scatter | solution.py:207
  85.3 1.0 slice_bitcast_fusion.8
  86.4 1.6 %collective-permute-start.11 = (bf16[160,256]{1,0:T(8,128)(2,1)S(1)}, bf16[160,256]{1,0:T(8,128)(2,1)S(1)}, u32[]{:S(2)}, u32[]{:S(2)}) collective-permute-start(bf16[160,256]{1,0:T(8,128)(2,1)S(1)} %get-tuple-element.70), channel_id=1, source_target_pairs={{0,8},{8,16},{16,24},{24,32},{32,40},{40,48},{48,56},{56,0},{1,9},... | collective-permute-start | bytes 245768 | tf_op jit(solution)/shard_map/ppermute | solution.py:29
  88.0 1.9 %collective-permute-start.12 = (bf16[160,256]{1,0:T(8,128)(2,1)S(1)}, bf16[160,256]{1,0:T(8,128)(2,1)S(1)}, u32[]{:S(2)}, u32[]{:S(2)}) collective-permute-start(bf16[160,256]{1,0:T(8,128)(2,1)S(1)} %get-tuple-element.68), channel_id=1, source_target_pairs={{0,56},{8,0},{16,8},{24,16},{32,24},{40,32},{48,40},{56,48},{1,57}... | collective-permute-start | bytes 245768 | tf_op jit(solution)/shard_map/ppermute | solution.py:29
  89.9 1.6 %convert_element_type.87 = f32[8,320,256]{2,1,0:T(8,128)S(1)} convert(bf16[8,320,256]{2,1,0:T(8,128)(2,1)} %bitcast.99) | non-fusion elementwise | flops 655360 | bytes 3932160 | tf_op jit(solution)/shard_map/convert_element_type | solution.py:229
  91.4 3.1 %collective-permute-done.11 = bf16[160,256]{1,0:T(8,128)(2,1)S(1)} collective-permute-done((bf16[160,256]{1,0:T(8,128)(2,1)S(1)}, bf16[160,256]{1,0:T(8,128)(2,1)S(1)}, u32[]{:S(2)}, u32[]{:S(2)}) %collective-permute-start.11) | collective-permute-done | bytes 81952 | tf_op jit(solution)/shard_map/ppermute | solution.py:29
  94.5 0.0 collective-permute-done.12
  94.6 1.6 %collective-permute-start.13 = (bf16[320,256]{1,0:T(8,128)(2,1)S(1)}, bf16[320,256]{1,0:T(8,128)(2,1)S(1)}, u32[]{:S(2)}, u32[]{:S(2)}) collective-permute-start(bf16[320,256]{1,0:T(8,128)(2,1)S(1)} %get-tuple-element.39), channel_id=1, source_target_pairs={{0,8},{8,16},{16,24},{24,32},{32,40},{40,48},{48,56},{56,0},{1,9},... | collective-permute-start | bytes 491528 | tf_op jit(solution)/shard_map/ppermute | solution.py:29
  96.3 1.7 %collective-permute-start.14 = (bf16[320,256]{1,0:T(8,128)(2,1)S(1)}, bf16[320,256]{1,0:T(8,128)(2,1)S(1)}, u32[]{:S(2)}, u32[]{:S(2)}) collective-permute-start(bf16[320,256]{1,0:T(8,128)(2,1)S(1)} %get-tuple-element.40), channel_id=1, source_target_pairs={{0,56},{8,0},{16,8},{24,16},{32,24},{40,32},{48,40},{56,48},{1,57}... | collective-permute-start | bytes 491528 | tf_op jit(solution)/shard_map/ppermute | solution.py:29
  97.9 8.0 %collective-permute-done.13 = bf16[320,256]{1,0:T(8,128)(2,1)S(1)} collective-permute-done((bf16[320,256]{1,0:T(8,128)(2,1)S(1)}, bf16[320,256]{1,0:T(8,128)(2,1)S(1)}, u32[]{:S(2)}, u32[]{:S(2)}) %collective-permute-start.13) | collective-permute-done | bytes 163872 | tf_op jit(solution)/shard_map/ppermute | solution.py:29
  105.9 0.4 collective-permute-done.14
  106.4 0.1 fusion.6
  106.5 3.3 %collective-permute-start.15 = (bf16[320,256]{1,0:T(8,128)(2,1)S(1)}, bf16[320,256]{1,0:T(8,128)(2,1)S(1)}, u32[]{:S(2)}, u32[]{:S(2)}) collective-permute-start(bf16[320,256]{1,0:T(8,128)(2,1)S(1)} %get-tuple-element.41), channel_id=1, source_target_pairs={{0,8},{8,16},{16,24},{24,32},{32,40},{40,48},{48,56},{56,0},{1,9},... | collective-permute-start | bytes 491528 | tf_op jit(solution)/shard_map/ppermute | solution.py:29
  109.8 0.0 collective-permute-start.16
  109.8 7.7 %collective-permute-done.15 = bf16[320,256]{1,0:T(8,128)(2,1)S(1)} collective-permute-done((bf16[320,256]{1,0:T(8,128)(2,1)S(1)}, bf16[320,256]{1,0:T(8,128)(2,1)S(1)}, u32[]{:S(2)}, u32[]{:S(2)}) %collective-permute-start.15) | collective-permute-done | bytes 163872 | tf_op jit(solution)/shard_map/ppermute | solution.py:29
  117.5 1.7 %collective-permute-done.16 = bf16[320,256]{1,0:T(8,128)(2,1)S(1)} collective-permute-done((bf16[320,256]{1,0:T(8,128)(2,1)S(1)}, bf16[320,256]{1,0:T(8,128)(2,1)S(1)}, u32[]{:S(2)}, u32[]{:S(2)}) %collective-permute-start.16) | collective-permute-done | bytes 163872 | tf_op jit(solution)/shard_map/ppermute | solution.py:29
  119.2 0.1 fusion.4
  119.3 1.9 %collective-permute-start.17 = (bf16[320,256]{1,0:T(8,128)(2,1)S(1)}, bf16[320,256]{1,0:T(8,128)(2,1)S(1)}, u32[]{:S(2)}, u32[]{:S(2)}) collective-permute-start(bf16[320,256]{1,0:T(8,128)(2,1)S(1)} %get-tuple-element.43), channel_id=1, source_target_pairs={{0,8},{8,16},{16,24},{24,32},{32,40},{40,48},{48,56},{56,0},{1,9},... | collective-permute-start | bytes 491528 | tf_op jit(solution)/shard_map/ppermute | solution.py:29
  121.2 1.5 collective-permute-start.18
  122.6 1.4 collective-permute-done.19.other_c
  124.0 8.5 %all-to-all-start = ((bf16[8,192,128]{2,1,0:T(8,128)(2,1)}), bf16[8,192,128]{2,1,0:T(8,128)(2,1)S(1)}, u32[]{:S(2)}, u32[]{:S(2)}) async-start(bf16[8,192,128]{2,1,0:T(8,128)(2,1)} %bitcast.101), calls=%async_computation.2 | async-start | bytes 786432 | tf_op jit(solution)/shard_map/all_to_all | solution.py:240
  132.5 1.0 fusion.11
  133.5 1.2 collective-permute-start.20
  134.7 12.2 %shard_map.129 = (bf16[256,512]{1,0:T(8,128)(2,1)}, bf16[256,8192]{1,0:T(8,128)(2,1)}) custom-call(s32[3]{0:T(128)} %pad_add_fusion.place, bf16[256,8192]{1,0:T(8,128)(2,1)} %bitcast.114, bf16[256,512]{1,0:T(8,128)(2,1)} %bitcast.117, bf16[8,4,256,256]{3,2,1,0:T(8,128)(2,1)} %bitcast.115, bf16[8,4,128,256]{3,2,1,0:T(8,128)(2,1)} %bitcast.14.weight_c, ...), custom_call_target="tpu_custom_call" | custom-call | flops 4294967296 | bytes 16777216 | tf_op jit(solution)/shard_map/pallas_call | solution.py:154
  146.9 1.1 all-to-all-done
  148.0 0.1 convert_reduce_fusion
  148.1 0.8 copy.15
  (34 shorter events, 0.3 us)
Async XLA Ops:
  8.0 55.2 %all-gather.5.cloned.1.call-start = ((), (), s32[]{:S(2)}) async-start(), calls=%async_computation.5 | async-start | bytes 2359296 | tf_op jit(solution)/shard_map/all_gather | solution.py:204
  8.9 5.8 %collective-permute-start = (bf16[128,256]{1,0:T(8,128)(2,1)S(1)}, bf16[128,256]{1,0:T(8,128)(2,1)S(1)}, u32[]{:S(2)}, u32[]{:S(2)}) collective-permute-start(bf16[128,256]{1,0:T(8,128)(2,1)S(1)} %get-tuple-element.77), channel_id=1, source_target_pairs={{0,6},{2,0},{4,2},{6,4},{1,7},{3,1},{5,3},{7,5},{8,14},{10,8},{12,... | collective-permute-start | bytes 196616 | tf_op jit(solution)/shard_map/ppermute | solution.py:29
  11.8 5.8 %collective-permute-start.1 = (bf16[128,256]{1,0:T(8,128)(2,1)S(1)}, bf16[128,256]{1,0:T(8,128)(2,1)S(1)}, u32[]{:S(2)}, u32[]{:S(2)}) collective-permute-start(bf16[128,256]{1,0:T(8,128)(2,1)S(1)} %get-tuple-element.77), channel_id=1, source_target_pairs={{0,4},{2,6},{4,0},{6,2},{1,5},{3,7},{5,1},{7,3},{8,12},{10,14},{12... | collective-permute-start | bytes 196616 | tf_op jit(solution)/shard_map/ppermute | solution.py:29
  12.6 5.7 %collective-permute-start.2 = (bf16[128,256]{1,0:T(8,128)(2,1)S(1)}, bf16[128,256]{1,0:T(8,128)(2,1)S(1)}, u32[]{:S(2)}, u32[]{:S(2)}) collective-permute-start(bf16[128,256]{1,0:T(8,128)(2,1)S(1)} %get-tuple-element.77), channel_id=1, source_target_pairs={{0,2},{2,4},{4,6},{6,0},{1,3},{3,5},{5,7},{7,1},{8,10},{10,12},{12... | collective-permute-start | bytes 196616 | tf_op jit(solution)/shard_map/ppermute | solution.py:29
  13.5 5.5 %collective-permute-start.3 = (bf16[128,256]{1,0:T(8,128)(2,1)S(1)}, bf16[128,256]{1,0:T(8,128)(2,1)S(1)}, u32[]{:S(2)}, u32[]{:S(2)}) collective-permute-start(bf16[128,256]{1,0:T(8,128)(2,1)S(1)} %get-tuple-element.75), channel_id=1, source_target_pairs={{0,1},{1,0},{2,3},{3,2},{4,5},{5,4},{6,7},{7,6},{8,9},{9,8},{10,11... | collective-permute-start | bytes 196616 | tf_op jit(solution)/shard_map/ppermute | solution.py:29
  19.0 66.3 %reduce-scatter.3.cloned.1.call-start = ((), (), s32[]{:S(2)}) async-start(), calls=%async_computation.3 | async-start | bytes 6553600 | tf_op jit(solution)/shard_map/reduce_scatter | solution.py:207
  26.3 1.5 copy-start.4
  26.3 35.1 %copy-start = (bf16[4,8,192,128]{3,2,1,0:T(8,128)(2,1)S(1)}, bf16[4,8,192,128]{3,2,1,0:T(8,128)(2,1)}, u32[]{:S(2)}) copy-start(bf16[4,8,192,128]{3,2,1,0:T(8,128)(2,1)} %get-tuple-element.32) | copy-start | bytes 4718596
  26.3 96.3 %reduce-scatter.5.cloned.1.call-start = ((), (), s32[]{:S(2)}) async-start(), calls=%async_computation.4 | async-start | bytes 1966080 | tf_op jit(solution)/shard_map/reduce_scatter | solution.py:217
  26.4 35.0 %collective-permute-start.7 = (bf16[4,8,192,128]{3,2,1,0:T(8,128)(2,1)}, bf16[4,8,192,128]{3,2,1,0:T(8,128)(2,1)S(1)}, u32[]{:S(2)}, u32[]{:S(2)}) collective-permute-start(bf16[4,8,192,128]{3,2,1,0:T(8,128)(2,1)} %get-tuple-element.30), channel_id=1, source_target_pairs={{0,1},{1,0},{2,3},{3,2},{4,5},{5,4},{6,7},{7,6},{8,9},{9,8},{10,11... | collective-permute-start | bytes 4718600 | tf_op jit(solution)/shard_map/ppermute | solution.py:29
  27.8 5.0 %collective-permute-start.4 = (bf16[256,256]{1,0:T(8,128)(2,1)S(1)}, bf16[256,256]{1,0:T(8,128)(2,1)S(1)}, u32[]{:S(2)}, u32[]{:S(2)}) collective-permute-start(bf16[256,256]{1,0:T(8,128)(2,1)S(1)} %get-tuple-element.74), channel_id=1, source_target_pairs={{0,6},{2,0},{4,2},{6,4},{1,7},{3,1},{5,3},{7,5},{8,14},{10,8},{12,... | collective-permute-start | bytes 393224 | tf_op jit(solution)/shard_map/ppermute | solution.py:29
  29.0 6.5 %collective-permute-start.5 = (bf16[256,256]{1,0:T(8,128)(2,1)S(1)}, bf16[256,256]{1,0:T(8,128)(2,1)S(1)}, u32[]{:S(2)}, u32[]{:S(2)}) collective-permute-start(bf16[256,256]{1,0:T(8,128)(2,1)S(1)} %get-tuple-element.74), channel_id=1, source_target_pairs={{0,4},{2,6},{4,0},{6,2},{1,5},{3,7},{5,1},{7,3},{8,12},{10,14},{12... | collective-permute-start | bytes 393224 | tf_op jit(solution)/shard_map/ppermute | solution.py:29
  30.5 6.4 %collective-permute-start.6 = (bf16[256,256]{1,0:T(8,128)(2,1)S(1)}, bf16[256,256]{1,0:T(8,128)(2,1)S(1)}, u32[]{:S(2)}, u32[]{:S(2)}) collective-permute-start(bf16[256,256]{1,0:T(8,128)(2,1)S(1)} %get-tuple-element.74), channel_id=1, source_target_pairs={{0,2},{2,4},{4,6},{6,0},{1,3},{3,5},{5,7},{7,1},{8,10},{10,12},{12... | collective-permute-start | bytes 393224 | tf_op jit(solution)/shard_map/ppermute | solution.py:29
  61.4 2.5 %copy-start.5 = (f32[1,16,64]{2,1,0:T(8,128)S(1)}, f32[1,16,64]{2,1,0:T(8,128)}, u32[]{:S(2)}) copy-start(f32[1,16,64]{2,1,0:T(8,128)} %param.15) | copy-start | bytes 12292
  61.4 2.7 %copy-start.6 = (s32[1,16,64]{2,1,0:T(8,128)S(1)}, s32[1,16,64]{2,1,0:T(8,128)}, u32[]{:S(2)}) copy-start(s32[1,16,64]{2,1,0:T(8,128)} %param.13) | copy-start | bytes 12292
  63.1 1.2 copy-start.7
  63.1 1.4 copy-start.1
  63.1 14.7 %copy-start.2 = (f32[16,8192]{1,0:T(8,128)S(1)}, f32[16,8192]{1,0:T(8,128)}, u32[]{:S(2)}) copy-start(f32[16,8192]{1,0:T(8,128)} %param.17) | copy-start | bytes 1572868
  63.1 14.7 %copy-start.3 = (f32[16,8192]{1,0:T(8,128)S(1)}, f32[16,8192]{1,0:T(8,128)}, u32[]{:S(2)}) copy-start(f32[16,8192]{1,0:T(8,128)} %param.16) | copy-start | bytes 1572868
  63.1 71.5 %all-gather.7.cloned.1.call-start = ((), (), s32[]{:S(2)}) async-start(), calls=%async_computation.6 | async-start | bytes 4718592 | tf_op jit(solution)/shard_map/all_gather | solution.py:220
  65.4 10.3 %collective-permute-start.10 = (bf16[16,8192]{1,0:T(8,128)(2,1)S(1)}, bf16[16,8192]{1,0:T(8,128)(2,1)S(1)}, u32[]{:S(2)}, u32[]{:S(2)}) collective-permute-start(bf16[16,8192]{1,0:T(8,128)(2,1)S(1)} %fusion), channel_id=1, source_target_pairs={{0,192},{64,128},{128,64},{192,0},{1,193},{65,129},{129,65},{193,1... | collective-permute-start | bytes 786440 | tf_op jit(solution)/shard_map/ppermute | solution.py:40
  65.5 10.2 %collective-permute-start.8 = (bf16[16,8192]{1,0:T(8,128)(2,1)S(1)}, bf16[16,8192]{1,0:T(8,128)(2,1)S(1)}, u32[]{:S(2)}, u32[]{:S(2)}) collective-permute-start(bf16[16,8192]{1,0:T(8,128)(2,1)S(1)} %fusion), channel_id=1, source_target_pairs={{0,64},{64,0},{1,65},{65,1},{2,66},{66,2},{3,67},{67,3},{4,68},{68... | collective-permute-start | bytes 786440 | tf_op jit(solution)/shard_map/ppermute | solution.py:29
  65.9 11.9 %collective-permute-start.9 = (bf16[16,8192]{1,0:T(8,128)(2,1)S(1)}, bf16[16,8192]{1,0:T(8,128)(2,1)S(1)}, u32[]{:S(2)}, u32[]{:S(2)}) collective-permute-start(bf16[16,8192]{1,0:T(8,128)(2,1)S(1)} %fusion), channel_id=1, source_target_pairs={{0,128},{128,0},{1,129},{129,1},{2,130},{130,2},{3,131},{131,3},{4... | collective-permute-start | bytes 786440 | tf_op jit(solution)/shard_map/ppermute | solution.py:29
  69.1 54.9 %collective-permute-start.19 = (bf16[8,4,128,256]{3,2,1,0:T(8,128)(2,1)}, bf16[8,4,128,256]{3,2,1,0:T(8,128)(2,1)}, u32[]{:S(2)}, u32[]{:S(2)}) collective-permute-start(bf16[8,4,128,256]{3,2,1,0:T(8,128)(2,1)} %bitcast.14.weight_c), channel_id=1, source_target_pairs={{0,1},{1,0},{2,3},{3,2},{4,5},{5,4},{6,7},{7,6},{8,9},{9,8},{10,11... | collective-permute-start | bytes 6291464 | tf_op jit(solution)/shard_map/ppermute | solution.py:29
  86.4 8.2 %collective-permute-start.11 = (bf16[160,256]{1,0:T(8,128)(2,1)S(1)}, bf16[160,256]{1,0:T(8,128)(2,1)S(1)}, u32[]{:S(2)}, u32[]{:S(2)}) collective-permute-start(bf16[160,256]{1,0:T(8,128)(2,1)S(1)} %get-tuple-element.70), channel_id=1, source_target_pairs={{0,8},{8,16},{16,24},{24,32},{32,40},{40,48},{48,56},{56,0},{1,9},... | collective-permute-start | bytes 245768 | tf_op jit(solution)/shard_map/ppermute | solution.py:29
  88.0 6.5 %collective-permute-start.12 = (bf16[160,256]{1,0:T(8,128)(2,1)S(1)}, bf16[160,256]{1,0:T(8,128)(2,1)S(1)}, u32[]{:S(2)}, u32[]{:S(2)}) collective-permute-start(bf16[160,256]{1,0:T(8,128)(2,1)S(1)} %get-tuple-element.68), channel_id=1, source_target_pairs={{0,56},{8,0},{16,8},{24,16},{32,24},{40,32},{48,40},{56,48},{1,57}... | collective-permute-start | bytes 245768 | tf_op jit(solution)/shard_map/ppermute | solution.py:29
  94.6 11.3 %collective-permute-start.13 = (bf16[320,256]{1,0:T(8,128)(2,1)S(1)}, bf16[320,256]{1,0:T(8,128)(2,1)S(1)}, u32[]{:S(2)}, u32[]{:S(2)}) collective-permute-start(bf16[320,256]{1,0:T(8,128)(2,1)S(1)} %get-tuple-element.39), channel_id=1, source_target_pairs={{0,8},{8,16},{16,24},{24,32},{32,40},{40,48},{48,56},{56,0},{1,9},... | collective-permute-start | bytes 491528 | tf_op jit(solution)/shard_map/ppermute | solution.py:29
  96.3 10.1 %collective-permute-start.14 = (bf16[320,256]{1,0:T(8,128)(2,1)S(1)}, bf16[320,256]{1,0:T(8,128)(2,1)S(1)}, u32[]{:S(2)}, u32[]{:S(2)}) collective-permute-start(bf16[320,256]{1,0:T(8,128)(2,1)S(1)} %get-tuple-element.40), channel_id=1, source_target_pairs={{0,56},{8,0},{16,8},{24,16},{32,24},{40,32},{48,40},{56,48},{1,57}... | collective-permute-start | bytes 491528 | tf_op jit(solution)/shard_map/ppermute | solution.py:29
  106.5 11.0 %collective-permute-start.15 = (bf16[320,256]{1,0:T(8,128)(2,1)S(1)}, bf16[320,256]{1,0:T(8,128)(2,1)S(1)}, u32[]{:S(2)}, u32[]{:S(2)}) collective-permute-start(bf16[320,256]{1,0:T(8,128)(2,1)S(1)} %get-tuple-element.41), channel_id=1, source_target_pairs={{0,8},{8,16},{16,24},{24,32},{32,40},{40,48},{48,56},{56,0},{1,9},... | collective-permute-start | bytes 491528 | tf_op jit(solution)/shard_map/ppermute | solution.py:29
  109.8 9.5 %collective-permute-start.16 = (bf16[320,256]{1,0:T(8,128)(2,1)S(1)}, bf16[320,256]{1,0:T(8,128)(2,1)S(1)}, u32[]{:S(2)}, u32[]{:S(2)}) collective-permute-start(bf16[320,256]{1,0:T(8,128)(2,1)S(1)} %get-tuple-element.42), channel_id=1, source_target_pairs={{0,56},{8,0},{16,8},{24,16},{32,24},{40,32},{48,40},{56,48},{1,57}... | collective-permute-start | bytes 491528 | tf_op jit(solution)/shard_map/ppermute | solution.py:29
  119.3 13.2 %collective-permute-start.17 = (bf16[320,256]{1,0:T(8,128)(2,1)S(1)}, bf16[320,256]{1,0:T(8,128)(2,1)S(1)}, u32[]{:S(2)}, u32[]{:S(2)}) collective-permute-start(bf16[320,256]{1,0:T(8,128)(2,1)S(1)} %get-tuple-element.43), channel_id=1, source_target_pairs={{0,8},{8,16},{16,24},{24,32},{32,40},{40,48},{48,56},{56,0},{1,9},... | collective-permute-start | bytes 491528 | tf_op jit(solution)/shard_map/ppermute | solution.py:29
  121.2 11.3 %collective-permute-start.18 = (bf16[320,256]{1,0:T(8,128)(2,1)S(1)}, bf16[320,256]{1,0:T(8,128)(2,1)}, u32[]{:S(2)}, u32[]{:S(2)}) collective-permute-start(bf16[320,256]{1,0:T(8,128)(2,1)S(1)} %get-tuple-element.44), channel_id=1, source_target_pairs={{0,56},{8,0},{16,8},{24,16},{32,24},{40,32},{48,40},{56,48},{1,57}... | collective-permute-start | bytes 491528 | tf_op jit(solution)/shard_map/ppermute | solution.py:29
  124.0 24.0 %all-to-all-start = ((bf16[8,192,128]{2,1,0:T(8,128)(2,1)}), bf16[8,192,128]{2,1,0:T(8,128)(2,1)S(1)}, u32[]{:S(2)}, u32[]{:S(2)}) async-start(bf16[8,192,128]{2,1,0:T(8,128)(2,1)} %bitcast.101), calls=%async_computation.2 | async-start | bytes 786432 | tf_op jit(solution)/shard_map/all_to_all | solution.py:240
  133.5 13.4 %collective-permute-start.20 = (bf16[320,128]{1,0:T(8,128)(2,1)S(1)}, bf16[320,128]{1,0:T(8,128)(2,1)S(1)}, u32[]{:S(2)}, u32[]{:S(2)}) collective-permute-start(bf16[320,128]{1,0:T(8,128)(2,1)S(1)} %select_convert_fusion), channel_id=1, source_target_pairs={{0,1},{1,0},{2,3},{3,2},{4,5},{5,4},{6,7},{7,6},{8,9},{9,8},{10,11... | collective-permute-start | bytes 245768 | tf_op jit(solution)/shard_map/ppermute | solution.py:29
Sparse Core Ops, SparseCore 0:
  19.1 42.3 all-gather.4
  65.8 68.6 all-gather.6
Sparse Core Ops, SparseCore 1:
  26.4 58.9 reduce-scatter.2
  88.3 27.8 reduce-scatter.4

commit v3 on v2

--- a/solution.py
+++ b/solution.py
@@ -114,61 +114,79 @@
     )(place, tokens, cot)
 
 
-def product_kernel(place, tokens, cot, weight_a, weight_c, other_c, keys, back, total):
-    j = pl.program_id(0)
-    part = weight_c.shape[2]
+def product_kernel(
+    place, tokens, cot, weight_a, weight_c, other_c, keys, back,
+    columns, cot_rows, a, c, other, backs, total, sems
+):
+    part = c.shape[2]
+    width = columns.shape[2]
+    load = pltpu.make_async_copy(cot, cot_rows, sems.at[0, Z])
+    load.start()
+    loads = []
+    for j in range(Z):
+        moves = (
+            (weight_a.at[j], a.at[j]),
+            (weight_c.at[j], c.at[j]),
+            (other_c.at[j], other.at[j]),
+            (tokens.at[:, j * width : (j + 1) * width], columns.at[j]),
+        )
+        loads.append(
+            [pltpu.make_async_copy(*move, sems.at[i, j]) for i, move in enumerate(moves)]
+        )
+        for move in loads[j]:
+            move.start()
+    load.wait()
     first = place[2] == 0
-    added = None
-    for k in range(X):
-        columns = slice(k * Y * part, (k + 1) * Y * part)
-        at = lax.rem(k - place[1] + X, X)
-        mine, theirs = weight_c[0, at], other_c[0, at]
-        right = jnp.concatenate(
-            [jnp.where(first, mine, theirs), jnp.where(first, theirs, mine)], axis=0
-        )
-        weight = jnp.concatenate([weight_a[0, at], right], axis=1)
-        product = jnp.dot(tokens[:, columns], weight, preferred_element_type=F32)
-        added = product if added is None else added + product
-        back[:, columns] = lax.dot_general(
-            cot[...], weight, (((1,), (1,)), ((), ())), preferred_element_type=F32
-        ).astype(BF16)
-
-    @pl.when(j == 0)
-    def _():
-        total[...] = added
-
-    @pl.when(j > 0)
-    def _():
-        total[...] += added
-
-    @pl.when(j == Z - 1)
-    def _():
-        keys[...] = total[...].astype(BF16)
+    stores = []
+    for j in range(Z):
+        for move in loads[j]:
+            move.wait()
+        added = None
+        for k in range(X):
+            block = slice(k * Y * part, (k + 1) * Y * part)
+            at = lax.rem(k - place[1] + X, X)
+            mine, theirs = c[j, at], other[j, at]
+            lower, upper = jnp.where(first, mine, theirs), jnp.where(first, theirs, mine)
+            weight = jnp.concatenate([a[j, at], jnp.concatenate([lower, upper])], axis=1)
+            product = jnp.dot(columns[j, :, block], weight, preferred_element_type=F32)
+            added = product if added is None else added + product
+            backs[j, :, block] = lax.dot_general(
+                cot_rows[...], weight, (((1,), (1,)), ((), ())), preferred_element_type=F32
+            ).astype(BF16)
+        if j == 0:
+            total[...] = added
+        elif j < Z - 1:
+            total[...] += added
+        else:
+            keys[...] = (total[...] + added).astype(BF16)
+        stores.append(
+            pltpu.make_async_copy(
+                backs.at[j], back.at[:, j * width : (j + 1) * width], sems.at[4, j]
+            )
+        )
+        stores[j].start()
+    for store in stores:
+        store.wait()
 
 
 def products(place, tokens, cot, weight_a, weight_c, other_c):
     rows, width = tokens.shape
     heads = cot.shape[1]
-    part = weight_c.shape[2]
-    by_z = lambda j, place: (j, 0, 0, 0)
+    anywhere = pl.BlockSpec(memory_space=pl.ANY)
     return pl.pallas_call(
         product_kernel,
-        grid_spec=pltpu.PrefetchScalarGridSpec(
-            num_scalar_prefetch=1,
-            grid=(Z,),
-            in_specs=[
-                pl.BlockSpec((rows, width // Z), lambda j, place: (0, j)),
-                pl.BlockSpec((rows, heads), lambda j, place: (0, 0)),
-                pl.BlockSpec((1, X, Y * part, WEIGHT_SPLIT), by_z),
-                pl.BlockSpec((1, X, part, heads - WEIGHT_SPLIT), by_z),
-                pl.BlockSpec((1, X, part, heads - WEIGHT_SPLIT), by_z),
-            ],
-            out_specs=[
-                pl.BlockSpec((rows, heads), lambda j, place: (0, 0)),
-                pl.BlockSpec((rows, width // Z), lambda j, place: (0, j)),
-            ],
-            scratch_shapes=[pltpu.VMEM((rows, heads), F32)],
-        ),
+        in_specs=[pl.BlockSpec(memory_space=pltpu.SMEM)] + [anywhere] * 5,
+        out_specs=[pl.BlockSpec(memory_space=pltpu.VMEM), anywhere],
+        scratch_shapes=[
+            pltpu.VMEM((Z, rows, width // Z), BF16),
+            pltpu.VMEM((rows, heads), BF16),
+            pltpu.VMEM(weight_a.shape, BF16),
+            pltpu.VMEM(weight_c.shape, BF16),
+            pltpu.VMEM(weight_c.shape, BF16),
+            pltpu.VMEM((Z, rows, width // Z), BF16),
+            pltpu.VMEM((rows, heads), F32),
+            pltpu.SemaphoreType.DMA((5, Z + 1)),
+        ],
         out_shape=[
             jax.ShapeDtypeStruct((rows, heads), BF16),
             jax.ShapeDtypeStruct((rows, width), BF16),

time: 158 us -> 157 us (level)
  Pallas kernels: 18.8 us -> 16.6 us
  waiting for transfers between devices: 71.3 us -> 73.3 us
    pallas_call x1, Pallas kernels: 12.2 us -> 10 us  [products(): pl.pallas_call(product_kernel, in_specs=[pl.BlockSpec(memory_space=pltpu....]
    all_to_all x1, waiting for transfers between devices: 1.1 us -> 3.06 us  [local(): grad_c = lax.all_to_all(after(grad_c_x, up, other_c), 'z', 0, 0, tiled=True)]
  transfers between devices with their start and end apart: 26 -> 26, of which waited for: 16 -> 16; matrix products, arithmetic and copies ran while one was open for 7% -> 7% of each run, Pallas kernels for 12% -> 11%
where the time goes in v3:
time: 157 us; the launch traced here: 156 us
  waiting for transfers between devices  73.3 us (47%)
  starting transfers between devices  38.5 us (25%)
  Pallas kernels  16.6 us (11%)
  between operations  15.7 us (10%)
  other arithmetic  8.96 us (6%)
  local copies, waits for them, and re-layouts  3.36 us (2%)
    ppermute x20, waiting for transfers between devices, shift(): lax.ppermute(block, axis, [(i, (i + by) % size) for i in range(size)])  57.9 us
    ppermute x20, starting transfers between devices, shift(): lax.ppermute(block, axis, [(i, (i + by) % size) for i in range(size)])  29.8 us
    pallas_call x1, Pallas kernels, products(): pl.pallas_call(product_kernel, in_specs=[pl.BlockSpec(memory_space=pltpu....  10 us
    all_to_all x1, starting transfers between devices, local(): grad_c = lax.all_to_all(after(grad_c_x, up, other_c), 'z', 0, 0, tiled=True)  8.46 us
    pallas_call x1, Pallas kernels, gradients(): pl.pallas_call(grad_kernel, in_specs=[pl.BlockSpec(memory_space=pltpu.SME...  6.55 us
    reduce_scatter x1, waiting for transfers between devices, local(): grad_a = lax.psum_scatter(grad_a, 'x', scatter_dimension=0, tiled=True)[0]  6.31 us
    ppermute x1, waiting for transfers between devices, outer_values(): far_core = lax.ppermute(values, ('yh', 'c'), [(i, 3 - i) for i in range(4)])  5.25 us
  transfers between devices with their start and end apart: 26, of which 16 were waited for; matrix products, arithmetic and copies ran while one was open for 7% of the time, Pallas kernels for 11%

profile of v3, /device:TPU:16, one launch (start us, length us, event | category | flops | bytes accessed | tf_op | source)
XLA Modules:
  0.0 156.4 jit_solution(10594628787989736464)
XLA Ops:
  8.0 0.0 all-gather.5.cloned.1.call-start
  8.0 0.9 fusion.18
  8.9 2.8 %collective-permute-start = (bf16[128,256]{1,0:T(8,128)(2,1)S(1)}, bf16[128,256]{1,0:T(8,128)(2,1)S(1)}, u32[]{:S(2)}, u32[]{:S(2)}) collective-permute-start(bf16[128,256]{1,0:T(8,128)(2,1)S(1)} %get-tuple-element.77), channel_id=1, source_target_pairs={{0,6},{2,0},{4,2},{6,4},{1,7},{3,1},{5,3},{7,5},{8,14},{10,8},{12,... | collective-permute-start | bytes 196616 | tf_op jit(solution)/shard_map/ppermute | solution.py:29
  11.8 0.8 collective-permute-start.1
  12.6 0.9 collective-permute-start.2
  13.5 1.3 collective-permute-start.3
  14.7 2.8 %collective-permute-done.1 = bf16[128,256]{1,0:T(8,128)(2,1)S(1)} collective-permute-done((bf16[128,256]{1,0:T(8,128)(2,1)S(1)}, bf16[128,256]{1,0:T(8,128)(2,1)S(1)}, u32[]{:S(2)}, u32[]{:S(2)}) %collective-permute-start.1) | collective-permute-done | bytes 65568 | tf_op jit(solution)/shard_map/ppermute | solution.py:29
  17.6 0.7 collective-permute-done.2
  18.2 0.7 pad_maximum_fusion.1
  19.0 0.0 all-gather.5.cloned.1.call-update
  19.0 0.0 reduce-scatter.3.cloned.1.call-start
  19.1 0.7 pad_add_fusion.place
  19.7 6.5 %shard_map.128 = (bf16[4,8,320,256]{3,2,1,0:T(8,128)(2,1)}, bf16[4,8,192,128]{3,2,1,0:T(8,128)(2,1)}, bf16[4,8,192,128]{3,2,1,0:T(8,128)(2,1)}) custom-call(s32[3]{0:T(128)} %pad_add_fusion.place, bf16[256,8192]{1,0:T(8,128)(2,1)} %bitcast.113, bf16[256,512]{1,0:T(8,128)(2,1)} %bitcast.116), custom_call_target="tpu_custom_call" | custom-call | flops 2147483648 | bytes 12582912 | tf_op jit(solution)/shard_map/pallas_call | solution.py:96
  26.3 0.0 reduce-scatter.5.cloned.1.call-start
  26.4 1.4 collective-permute-start.7
  27.8 1.2 collective-permute-start.4
  29.0 1.5 collective-permute-start.5
  30.5 0.1 collective-permute-start.6
  30.6 2.2 %collective-permute-done.4 = bf16[256,256]{1,0:T(8,128)(2,1)S(1)} collective-permute-done((bf16[256,256]{1,0:T(8,128)(2,1)S(1)}, bf16[256,256]{1,0:T(8,128)(2,1)S(1)}, u32[]{:S(2)}, u32[]{:S(2)}) %collective-permute-start.4) | collective-permute-done | bytes 131104 | tf_op jit(solution)/shard_map/ppermute | solution.py:29
  32.8 2.6 %collective-permute-done.5 = bf16[256,256]{1,0:T(8,128)(2,1)S(1)} collective-permute-done((bf16[256,256]{1,0:T(8,128)(2,1)S(1)}, bf16[256,256]{1,0:T(8,128)(2,1)S(1)}, u32[]{:S(2)}, u32[]{:S(2)}) %collective-permute-start.5) | collective-permute-done | bytes 131104 | tf_op jit(solution)/shard_map/ppermute | solution.py:29
  35.4 1.4 collective-permute-done.6
  36.8 0.9 pad_maximum_fusion
  37.7 23.7 %collective-permute-done.7 = bf16[4,8,192,128]{3,2,1,0:T(8,128)(2,1)S(1)} collective-permute-done((bf16[4,8,192,128]{3,2,1,0:T(8,128)(2,1)}, bf16[4,8,192,128]{3,2,1,0:T(8,128)(2,1)S(1)}, u32[]{:S(2)}, u32[]{:S(2)}) %collective-permute-start.7) | collective-permute-done | bytes 1572896 | tf_op jit(solution)/shard_map/ppermute | solution.py:29
  61.4 1.7 %add_convert_fusion = bf16[4,8,192,128]{3,2,1,0:T(8,128)(2,1)} fusion(bf16[4,8,192,128]{3,2,1,0:T(8,128)(2,1)S(1)} %collective-permute-done.7, bf16[4,8,192,128]{3,2,1,0:T(8,128)(2,1)S(1)} %copy-done), kind=kLoop, calls=%fused_computation | loop fusion | flops 3145728 | bytes 4718592 | tf_op jit(solution)/shard_map/convert_element_type | solution.py:234
  63.1 0.0 all-gather.7.cloned.1.call-start
  63.2 0.7 all-gather.7.cloned.1.call-update
  63.9 0.2 mul.35
  64.1 0.2 sub.17
  64.3 0.2 add.64
  64.5 0.9 fusion
  65.4 0.1 collective-permute-start.10
  65.5 0.4 collective-permute-start.8
  65.9 3.2 %collective-permute-start.9 = (bf16[16,8192]{1,0:T(8,128)(2,1)S(1)}, bf16[16,8192]{1,0:T(8,128)(2,1)S(1)}, u32[]{:S(2)}, u32[]{:S(2)}) collective-permute-start(bf16[16,8192]{1,0:T(8,128)(2,1)S(1)} %fusion), channel_id=1, source_target_pairs={{0,128},{128,0},{1,129},{129,1},{2,130},{130,2},{3,131},{131,3},{4... | collective-permute-start | bytes 786440 | tf_op jit(solution)/shard_map/ppermute | solution.py:29
  69.1 1.3 collective-permute-start.19
  70.4 5.2 %collective-permute-done.10 = bf16[16,8192]{1,0:T(8,128)(2,1)S(1)} collective-permute-done((bf16[16,8192]{1,0:T(8,128)(2,1)S(1)}, bf16[16,8192]{1,0:T(8,128)(2,1)S(1)}, u32[]{:S(2)}, u32[]{:S(2)}) %collective-permute-start.10) | collective-permute-done | bytes 262176 | tf_op jit(solution)/shard_map/ppermute | solution.py:40
  75.7 2.1 %collective-permute-done.9 = bf16[16,8192]{1,0:T(8,128)(2,1)S(1)} collective-permute-done((bf16[16,8192]{1,0:T(8,128)(2,1)S(1)}, bf16[16,8192]{1,0:T(8,128)(2,1)S(1)}, u32[]{:S(2)}, u32[]{:S(2)}) %collective-permute-start.9) | collective-permute-done | bytes 262176 | tf_op jit(solution)/shard_map/ppermute | solution.py:29
  77.8 1.2 multiply_subtract_fusion
  79.0 6.3 %reduce-scatter.3.cloned.1.call-done = bf16[1,8,320,256]{3,2,1,0:T(8,128)(2,1)} async-done(((bf16[4,8,320,256]{3,2,1,0:T(8,128)(2,1)}), bf16[1,8,320,256]{3,2,1,0:T(8,128)(2,1)}) %reduce-scatter.3.cloned.1.call-update) | async-done | bytes 1310736 | tf_op jit(solution)/shard_map/reduce_scatter | solution.py:225
  85.3 1.0 slice_bitcast_fusion.8
  86.4 1.6 %collective-permute-start.11 = (bf16[160,256]{1,0:T(8,128)(2,1)S(1)}, bf16[160,256]{1,0:T(8,128)(2,1)S(1)}, u32[]{:S(2)}, u32[]{:S(2)}) collective-permute-start(bf16[160,256]{1,0:T(8,128)(2,1)S(1)} %get-tuple-element.70), channel_id=1, source_target_pairs={{0,8},{8,16},{16,24},{24,32},{32,40},{40,48},{48,56},{56,0},{1,9},... | collective-permute-start | bytes 245768 | tf_op jit(solution)/shard_map/ppermute | solution.py:29
  88.0 1.9 %collective-permute-start.12 = (bf16[160,256]{1,0:T(8,128)(2,1)S(1)}, bf16[160,256]{1,0:T(8,128)(2,1)S(1)}, u32[]{:S(2)}, u32[]{:S(2)}) collective-permute-start(bf16[160,256]{1,0:T(8,128)(2,1)S(1)} %get-tuple-element.68), channel_id=1, source_target_pairs={{0,56},{8,0},{16,8},{24,16},{32,24},{40,32},{48,40},{56,48},{1,57}... | collective-permute-start | bytes 245768 | tf_op jit(solution)/shard_map/ppermute | solution.py:29
  89.9 1.6 %convert_element_type.87 = f32[8,320,256]{2,1,0:T(8,128)S(1)} convert(bf16[8,320,256]{2,1,0:T(8,128)(2,1)} %bitcast.99) | non-fusion elementwise | flops 655360 | bytes 3932160 | tf_op jit(solution)/shard_map/convert_element_type | solution.py:247
  91.4 3.1 %collective-permute-done.11 = bf16[160,256]{1,0:T(8,128)(2,1)S(1)} collective-permute-done((bf16[160,256]{1,0:T(8,128)(2,1)S(1)}, bf16[160,256]{1,0:T(8,128)(2,1)S(1)}, u32[]{:S(2)}, u32[]{:S(2)}) %collective-permute-start.11) | collective-permute-done | bytes 81952 | tf_op jit(solution)/shard_map/ppermute | solution.py:29
  94.5 0.0 collective-permute-done.12
  94.6 1.6 %collective-permute-start.13 = (bf16[320,256]{1,0:T(8,128)(2,1)S(1)}, bf16[320,256]{1,0:T(8,128)(2,1)S(1)}, u32[]{:S(2)}, u32[]{:S(2)}) collective-permute-start(bf16[320,256]{1,0:T(8,128)(2,1)S(1)} %get-tuple-element.39), channel_id=1, source_target_pairs={{0,8},{8,16},{16,24},{24,32},{32,40},{40,48},{48,56},{56,0},{1,9},... | collective-permute-start | bytes 491528 | tf_op jit(solution)/shard_map/ppermute | solution.py:29
  96.3 1.7 %collective-permute-start.14 = (bf16[320,256]{1,0:T(8,128)(2,1)S(1)}, bf16[320,256]{1,0:T(8,128)(2,1)S(1)}, u32[]{:S(2)}, u32[]{:S(2)}) collective-permute-start(bf16[320,256]{1,0:T(8,128)(2,1)S(1)} %get-tuple-element.40), channel_id=1, source_target_pairs={{0,56},{8,0},{16,8},{24,16},{32,24},{40,32},{48,40},{56,48},{1,57}... | collective-permute-start | bytes 491528 | tf_op jit(solution)/shard_map/ppermute | solution.py:29
  97.9 8.0 %collective-permute-done.13 = bf16[320,256]{1,0:T(8,128)(2,1)S(1)} collective-permute-done((bf16[320,256]{1,0:T(8,128)(2,1)S(1)}, bf16[320,256]{1,0:T(8,128)(2,1)S(1)}, u32[]{:S(2)}, u32[]{:S(2)}) %collective-permute-start.13) | collective-permute-done | bytes 163872 | tf_op jit(solution)/shard_map/ppermute | solution.py:29
  105.9 0.4 collective-permute-done.14
  106.4 0.1 fusion.6
  106.5 3.3 %collective-permute-start.15 = (bf16[320,256]{1,0:T(8,128)(2,1)S(1)}, bf16[320,256]{1,0:T(8,128)(2,1)S(1)}, u32[]{:S(2)}, u32[]{:S(2)}) collective-permute-start(bf16[320,256]{1,0:T(8,128)(2,1)S(1)} %get-tuple-element.41), channel_id=1, source_target_pairs={{0,8},{8,16},{16,24},{24,32},{32,40},{40,48},{48,56},{56,0},{1,9},... | collective-permute-start | bytes 491528 | tf_op jit(solution)/shard_map/ppermute | solution.py:29
  109.8 0.0 collective-permute-start.16
  109.8 7.7 %collective-permute-done.15 = bf16[320,256]{1,0:T(8,128)(2,1)S(1)} collective-permute-done((bf16[320,256]{1,0:T(8,128)(2,1)S(1)}, bf16[320,256]{1,0:T(8,128)(2,1)S(1)}, u32[]{:S(2)}, u32[]{:S(2)}) %collective-permute-start.15) | collective-permute-done | bytes 163872 | tf_op jit(solution)/shard_map/ppermute | solution.py:29
  117.5 1.7 %collective-permute-done.16 = bf16[320,256]{1,0:T(8,128)(2,1)S(1)} collective-permute-done((bf16[320,256]{1,0:T(8,128)(2,1)S(1)}, bf16[320,256]{1,0:T(8,128)(2,1)S(1)}, u32[]{:S(2)}, u32[]{:S(2)}) %collective-permute-start.16) | collective-permute-done | bytes 163872 | tf_op jit(solution)/shard_map/ppermute | solution.py:29
  119.2 0.1 fusion.4
  119.3 1.9 %collective-permute-start.17 = (bf16[320,256]{1,0:T(8,128)(2,1)S(1)}, bf16[320,256]{1,0:T(8,128)(2,1)S(1)}, u32[]{:S(2)}, u32[]{:S(2)}) collective-permute-start(bf16[320,256]{1,0:T(8,128)(2,1)S(1)} %get-tuple-element.43), channel_id=1, source_target_pairs={{0,8},{8,16},{16,24},{24,32},{32,40},{40,48},{48,56},{56,0},{1,9},... | collective-permute-start | bytes 491528 | tf_op jit(solution)/shard_map/ppermute | solution.py:29
  121.2 1.5 collective-permute-start.18
  122.6 1.4 collective-permute-done.19.other_c
  124.0 8.5 %all-to-all-start = ((bf16[8,192,128]{2,1,0:T(8,128)(2,1)}), bf16[8,192,128]{2,1,0:T(8,128)(2,1)S(1)}, u32[]{:S(2)}, u32[]{:S(2)}) async-start(bf16[8,192,128]{2,1,0:T(8,128)(2,1)} %bitcast.101), calls=%async_computation.2 | async-start | bytes 786432 | tf_op jit(solution)/shard_map/all_to_all | solution.py:258
  132.5 1.0 fusion.11
  133.5 1.4 collective-permute-start.20
  134.9 10.0 %shard_map.129 = (bf16[256,512]{1,0:T(8,128)(2,1)}, bf16[256,8192]{1,0:T(8,128)(2,1)}) custom-call(s32[3]{0:T(128)} %pad_add_fusion.place, bf16[256,8192]{1,0:T(8,128)(2,1)} %bitcast.114, bf16[256,512]{1,0:T(8,128)(2,1)} %bitcast.117, bf16[8,4,256,256]{3,2,1,0:T(8,128)(2,1)} %bitcast.115, bf16[8,4,128,256]{3,2,1,0:T(8,128)(2,1)} %bitcast.14.weight_c, ...), custom_call_target="tpu_custom_call" | custom-call | flops 4294967296 | bytes 16777216 | tf_op jit(solution)/shard_map/pallas_call | solution.py:176
  145.0 3.1 %all-to-all-done = bf16[8,192,128]{2,1,0:T(8,128)(2,1)S(1)} async-done(((bf16[8,192,128]{2,1,0:T(8,128)(2,1)}), bf16[8,192,128]{2,1,0:T(8,128)(2,1)S(1)}, u32[]{:S(2)}, u32[]{:S(2)}) %all-to-all-start) | async-done | bytes 393248 | tf_op jit(solution)/shard_map/all_to_all | solution.py:258
  148.0 0.1 convert_reduce_fusion
  148.1 0.8 copy.15
  (34 shorter events, 0.3 us)
Async XLA Ops:
  8.0 55.2 %all-gather.5.cloned.1.call-start = ((), (), s32[]{:S(2)}) async-start(), calls=%async_computation.5 | async-start | bytes 2359296 | tf_op jit(solution)/shard_map/all_gather | solution.py:222
  8.9 5.8 %collective-permute-start = (bf16[128,256]{1,0:T(8,128)(2,1)S(1)}, bf16[128,256]{1,0:T(8,128)(2,1)S(1)}, u32[]{:S(2)}, u32[]{:S(2)}) collective-permute-start(bf16[128,256]{1,0:T(8,128)(2,1)S(1)} %get-tuple-element.77), channel_id=1, source_target_pairs={{0,6},{2,0},{4,2},{6,4},{1,7},{3,1},{5,3},{7,5},{8,14},{10,8},{12,... | collective-permute-start | bytes 196616 | tf_op jit(solution)/shard_map/ppermute | solution.py:29
  11.8 5.8 %collective-permute-start.1 = (bf16[128,256]{1,0:T(8,128)(2,1)S(1)}, bf16[128,256]{1,0:T(8,128)(2,1)S(1)}, u32[]{:S(2)}, u32[]{:S(2)}) collective-permute-start(bf16[128,256]{1,0:T(8,128)(2,1)S(1)} %get-tuple-element.77), channel_id=1, source_target_pairs={{0,4},{2,6},{4,0},{6,2},{1,5},{3,7},{5,1},{7,3},{8,12},{10,14},{12... | collective-permute-start | bytes 196616 | tf_op jit(solution)/shard_map/ppermute | solution.py:29
  12.6 5.7 %collective-permute-start.2 = (bf16[128,256]{1,0:T(8,128)(2,1)S(1)}, bf16[128,256]{1,0:T(8,128)(2,1)S(1)}, u32[]{:S(2)}, u32[]{:S(2)}) collective-permute-start(bf16[128,256]{1,0:T(8,128)(2,1)S(1)} %get-tuple-element.77), channel_id=1, source_target_pairs={{0,2},{2,4},{4,6},{6,0},{1,3},{3,5},{5,7},{7,1},{8,10},{10,12},{12... | collective-permute-start | bytes 196616 | tf_op jit(solution)/shard_map/ppermute | solution.py:29
  13.5 5.5 %collective-permute-start.3 = (bf16[128,256]{1,0:T(8,128)(2,1)S(1)}, bf16[128,256]{1,0:T(8,128)(2,1)S(1)}, u32[]{:S(2)}, u32[]{:S(2)}) collective-permute-start(bf16[128,256]{1,0:T(8,128)(2,1)S(1)} %get-tuple-element.75), channel_id=1, source_target_pairs={{0,1},{1,0},{2,3},{3,2},{4,5},{5,4},{6,7},{7,6},{8,9},{9,8},{10,11... | collective-permute-start | bytes 196616 | tf_op jit(solution)/shard_map/ppermute | solution.py:29
  19.0 66.3 %reduce-scatter.3.cloned.1.call-start = ((), (), s32[]{:S(2)}) async-start(), calls=%async_computation.3 | async-start | bytes 6553600 | tf_op jit(solution)/shard_map/reduce_scatter | solution.py:225
  26.3 1.5 copy-start.4
  26.3 35.1 %copy-start = (bf16[4,8,192,128]{3,2,1,0:T(8,128)(2,1)S(1)}, bf16[4,8,192,128]{3,2,1,0:T(8,128)(2,1)}, u32[]{:S(2)}) copy-start(bf16[4,8,192,128]{3,2,1,0:T(8,128)(2,1)} %get-tuple-element.32) | copy-start | bytes 4718596
  26.3 96.3 %reduce-scatter.5.cloned.1.call-start = ((), (), s32[]{:S(2)}) async-start(), calls=%async_computation.4 | async-start | bytes 1966080 | tf_op jit(solution)/shard_map/reduce_scatter | solution.py:235
  26.4 35.0 %collective-permute-start.7 = (bf16[4,8,192,128]{3,2,1,0:T(8,128)(2,1)}, bf16[4,8,192,128]{3,2,1,0:T(8,128)(2,1)S(1)}, u32[]{:S(2)}, u32[]{:S(2)}) collective-permute-start(bf16[4,8,192,128]{3,2,1,0:T(8,128)(2,1)} %get-tuple-element.30), channel_id=1, source_target_pairs={{0,1},{1,0},{2,3},{3,2},{4,5},{5,4},{6,7},{7,6},{8,9},{9,8},{10,11... | collective-permute-start | bytes 4718600 | tf_op jit(solution)/shard_map/ppermute | solution.py:29
  27.8 5.0 %collective-permute-start.4 = (bf16[256,256]{1,0:T(8,128)(2,1)S(1)}, bf16[256,256]{1,0:T(8,128)(2,1)S(1)}, u32[]{:S(2)}, u32[]{:S(2)}) collective-permute-start(bf16[256,256]{1,0:T(8,128)(2,1)S(1)} %get-tuple-element.74), channel_id=1, source_target_pairs={{0,6},{2,0},{4,2},{6,4},{1,7},{3,1},{5,3},{7,5},{8,14},{10,8},{12,... | collective-permute-start | bytes 393224 | tf_op jit(solution)/shard_map/ppermute | solution.py:29
  29.0 6.5 %collective-permute-start.5 = (bf16[256,256]{1,0:T(8,128)(2,1)S(1)}, bf16[256,256]{1,0:T(8,128)(2,1)S(1)}, u32[]{:S(2)}, u32[]{:S(2)}) collective-permute-start(bf16[256,256]{1,0:T(8,128)(2,1)S(1)} %get-tuple-element.74), channel_id=1, source_target_pairs={{0,4},{2,6},{4,0},{6,2},{1,5},{3,7},{5,1},{7,3},{8,12},{10,14},{12... | collective-permute-start | bytes 393224 | tf_op jit(solution)/shard_map/ppermute | solution.py:29
  30.5 6.4 %collective-permute-start.6 = (bf16[256,256]{1,0:T(8,128)(2,1)S(1)}, bf16[256,256]{1,0:T(8,128)(2,1)S(1)}, u32[]{:S(2)}, u32[]{:S(2)}) collective-permute-start(bf16[256,256]{1,0:T(8,128)(2,1)S(1)} %get-tuple-element.74), channel_id=1, source_target_pairs={{0,2},{2,4},{4,6},{6,0},{1,3},{3,5},{5,7},{7,1},{8,10},{10,12},{12... | collective-permute-start | bytes 393224 | tf_op jit(solution)/shard_map/ppermute | solution.py:29
  61.4 2.5 %copy-start.5 = (f32[1,16,64]{2,1,0:T(8,128)S(1)}, f32[1,16,64]{2,1,0:T(8,128)}, u32[]{:S(2)}) copy-start(f32[1,16,64]{2,1,0:T(8,128)} %param.15) | copy-start | bytes 12292
  61.4 2.7 %copy-start.6 = (s32[1,16,64]{2,1,0:T(8,128)S(1)}, s32[1,16,64]{2,1,0:T(8,128)}, u32[]{:S(2)}) copy-start(s32[1,16,64]{2,1,0:T(8,128)} %param.13) | copy-start | bytes 12292
  63.1 1.2 copy-start.7
  63.1 1.4 copy-start.1
  63.1 14.7 %copy-start.2 = (f32[16,8192]{1,0:T(8,128)S(1)}, f32[16,8192]{1,0:T(8,128)}, u32[]{:S(2)}) copy-start(f32[16,8192]{1,0:T(8,128)} %param.17) | copy-start | bytes 1572868
  63.1 14.7 %copy-start.3 = (f32[16,8192]{1,0:T(8,128)S(1)}, f32[16,8192]{1,0:T(8,128)}, u32[]{:S(2)}) copy-start(f32[16,8192]{1,0:T(8,128)} %param.16) | copy-start | bytes 1572868
  63.1 71.8 %all-gather.7.cloned.1.call-start = ((), (), s32[]{:S(2)}) async-start(), calls=%async_computation.6 | async-start | bytes 4718592 | tf_op jit(solution)/shard_map/all_gather | solution.py:238
  65.4 10.3 %collective-permute-start.10 = (bf16[16,8192]{1,0:T(8,128)(2,1)S(1)}, bf16[16,8192]{1,0:T(8,128)(2,1)S(1)}, u32[]{:S(2)}, u32[]{:S(2)}) collective-permute-start(bf16[16,8192]{1,0:T(8,128)(2,1)S(1)} %fusion), channel_id=1, source_target_pairs={{0,192},{64,128},{128,64},{192,0},{1,193},{65,129},{129,65},{193,1... | collective-permute-start | bytes 786440 | tf_op jit(solution)/shard_map/ppermute | solution.py:40
  65.5 10.2 %collective-permute-start.8 = (bf16[16,8192]{1,0:T(8,128)(2,1)S(1)}, bf16[16,8192]{1,0:T(8,128)(2,1)S(1)}, u32[]{:S(2)}, u32[]{:S(2)}) collective-permute-start(bf16[16,8192]{1,0:T(8,128)(2,1)S(1)} %fusion), channel_id=1, source_target_pairs={{0,64},{64,0},{1,65},{65,1},{2,66},{66,2},{3,67},{67,3},{4,68},{68... | collective-permute-start | bytes 786440 | tf_op jit(solution)/shard_map/ppermute | solution.py:29
  65.9 11.9 %collective-permute-start.9 = (bf16[16,8192]{1,0:T(8,128)(2,1)S(1)}, bf16[16,8192]{1,0:T(8,128)(2,1)S(1)}, u32[]{:S(2)}, u32[]{:S(2)}) collective-permute-start(bf16[16,8192]{1,0:T(8,128)(2,1)S(1)} %fusion), channel_id=1, source_target_pairs={{0,128},{128,0},{1,129},{129,1},{2,130},{130,2},{3,131},{131,3},{4... | collective-permute-start | bytes 786440 | tf_op jit(solution)/shard_map/ppermute | solution.py:29
  69.1 54.9 %collective-permute-start.19 = (bf16[8,4,128,256]{3,2,1,0:T(8,128)(2,1)}, bf16[8,4,128,256]{3,2,1,0:T(8,128)(2,1)}, u32[]{:S(2)}, u32[]{:S(2)}) collective-permute-start(bf16[8,4,128,256]{3,2,1,0:T(8,128)(2,1)} %bitcast.14.weight_c), channel_id=1, source_target_pairs={{0,1},{1,0},{2,3},{3,2},{4,5},{5,4},{6,7},{7,6},{8,9},{9,8},{10,11... | collective-permute-start | bytes 6291464 | tf_op jit(solution)/shard_map/ppermute | solution.py:29
  86.4 8.2 %collective-permute-start.11 = (bf16[160,256]{1,0:T(8,128)(2,1)S(1)}, bf16[160,256]{1,0:T(8,128)(2,1)S(1)}, u32[]{:S(2)}, u32[]{:S(2)}) collective-permute-start(bf16[160,256]{1,0:T(8,128)(2,1)S(1)} %get-tuple-element.70), channel_id=1, source_target_pairs={{0,8},{8,16},{16,24},{24,32},{32,40},{40,48},{48,56},{56,0},{1,9},... | collective-permute-start | bytes 245768 | tf_op jit(solution)/shard_map/ppermute | solution.py:29
  88.0 6.5 %collective-permute-start.12 = (bf16[160,256]{1,0:T(8,128)(2,1)S(1)}, bf16[160,256]{1,0:T(8,128)(2,1)S(1)}, u32[]{:S(2)}, u32[]{:S(2)}) collective-permute-start(bf16[160,256]{1,0:T(8,128)(2,1)S(1)} %get-tuple-element.68), channel_id=1, source_target_pairs={{0,56},{8,0},{16,8},{24,16},{32,24},{40,32},{48,40},{56,48},{1,57}... | collective-permute-start | bytes 245768 | tf_op jit(solution)/shard_map/ppermute | solution.py:29
  94.6 11.3 %collective-permute-start.13 = (bf16[320,256]{1,0:T(8,128)(2,1)S(1)}, bf16[320,256]{1,0:T(8,128)(2,1)S(1)}, u32[]{:S(2)}, u32[]{:S(2)}) collective-permute-start(bf16[320,256]{1,0:T(8,128)(2,1)S(1)} %get-tuple-element.39), channel_id=1, source_target_pairs={{0,8},{8,16},{16,24},{24,32},{32,40},{40,48},{48,56},{56,0},{1,9},... | collective-permute-start | bytes 491528 | tf_op jit(solution)/shard_map/ppermute | solution.py:29
  96.3 10.1 %collective-permute-start.14 = (bf16[320,256]{1,0:T(8,128)(2,1)S(1)}, bf16[320,256]{1,0:T(8,128)(2,1)S(1)}, u32[]{:S(2)}, u32[]{:S(2)}) collective-permute-start(bf16[320,256]{1,0:T(8,128)(2,1)S(1)} %get-tuple-element.40), channel_id=1, source_target_pairs={{0,56},{8,0},{16,8},{24,16},{32,24},{40,32},{48,40},{56,48},{1,57}... | collective-permute-start | bytes 491528 | tf_op jit(solution)/shard_map/ppermute | solution.py:29
  106.5 11.0 %collective-permute-start.15 = (bf16[320,256]{1,0:T(8,128)(2,1)S(1)}, bf16[320,256]{1,0:T(8,128)(2,1)S(1)}, u32[]{:S(2)}, u32[]{:S(2)}) collective-permute-start(bf16[320,256]{1,0:T(8,128)(2,1)S(1)} %get-tuple-element.41), channel_id=1, source_target_pairs={{0,8},{8,16},{16,24},{24,32},{32,40},{40,48},{48,56},{56,0},{1,9},... | collective-permute-start | bytes 491528 | tf_op jit(solution)/shard_map/ppermute | solution.py:29
  109.8 9.5 %collective-permute-start.16 = (bf16[320,256]{1,0:T(8,128)(2,1)S(1)}, bf16[320,256]{1,0:T(8,128)(2,1)S(1)}, u32[]{:S(2)}, u32[]{:S(2)}) collective-permute-start(bf16[320,256]{1,0:T(8,128)(2,1)S(1)} %get-tuple-element.42), channel_id=1, source_target_pairs={{0,56},{8,0},{16,8},{24,16},{32,24},{40,32},{48,40},{56,48},{1,57}... | collective-permute-start | bytes 491528 | tf_op jit(solution)/shard_map/ppermute | solution.py:29
  119.3 13.2 %collective-permute-start.17 = (bf16[320,256]{1,0:T(8,128)(2,1)S(1)}, bf16[320,256]{1,0:T(8,128)(2,1)S(1)}, u32[]{:S(2)}, u32[]{:S(2)}) collective-permute-start(bf16[320,256]{1,0:T(8,128)(2,1)S(1)} %get-tuple-element.43), channel_id=1, source_target_pairs={{0,8},{8,16},{16,24},{24,32},{32,40},{40,48},{48,56},{56,0},{1,9},... | collective-permute-start | bytes 491528 | tf_op jit(solution)/shard_map/ppermute | solution.py:29
  121.2 11.3 %collective-permute-start.18 = (bf16[320,256]{1,0:T(8,128)(2,1)S(1)}, bf16[320,256]{1,0:T(8,128)(2,1)}, u32[]{:S(2)}, u32[]{:S(2)}) collective-permute-start(bf16[320,256]{1,0:T(8,128)(2,1)S(1)} %get-tuple-element.44), channel_id=1, source_target_pairs={{0,56},{8,0},{16,8},{24,16},{32,24},{40,32},{48,40},{56,48},{1,57}... | collective-permute-start | bytes 491528 | tf_op jit(solution)/shard_map/ppermute | solution.py:29
  124.0 24.0 %all-to-all-start = ((bf16[8,192,128]{2,1,0:T(8,128)(2,1)}), bf16[8,192,128]{2,1,0:T(8,128)(2,1)S(1)}, u32[]{:S(2)}, u32[]{:S(2)}) async-start(bf16[8,192,128]{2,1,0:T(8,128)(2,1)} %bitcast.101), calls=%async_computation.2 | async-start | bytes 786432 | tf_op jit(solution)/shard_map/all_to_all | solution.py:258
  133.5 11.5 %collective-permute-start.20 = (bf16[320,128]{1,0:T(8,128)(2,1)S(1)}, bf16[320,128]{1,0:T(8,128)(2,1)S(1)}, u32[]{:S(2)}, u32[]{:S(2)}) collective-permute-start(bf16[320,128]{1,0:T(8,128)(2,1)S(1)} %select_convert_fusion), channel_id=1, source_target_pairs={{0,1},{1,0},{2,3},{3,2},{4,5},{5,4},{6,7},{7,6},{8,9},{9,8},{10,11... | collective-permute-start | bytes 245768 | tf_op jit(solution)/shard_map/ppermute | solution.py:29
Sparse Core Ops, SparseCore 0:
  19.1 42.3 all-gather.4
  65.8 68.6 all-gather.6
Sparse Core Ops, SparseCore 1:
  26.4 58.9 reduce-scatter.2
  88.3 27.8 reduce-scatter.4

commit v4 on v3

--- a/solution.py
+++ b/solution.py
@@ -11,7 +11,7 @@
 GROUP = 128
 Z, X, Y = 8, 4, 2
 WEIGHT_SPLIT = 256
-GRAD_SPLIT = 320
+GRAD_SPLIT = 352
 F32, BF16 = jnp.float32, jnp.bfloat16
 VMEM_LIMIT = 56 * 1024 * 1024
 

time: 157 us -> 156 us (level)
  starting transfers between devices: 38.5 us -> 35.8 us
    reduce_scatter x1, waiting for transfers between devices: 6.31 us -> 12.9 us  [local(): grad_a = lax.psum_scatter(grad_a, 'x', scatter_dimension=0, tiled=True)[0]]
    ppermute x20, waiting for transfers between devices: 57.9 us -> 51.7 us  [shift(): lax.ppermute(block, axis, [(i, (i + by) % size) for i in range(size)])]
    all_gather x1, waiting for transfers between devices: 0.02 us -> 4.29 us  [local(): weight_c = lax.all_gather(weight_c, 'z')]
    all_to_all x1, waiting for transfers between devices: 3.06 us -> 0.01 us  [local(): grad_c = lax.all_to_all(after(grad_c_x, up, other_c), 'z', 0, 0, tiled=True)]
    all_to_all x1, starting transfers between devices: 8.46 us -> 5.77 us  [local(): grad_c = lax.all_to_all(after(grad_c_x, up, other_c), 'z', 0, 0, tiled=True)]
where the time goes in v4:
time: 156 us; the launch traced here: 155 us
  waiting for transfers between devices  73.8 us (47%)
  starting transfers between devices  35.8 us (23%)
  Pallas kernels  16.6 us (11%)
  between operations  15.7 us (10%)
  other arithmetic  9.67 us (6%)
  local copies, waits for them, and re-layouts  3.37 us (2%)
    ppermute x20, waiting for transfers between devices, shift(): lax.ppermute(block, axis, [(i, (i + by) % size) for i in range(size)])  51.7 us
    ppermute x20, starting transfers between devices, shift(): lax.ppermute(block, axis, [(i, (i + by) % size) for i in range(size)])  29.8 us
    reduce_scatter x1, waiting for transfers between devices, local(): grad_a = lax.psum_scatter(grad_a, 'x', scatter_dimension=0, tiled=True)[0]  12.9 us
    pallas_call x1, Pallas kernels, products(): pl.pallas_call(product_kernel, in_specs=[pl.BlockSpec(memory_space=pltpu....  10 us
    pallas_call x1, Pallas kernels, gradients(): pl.pallas_call(grad_kernel, in_specs=[pl.BlockSpec(memory_space=pltpu.SME...  6.55 us
    all_to_all x1, starting transfers between devices, local(): grad_c = lax.all_to_all(after(grad_c_x, up, other_c), 'z', 0, 0, tiled=True)  5.77 us
    ppermute x1, waiting for transfers between devices, outer_values(): far_core = lax.ppermute(values, ('yh', 'c'), [(i, 3 - i) for i in range(4)])  4.79 us
    all_gather x1, waiting for transfers between devices, local(): weight_c = lax.all_gather(weight_c, 'z')  4.29 us
  transfers between devices with their start and end apart: 26, of which 16 were waited for; matrix products, arithmetic and copies ran while one was open for 7% of the time, Pallas kernels for 11%

profile of v4, /device:TPU:16, one launch (start us, length us, event | category | flops | bytes accessed | tf_op | source)
XLA Modules:
  0.0 154.9 jit_solution(11312509142403091750)
XLA Ops:
  8.0 0.0 all-gather.5.cloned.1.call-start
  8.0 0.9 fusion.18
  8.9 2.8 %collective-permute-start = (bf16[128,256]{1,0:T(8,128)(2,1)S(1)}, bf16[128,256]{1,0:T(8,128)(2,1)S(1)}, u32[]{:S(2)}, u32[]{:S(2)}) collective-permute-start(bf16[128,256]{1,0:T(8,128)(2,1)S(1)} %get-tuple-element.77), channel_id=1, source_target_pairs={{0,6},{2,0},{4,2},{6,4},{1,7},{3,1},{5,3},{7,5},{8,14},{10,8},{12,... | collective-permute-start | bytes 196616 | tf_op jit(solution)/shard_map/ppermute | solution.py:29
  11.8 0.8 collective-permute-start.1
  12.6 0.9 collective-permute-start.2
  13.5 1.3 collective-permute-start.3
  14.7 2.8 %collective-permute-done.1 = bf16[128,256]{1,0:T(8,128)(2,1)S(1)} collective-permute-done((bf16[128,256]{1,0:T(8,128)(2,1)S(1)}, bf16[128,256]{1,0:T(8,128)(2,1)S(1)}, u32[]{:S(2)}, u32[]{:S(2)}) %collective-permute-start.1) | collective-permute-done | bytes 65568 | tf_op jit(solution)/shard_map/ppermute | solution.py:29
  17.6 0.7 collective-permute-done.2
  18.2 0.7 pad_maximum_fusion.1
  19.0 0.0 all-gather.5.cloned.1.call-update
  19.0 0.0 reduce-scatter.3.cloned.1.call-start
  19.1 0.6 pad_add_fusion.place
  19.7 6.6 %shard_map.128 = (bf16[4,8,352,256]{3,2,1,0:T(8,128)(2,1)}, bf16[4,8,160,128]{3,2,1,0:T(8,128)(2,1)}, bf16[4,8,160,128]{3,2,1,0:T(8,128)(2,1)}) custom-call(s32[3]{0:T(128)} %pad_add_fusion.place, bf16[256,8192]{1,0:T(8,128)(2,1)} %bitcast.113, bf16[256,512]{1,0:T(8,128)(2,1)} %bitcast.116), custom_call_target="tpu_custom_call" | custom-call | flops 2147483648 | bytes 12582912 | tf_op jit(solution)/shard_map/pallas_call | solution.py:96
  26.2 0.0 reduce-scatter.3.cloned.1.call-update
  26.3 0.0 reduce-scatter.5.cloned.1.call-start
  26.3 1.4 collective-permute-start.7
  27.7 1.2 collective-permute-start.4
  28.9 1.5 collective-permute-start.5
  30.4 0.1 collective-permute-start.6
  30.6 2.2 %collective-permute-done.4 = bf16[256,256]{1,0:T(8,128)(2,1)S(1)} collective-permute-done((bf16[256,256]{1,0:T(8,128)(2,1)S(1)}, bf16[256,256]{1,0:T(8,128)(2,1)S(1)}, u32[]{:S(2)}, u32[]{:S(2)}) %collective-permute-start.4) | collective-permute-done | bytes 131104 | tf_op jit(solution)/shard_map/ppermute | solution.py:29
  32.8 2.6 %collective-permute-done.5 = bf16[256,256]{1,0:T(8,128)(2,1)S(1)} collective-permute-done((bf16[256,256]{1,0:T(8,128)(2,1)S(1)}, bf16[256,256]{1,0:T(8,128)(2,1)S(1)}, u32[]{:S(2)}, u32[]{:S(2)}) %collective-permute-start.5) | collective-permute-done | bytes 131104 | tf_op jit(solution)/shard_map/ppermute | solution.py:29
  35.4 1.4 collective-permute-done.6
  36.8 0.9 pad_maximum_fusion
  37.7 18.1 %collective-permute-done.7 = bf16[4,8,160,128]{3,2,1,0:T(8,128)(2,1)S(1)} collective-permute-done((bf16[4,8,160,128]{3,2,1,0:T(8,128)(2,1)}, bf16[4,8,160,128]{3,2,1,0:T(8,128)(2,1)S(1)}, u32[]{:S(2)}, u32[]{:S(2)}) %collective-permute-start.7) | collective-permute-done | bytes 1310752 | tf_op jit(solution)/shard_map/ppermute | solution.py:29
  55.7 1.4 add_convert_fusion
  57.1 0.0 reduce-scatter.5.cloned.1.call-update
  57.2 0.0 all-gather.7.cloned.1.call-start
  57.2 4.3 %all-gather.5.cloned.1.call-done = bf16[32,128,256]{2,1,0:T(8,128)(2,1)} async-done(((bf16[4,128,256]{2,1,0:T(8,128)(2,1)}), bf16[32,128,256]{2,1,0:T(8,128)(2,1)}) %all-gather.5.cloned.1.call-update) | async-done | bytes 2097168 | tf_op jit(solution)/shard_map/all_gather | solution.py:222
  61.5 0.0 all-gather.7.cloned.1.call-update
  61.5 0.2 mul.35
  61.7 0.2 sub.17
  61.9 0.2 add.64
  62.2 0.9 fusion
  63.0 0.1 collective-permute-start.10
  63.1 0.6 collective-permute-start.8
  63.8 3.0 %collective-permute-start.9 = (bf16[16,8192]{1,0:T(8,128)(2,1)S(1)}, bf16[16,8192]{1,0:T(8,128)(2,1)S(1)}, u32[]{:S(2)}, u32[]{:S(2)}) collective-permute-start(bf16[16,8192]{1,0:T(8,128)(2,1)S(1)} %fusion), channel_id=1, source_target_pairs={{0,128},{128,0},{1,129},{129,1},{2,130},{130,2},{3,131},{131,3},{4... | collective-permute-start | bytes 786440 | tf_op jit(solution)/shard_map/ppermute | solution.py:29
  66.8 1.2 collective-permute-start.19
  68.0 4.8 %collective-permute-done.10 = bf16[16,8192]{1,0:T(8,128)(2,1)S(1)} collective-permute-done((bf16[16,8192]{1,0:T(8,128)(2,1)S(1)}, bf16[16,8192]{1,0:T(8,128)(2,1)S(1)}, u32[]{:S(2)}, u32[]{:S(2)}) %collective-permute-start.10) | collective-permute-done | bytes 262176 | tf_op jit(solution)/shard_map/ppermute | solution.py:40
  72.8 2.7 %collective-permute-done.9 = bf16[16,8192]{1,0:T(8,128)(2,1)S(1)} collective-permute-done((bf16[16,8192]{1,0:T(8,128)(2,1)S(1)}, bf16[16,8192]{1,0:T(8,128)(2,1)S(1)}, u32[]{:S(2)}, u32[]{:S(2)}) %collective-permute-start.9) | collective-permute-done | bytes 262176 | tf_op jit(solution)/shard_map/ppermute | solution.py:29
  75.5 1.2 multiply_subtract_fusion
  76.7 12.9 %reduce-scatter.3.cloned.1.call-done = bf16[1,8,352,256]{3,2,1,0:T(8,128)(2,1)} async-done(((bf16[4,8,352,256]{3,2,1,0:T(8,128)(2,1)}), bf16[1,8,352,256]{3,2,1,0:T(8,128)(2,1)}) %reduce-scatter.3.cloned.1.call-update) | async-done | bytes 1441808 | tf_op jit(solution)/shard_map/reduce_scatter | solution.py:225
  89.6 1.0 slice_bitcast_fusion.8
  90.6 1.6 %collective-permute-start.11 = (bf16[176,256]{1,0:T(8,128)(2,1)S(1)}, bf16[176,256]{1,0:T(8,128)(2,1)S(1)}, u32[]{:S(2)}, u32[]{:S(2)}) collective-permute-start(bf16[176,256]{1,0:T(8,128)(2,1)S(1)} %get-tuple-element.70), channel_id=1, source_target_pairs={{0,8},{8,16},{16,24},{24,32},{32,40},{40,48},{48,56},{56,0},{1,9},... | collective-permute-start | bytes 270344 | tf_op jit(solution)/shard_map/ppermute | solution.py:29
  92.2 1.9 %collective-permute-start.12 = (bf16[176,256]{1,0:T(8,128)(2,1)S(1)}, bf16[176,256]{1,0:T(8,128)(2,1)S(1)}, u32[]{:S(2)}, u32[]{:S(2)}) collective-permute-start(bf16[176,256]{1,0:T(8,128)(2,1)S(1)} %get-tuple-element.68), channel_id=1, source_target_pairs={{0,56},{8,0},{16,8},{24,16},{32,24},{40,32},{48,40},{56,48},{1,57}... | collective-permute-start | bytes 270344 | tf_op jit(solution)/shard_map/ppermute | solution.py:29
  94.1 1.6 %convert_element_type.87 = f32[8,352,256]{2,1,0:T(8,128)S(1)} convert(bf16[8,352,256]{2,1,0:T(8,128)(2,1)} %bitcast.96) | non-fusion elementwise | flops 720896 | bytes 4325376 | tf_op jit(solution)/shard_map/convert_element_type | solution.py:247
  95.8 3.3 %collective-permute-done.11 = bf16[176,256]{1,0:T(8,128)(2,1)S(1)} collective-permute-done((bf16[176,256]{1,0:T(8,128)(2,1)S(1)}, bf16[176,256]{1,0:T(8,128)(2,1)S(1)}, u32[]{:S(2)}, u32[]{:S(2)}) %collective-permute-start.11) | collective-permute-done | bytes 90144 | tf_op jit(solution)/shard_map/ppermute | solution.py:29
  99.1 0.1 collective-permute-done.12
  99.2 1.6 %collective-permute-start.13 = (bf16[352,256]{1,0:T(8,128)(2,1)S(1)}, bf16[352,256]{1,0:T(8,128)(2,1)S(1)}, u32[]{:S(2)}, u32[]{:S(2)}) collective-permute-start(bf16[352,256]{1,0:T(8,128)(2,1)S(1)} %get-tuple-element.39), channel_id=1, source_target_pairs={{0,8},{8,16},{16,24},{24,32},{32,40},{40,48},{48,56},{56,0},{1,9},... | collective-permute-start | bytes 540680 | tf_op jit(solution)/shard_map/ppermute | solution.py:29
  100.9 1.7 %collective-permute-start.14 = (bf16[352,256]{1,0:T(8,128)(2,1)S(1)}, bf16[352,256]{1,0:T(8,128)(2,1)S(1)}, u32[]{:S(2)}, u32[]{:S(2)}) collective-permute-start(bf16[352,256]{1,0:T(8,128)(2,1)S(1)} %get-tuple-element.40), channel_id=1, source_target_pairs={{0,56},{8,0},{16,8},{24,16},{32,24},{40,32},{48,40},{56,48},{1,57}... | collective-permute-start | bytes 540680 | tf_op jit(solution)/shard_map/ppermute | solution.py:29
  102.6 8.7 %collective-permute-done.13 = bf16[352,256]{1,0:T(8,128)(2,1)S(1)} collective-permute-done((bf16[352,256]{1,0:T(8,128)(2,1)S(1)}, bf16[352,256]{1,0:T(8,128)(2,1)S(1)}, u32[]{:S(2)}, u32[]{:S(2)}) %collective-permute-start.13) | collective-permute-done | bytes 180256 | tf_op jit(solution)/shard_map/ppermute | solution.py:29
  111.2 0.4 collective-permute-done.14
  111.6 0.1 fusion.6
  111.7 3.3 %collective-permute-start.15 = (bf16[352,256]{1,0:T(8,128)(2,1)S(1)}, bf16[352,256]{1,0:T(8,128)(2,1)S(1)}, u32[]{:S(2)}, u32[]{:S(2)}) collective-permute-start(bf16[352,256]{1,0:T(8,128)(2,1)S(1)} %get-tuple-element.41), channel_id=1, source_target_pairs={{0,8},{8,16},{16,24},{24,32},{32,40},{40,48},{48,56},{56,0},{1,9},... | collective-permute-start | bytes 540680 | tf_op jit(solution)/shard_map/ppermute | solution.py:29
  115.1 8.4 %collective-permute-done.15 = bf16[352,256]{1,0:T(8,128)(2,1)S(1)} collective-permute-done((bf16[352,256]{1,0:T(8,128)(2,1)S(1)}, bf16[352,256]{1,0:T(8,128)(2,1)S(1)}, u32[]{:S(2)}, u32[]{:S(2)}) %collective-permute-start.15) | collective-permute-done | bytes 180256 | tf_op jit(solution)/shard_map/ppermute | solution.py:29
  123.4 0.4 collective-permute-done.16
  123.8 0.1 fusion.4
  123.9 1.6 %collective-permute-start.17 = (bf16[352,256]{1,0:T(8,128)(2,1)S(1)}, bf16[352,256]{1,0:T(8,128)(2,1)S(1)}, u32[]{:S(2)}, u32[]{:S(2)}) collective-permute-start(bf16[352,256]{1,0:T(8,128)(2,1)S(1)} %get-tuple-element.43), channel_id=1, source_target_pairs={{0,8},{8,16},{16,24},{24,32},{32,40},{40,48},{48,56},{56,0},{1,9},... | collective-permute-start | bytes 540680 | tf_op jit(solution)/shard_map/ppermute | solution.py:29
  125.5 1.7 %collective-permute-start.18 = (bf16[352,256]{1,0:T(8,128)(2,1)S(1)}, bf16[352,256]{1,0:T(8,128)(2,1)}, u32[]{:S(2)}, u32[]{:S(2)}) collective-permute-start(bf16[352,256]{1,0:T(8,128)(2,1)S(1)} %get-tuple-element.44), channel_id=1, source_target_pairs={{0,56},{8,0},{16,8},{24,16},{32,24},{40,32},{48,40},{56,48},{1,57}... | collective-permute-start | bytes 540680 | tf_op jit(solution)/shard_map/ppermute | solution.py:29
  127.2 5.8 %all-to-all-start = ((bf16[8,160,128]{2,1,0:T(8,128)(2,1)}), bf16[8,160,128]{2,1,0:T(8,128)(2,1)}, u32[]{:S(2)}, u32[]{:S(2)}) async-start(bf16[8,160,128]{2,1,0:T(8,128)(2,1)} %bitcast.101), calls=%async_computation.2 | async-start | bytes 655360 | tf_op jit(solution)/shard_map/all_to_all | solution.py:258
  133.0 1.0 fusion.11
  134.0 1.5 collective-permute-start.20
  135.5 10.0 %shard_map.129 = (bf16[256,512]{1,0:T(8,128)(2,1)}, bf16[256,8192]{1,0:T(8,128)(2,1)}) custom-call(s32[3]{0:T(128)} %pad_add_fusion.place, bf16[256,8192]{1,0:T(8,128)(2,1)} %bitcast.114, bf16[256,512]{1,0:T(8,128)(2,1)} %bitcast.117, bf16[8,4,256,256]{3,2,1,0:T(8,128)(2,1)} %bitcast.115, bf16[8,4,128,256]{3,2,1,0:T(8,128)(2,1)} %bitcast.14.weight_c, ...), custom_call_target="tpu_custom_call" | custom-call | flops 4294967296 | bytes 16777216 | tf_op jit(solution)/shard_map/pallas_call | solution.py:176
  145.6 1.0 convert_reduce_fusion
  146.7 0.8 copy.15
  (34 shorter events, 0.2 us)
Async XLA Ops:
  8.0 53.5 %all-gather.5.cloned.1.call-start = ((), (), s32[]{:S(2)}) async-start(), calls=%async_computation.5 | async-start | bytes 2359296 | tf_op jit(solution)/shard_map/all_gather | solution.py:222
  8.9 5.8 %collective-permute-start = (bf16[128,256]{1,0:T(8,128)(2,1)S(1)}, bf16[128,256]{1,0:T(8,128)(2,1)S(1)}, u32[]{:S(2)}, u32[]{:S(2)}) collective-permute-start(bf16[128,256]{1,0:T(8,128)(2,1)S(1)} %get-tuple-element.77), channel_id=1, source_target_pairs={{0,6},{2,0},{4,2},{6,4},{1,7},{3,1},{5,3},{7,5},{8,14},{10,8},{12,... | collective-permute-start | bytes 196616 | tf_op jit(solution)/shard_map/ppermute | solution.py:29
  11.8 5.8 %collective-permute-start.1 = (bf16[128,256]{1,0:T(8,128)(2,1)S(1)}, bf16[128,256]{1,0:T(8,128)(2,1)S(1)}, u32[]{:S(2)}, u32[]{:S(2)}) collective-permute-start(bf16[128,256]{1,0:T(8,128)(2,1)S(1)} %get-tuple-element.77), channel_id=1, source_target_pairs={{0,4},{2,6},{4,0},{6,2},{1,5},{3,7},{5,1},{7,3},{8,12},{10,14},{12... | collective-permute-start | bytes 196616 | tf_op jit(solution)/shard_map/ppermute | solution.py:29
  12.6 5.7 %collective-permute-start.2 = (bf16[128,256]{1,0:T(8,128)(2,1)S(1)}, bf16[128,256]{1,0:T(8,128)(2,1)S(1)}, u32[]{:S(2)}, u32[]{:S(2)}) collective-permute-start(bf16[128,256]{1,0:T(8,128)(2,1)S(1)} %get-tuple-element.77), channel_id=1, source_target_pairs={{0,2},{2,4},{4,6},{6,0},{1,3},{3,5},{5,7},{7,1},{8,10},{10,12},{12... | collective-permute-start | bytes 196616 | tf_op jit(solution)/shard_map/ppermute | solution.py:29
  13.5 5.5 %collective-permute-start.3 = (bf16[128,256]{1,0:T(8,128)(2,1)S(1)}, bf16[128,256]{1,0:T(8,128)(2,1)S(1)}, u32[]{:S(2)}, u32[]{:S(2)}) collective-permute-start(bf16[128,256]{1,0:T(8,128)(2,1)S(1)} %get-tuple-element.75), channel_id=1, source_target_pairs={{0,1},{1,0},{2,3},{3,2},{4,5},{5,4},{6,7},{7,6},{8,9},{9,8},{10,11... | collective-permute-start | bytes 196616 | tf_op jit(solution)/shard_map/ppermute | solution.py:29
  19.0 70.6 %reduce-scatter.3.cloned.1.call-start = ((), (), s32[]{:S(2)}) async-start(), calls=%async_computation.3 | async-start | bytes 7208960 | tf_op jit(solution)/shard_map/reduce_scatter | solution.py:225
  26.2 1.5 copy-start.4
  26.2 29.5 %copy-start = (bf16[4,8,160,128]{3,2,1,0:T(8,128)(2,1)S(1)}, bf16[4,8,160,128]{3,2,1,0:T(8,128)(2,1)}, u32[]{:S(2)}) copy-start(bf16[4,8,160,128]{3,2,1,0:T(8,128)(2,1)} %get-tuple-element.32) | copy-start | bytes 3932164
  26.3 100.9 %reduce-scatter.5.cloned.1.call-start = ((), (), s32[]{:S(2)}) async-start(), calls=%async_computation.4 | async-start | bytes 1638400 | tf_op jit(solution)/shard_map/reduce_scatter | solution.py:235
  26.3 29.4 %collective-permute-start.7 = (bf16[4,8,160,128]{3,2,1,0:T(8,128)(2,1)}, bf16[4,8,160,128]{3,2,1,0:T(8,128)(2,1)S(1)}, u32[]{:S(2)}, u32[]{:S(2)}) collective-permute-start(bf16[4,8,160,128]{3,2,1,0:T(8,128)(2,1)} %get-tuple-element.30), channel_id=1, source_target_pairs={{0,1},{1,0},{2,3},{3,2},{4,5},{5,4},{6,7},{7,6},{8,9},{9,8},{10,11... | collective-permute-start | bytes 3932168 | tf_op jit(solution)/shard_map/ppermute | solution.py:29
  27.7 5.0 %collective-permute-start.4 = (bf16[256,256]{1,0:T(8,128)(2,1)S(1)}, bf16[256,256]{1,0:T(8,128)(2,1)S(1)}, u32[]{:S(2)}, u32[]{:S(2)}) collective-permute-start(bf16[256,256]{1,0:T(8,128)(2,1)S(1)} %get-tuple-element.74), channel_id=1, source_target_pairs={{0,6},{2,0},{4,2},{6,4},{1,7},{3,1},{5,3},{7,5},{8,14},{10,8},{12,... | collective-permute-start | bytes 393224 | tf_op jit(solution)/shard_map/ppermute | solution.py:29
  28.9 6.5 %collective-permute-start.5 = (bf16[256,256]{1,0:T(8,128)(2,1)S(1)}, bf16[256,256]{1,0:T(8,128)(2,1)S(1)}, u32[]{:S(2)}, u32[]{:S(2)}) collective-permute-start(bf16[256,256]{1,0:T(8,128)(2,1)S(1)} %get-tuple-element.74), channel_id=1, source_target_pairs={{0,4},{2,6},{4,0},{6,2},{1,5},{3,7},{5,1},{7,3},{8,12},{10,14},{12... | collective-permute-start | bytes 393224 | tf_op jit(solution)/shard_map/ppermute | solution.py:29
  30.4 6.4 %collective-permute-start.6 = (bf16[256,256]{1,0:T(8,128)(2,1)S(1)}, bf16[256,256]{1,0:T(8,128)(2,1)S(1)}, u32[]{:S(2)}, u32[]{:S(2)}) collective-permute-start(bf16[256,256]{1,0:T(8,128)(2,1)S(1)} %get-tuple-element.74), channel_id=1, source_target_pairs={{0,2},{2,4},{4,6},{6,0},{1,3},{3,5},{5,7},{7,1},{8,10},{10,12},{12... | collective-permute-start | bytes 393224 | tf_op jit(solution)/shard_map/ppermute | solution.py:29
  55.7 5.8 %copy-start.5 = (f32[1,16,64]{2,1,0:T(8,128)S(1)}, f32[1,16,64]{2,1,0:T(8,128)}, u32[]{:S(2)}) copy-start(f32[1,16,64]{2,1,0:T(8,128)} %param.15) | copy-start | bytes 12292
  55.7 6.0 %copy-start.6 = (s32[1,16,64]{2,1,0:T(8,128)S(1)}, s32[1,16,64]{2,1,0:T(8,128)}, u32[]{:S(2)}) copy-start(s32[1,16,64]{2,1,0:T(8,128)} %param.13) | copy-start | bytes 12292
  55.7 6.2 %copy-start.7 = (f32[1,16,64]{2,1,0:T(8,128)S(1)}, f32[1,16,64]{2,1,0:T(8,128)}, u32[]{:S(2)}) copy-start(f32[1,16,64]{2,1,0:T(8,128)} %param.14) | copy-start | bytes 12292
  57.1 5.0 %copy-start.1 = (s32[1,16,8192]{2,1,0:T(8,128)S(1)}, s32[1,16,8192]{2,1,0:T(8,128)}, u32[]{:S(2)}) copy-start(s32[1,16,8192]{2,1,0:T(8,128)} %param.12) | copy-start | bytes 1572868
  57.1 18.3 %copy-start.2 = (f32[16,8192]{1,0:T(8,128)S(1)}, f32[16,8192]{1,0:T(8,128)}, u32[]{:S(2)}) copy-start(f32[16,8192]{1,0:T(8,128)} %param.17) | copy-start | bytes 1572868
  57.1 18.3 %copy-start.3 = (f32[16,8192]{1,0:T(8,128)S(1)}, f32[16,8192]{1,0:T(8,128)}, u32[]{:S(2)}) copy-start(f32[16,8192]{1,0:T(8,128)} %param.16) | copy-start | bytes 1572868
  57.2 78.4 %all-gather.7.cloned.1.call-start = ((), (), s32[]{:S(2)}) async-start(), calls=%async_computation.6 | async-start | bytes 4718592 | tf_op jit(solution)/shard_map/all_gather | solution.py:238
  63.0 9.7 %collective-permute-start.10 = (bf16[16,8192]{1,0:T(8,128)(2,1)S(1)}, bf16[16,8192]{1,0:T(8,128)(2,1)S(1)}, u32[]{:S(2)}, u32[]{:S(2)}) collective-permute-start(bf16[16,8192]{1,0:T(8,128)(2,1)S(1)} %fusion), channel_id=1, source_target_pairs={{0,192},{64,128},{128,64},{192,0},{1,193},{65,129},{129,65},{193,1... | collective-permute-start | bytes 786440 | tf_op jit(solution)/shard_map/ppermute | solution.py:40
  63.1 9.6 %collective-permute-start.8 = (bf16[16,8192]{1,0:T(8,128)(2,1)S(1)}, bf16[16,8192]{1,0:T(8,128)(2,1)S(1)}, u32[]{:S(2)}, u32[]{:S(2)}) collective-permute-start(bf16[16,8192]{1,0:T(8,128)(2,1)S(1)} %fusion), channel_id=1, source_target_pairs={{0,64},{64,0},{1,65},{65,1},{2,66},{66,2},{3,67},{67,3},{4,68},{68... | collective-permute-start | bytes 786440 | tf_op jit(solution)/shard_map/ppermute | solution.py:29
  63.8 11.7 %collective-permute-start.9 = (bf16[16,8192]{1,0:T(8,128)(2,1)S(1)}, bf16[16,8192]{1,0:T(8,128)(2,1)S(1)}, u32[]{:S(2)}, u32[]{:S(2)}) collective-permute-start(bf16[16,8192]{1,0:T(8,128)(2,1)S(1)} %fusion), channel_id=1, source_target_pairs={{0,128},{128,0},{1,129},{129,1},{2,130},{130,2},{3,131},{131,3},{4... | collective-permute-start | bytes 786440 | tf_op jit(solution)/shard_map/ppermute | solution.py:29
  66.8 60.4 %collective-permute-start.19 = (bf16[8,4,128,256]{3,2,1,0:T(8,128)(2,1)}, bf16[8,4,128,256]{3,2,1,0:T(8,128)(2,1)}, u32[]{:S(2)}, u32[]{:S(2)}) collective-permute-start(bf16[8,4,128,256]{3,2,1,0:T(8,128)(2,1)} %bitcast.14.weight_c), channel_id=1, source_target_pairs={{0,1},{1,0},{2,3},{3,2},{4,5},{5,4},{6,7},{7,6},{8,9},{9,8},{10,11... | collective-permute-start | bytes 6291464 | tf_op jit(solution)/shard_map/ppermute | solution.py:29
  90.6 8.5 %collective-permute-start.11 = (bf16[176,256]{1,0:T(8,128)(2,1)S(1)}, bf16[176,256]{1,0:T(8,128)(2,1)S(1)}, u32[]{:S(2)}, u32[]{:S(2)}) collective-permute-start(bf16[176,256]{1,0:T(8,128)(2,1)S(1)} %get-tuple-element.70), channel_id=1, source_target_pairs={{0,8},{8,16},{16,24},{24,32},{32,40},{40,48},{48,56},{56,0},{1,9},... | collective-permute-start | bytes 270344 | tf_op jit(solution)/shard_map/ppermute | solution.py:29
  92.2 6.9 %collective-permute-start.12 = (bf16[176,256]{1,0:T(8,128)(2,1)S(1)}, bf16[176,256]{1,0:T(8,128)(2,1)S(1)}, u32[]{:S(2)}, u32[]{:S(2)}) collective-permute-start(bf16[176,256]{1,0:T(8,128)(2,1)S(1)} %get-tuple-element.68), channel_id=1, source_target_pairs={{0,56},{8,0},{16,8},{24,16},{32,24},{40,32},{48,40},{56,48},{1,57}... | collective-permute-start | bytes 270344 | tf_op jit(solution)/shard_map/ppermute | solution.py:29
  99.2 12.0 %collective-permute-start.13 = (bf16[352,256]{1,0:T(8,128)(2,1)S(1)}, bf16[352,256]{1,0:T(8,128)(2,1)S(1)}, u32[]{:S(2)}, u32[]{:S(2)}) collective-permute-start(bf16[352,256]{1,0:T(8,128)(2,1)S(1)} %get-tuple-element.39), channel_id=1, source_target_pairs={{0,8},{8,16},{16,24},{24,32},{32,40},{40,48},{48,56},{56,0},{1,9},... | collective-permute-start | bytes 540680 | tf_op jit(solution)/shard_map/ppermute | solution.py:29
  100.9 10.8 %collective-permute-start.14 = (bf16[352,256]{1,0:T(8,128)(2,1)S(1)}, bf16[352,256]{1,0:T(8,128)(2,1)S(1)}, u32[]{:S(2)}, u32[]{:S(2)}) collective-permute-start(bf16[352,256]{1,0:T(8,128)(2,1)S(1)} %get-tuple-element.40), channel_id=1, source_target_pairs={{0,56},{8,0},{16,8},{24,16},{32,24},{40,32},{48,40},{56,48},{1,57}... | collective-permute-start | bytes 540680 | tf_op jit(solution)/shard_map/ppermute | solution.py:29
  111.7 11.7 %collective-permute-start.15 = (bf16[352,256]{1,0:T(8,128)(2,1)S(1)}, bf16[352,256]{1,0:T(8,128)(2,1)S(1)}, u32[]{:S(2)}, u32[]{:S(2)}) collective-permute-start(bf16[352,256]{1,0:T(8,128)(2,1)S(1)} %get-tuple-element.41), channel_id=1, source_target_pairs={{0,8},{8,16},{16,24},{24,32},{32,40},{40,48},{48,56},{56,0},{1,9},... | collective-permute-start | bytes 540680 | tf_op jit(solution)/shard_map/ppermute | solution.py:29
  115.1 8.8 %collective-permute-start.16 = (bf16[352,256]{1,0:T(8,128)(2,1)S(1)}, bf16[352,256]{1,0:T(8,128)(2,1)S(1)}, u32[]{:S(2)}, u32[]{:S(2)}) collective-permute-start(bf16[352,256]{1,0:T(8,128)(2,1)S(1)} %get-tuple-element.42), channel_id=1, source_target_pairs={{0,56},{8,0},{16,8},{24,16},{32,24},{40,32},{48,40},{56,48},{1,57}... | collective-permute-start | bytes 540680 | tf_op jit(solution)/shard_map/ppermute | solution.py:29
  123.9 9.1 %collective-permute-start.17 = (bf16[352,256]{1,0:T(8,128)(2,1)S(1)}, bf16[352,256]{1,0:T(8,128)(2,1)S(1)}, u32[]{:S(2)}, u32[]{:S(2)}) collective-permute-start(bf16[352,256]{1,0:T(8,128)(2,1)S(1)} %get-tuple-element.43), channel_id=1, source_target_pairs={{0,8},{8,16},{16,24},{24,32},{32,40},{40,48},{48,56},{56,0},{1,9},... | collective-permute-start | bytes 540680 | tf_op jit(solution)/shard_map/ppermute | solution.py:29
  125.5 7.5 %collective-permute-start.18 = (bf16[352,256]{1,0:T(8,128)(2,1)S(1)}, bf16[352,256]{1,0:T(8,128)(2,1)}, u32[]{:S(2)}, u32[]{:S(2)}) collective-permute-start(bf16[352,256]{1,0:T(8,128)(2,1)S(1)} %get-tuple-element.44), channel_id=1, source_target_pairs={{0,56},{8,0},{16,8},{24,16},{32,24},{40,32},{48,40},{56,48},{1,57}... | collective-permute-start | bytes 540680 | tf_op jit(solution)/shard_map/ppermute | solution.py:29
  127.2 18.4 %all-to-all-start = ((bf16[8,160,128]{2,1,0:T(8,128)(2,1)}), bf16[8,160,128]{2,1,0:T(8,128)(2,1)}, u32[]{:S(2)}, u32[]{:S(2)}) async-start(bf16[8,160,128]{2,1,0:T(8,128)(2,1)} %bitcast.101), calls=%async_computation.2 | async-start | bytes 655360 | tf_op jit(solution)/shard_map/all_to_all | solution.py:258
  134.0 11.6 %collective-permute-start.20 = (bf16[352,128]{1,0:T(8,128)(2,1)S(1)}, bf16[352,128]{1,0:T(8,128)(2,1)S(1)}, u32[]{:S(2)}, u32[]{:S(2)}) collective-permute-start(bf16[352,128]{1,0:T(8,128)(2,1)S(1)} %select_convert_fusion), channel_id=1, source_target_pairs={{0,1},{1,0},{2,3},{3,2},{4,5},{5,4},{6,7},{7,6},{8,9},{9,8},{10,11... | collective-permute-start | bytes 270344 | tf_op jit(solution)/shard_map/ppermute | solution.py:29
Sparse Core Ops, SparseCore 0:
  19.1 42.3 all-gather.4
  63.3 62.8 all-gather.6
Sparse Core Ops, SparseCore 1:
  26.4 63.2 reduce-scatter.2
  92.6 26.7 reduce-scatter.4

commit v5 on v4

--- a/solution.py
+++ b/solution.py
@@ -11,7 +11,7 @@
 GROUP = 128
 Z, X, Y = 8, 4, 2
 WEIGHT_SPLIT = 256
-GRAD_SPLIT = 352
+GRAD_SPLIT = 336
 F32, BF16 = jnp.float32, jnp.bfloat16
 VMEM_LIMIT = 56 * 1024 * 1024
 
@@ -243,7 +243,7 @@
     new_momentum, new_params = outer_step(exchanged, momentum, params)
 
     grad_a = after(grad_a, new_params)
-    half = GRAD_SPLIT // 2
+    half = GRAD_SPLIT // 32 * 16
     at = grad_a.astype(F32)
     up, down = shift(grad_a[4][:half], "z", 1), shift(grad_a[4][half:], "z", -1)
     up = jnp.concatenate([at[3][:half] + up.astype(F32), at[3][half:]]).astype(BF16)

time: 156 us -> 156 us (level)
  starting transfers between devices: 35.8 us -> 34.2 us
    ppermute x20, waiting for transfers between devices: 51.7 us -> 57 us  [shift(): lax.ppermute(block, axis, [(i, (i + by) % size) for i in range(size)])]
    all_gather x1, waiting for transfers between devices: 4.29 us -> 1.34 us  [local(): weight_c = lax.all_gather(weight_c, 'z')]
    reduce_scatter x1, waiting for transfers between devices: 12.9 us -> 10.9 us  [local(): grad_a = lax.psum_scatter(grad_a, 'x', scatter_dimension=0, tiled=True)[0]]
  transfers between devices with their start and end apart: 26 -> 26, of which waited for: 16 -> 17; matrix products, arithmetic and copies ran while one was open for 7% -> 8% of each run, Pallas kernels for 11% -> 11%
where the time goes in v5:
time: 156 us; the launch traced here: 155 us
  waiting for transfers between devices  74.1 us (47%)
  starting transfers between devices  34.2 us (22%)
  Pallas kernels  16.6 us (11%)
  between operations  15.7 us (10%)
  other arithmetic  9.59 us (6%)
  local copies, waits for them, and re-layouts  4.88 us (3%)
    ppermute x20, waiting for transfers between devices, shift(): lax.ppermute(block, axis, [(i, (i + by) % size) for i in range(size)])  57 us
    ppermute x20, starting transfers between devices, shift(): lax.ppermute(block, axis, [(i, (i + by) % size) for i in range(size)])  29.7 us
    reduce_scatter x1, waiting for transfers between devices, local(): grad_a = lax.psum_scatter(grad_a, 'x', scatter_dimension=0, tiled=True)[0]  10.9 us
    pallas_call x1, Pallas kernels, products(): pl.pallas_call(product_kernel, in_specs=[pl.BlockSpec(memory_space=pltpu....  10 us
    pallas_call x1, Pallas kernels, gradients(): pl.pallas_call(grad_kernel, in_specs=[pl.BlockSpec(memory_space=pltpu.SME...  6.55 us
    ppermute x1, waiting for transfers between devices, outer_values(): far_core = lax.ppermute(values, ('yh', 'c'), [(i, 3 - i) for i in range(4)])  4.78 us
    all_to_all x1, starting transfers between devices, local(): grad_c = lax.all_to_all(after(grad_c_x, up, other_c), 'z', 0, 0, tiled=True)  4.32 us
  transfers between devices with their start and end apart: 26, of which 17 were waited for; matrix products, arithmetic and copies ran while one was open for 8% of the time, Pallas kernels for 11%

profile of v5, /device:TPU:16, one launch (start us, length us, event | category | flops | bytes accessed | tf_op | source)
XLA Modules:
  0.0 155.1 jit_solution(5749087088157989856)
XLA Ops:
  8.0 0.0 all-gather.5.cloned.1.call-start
  8.0 0.9 fusion.18
  8.9 2.8 %collective-permute-start = (bf16[128,256]{1,0:T(8,128)(2,1)S(1)}, bf16[128,256]{1,0:T(8,128)(2,1)S(1)}, u32[]{:S(2)}, u32[]{:S(2)}) collective-permute-start(bf16[128,256]{1,0:T(8,128)(2,1)S(1)} %get-tuple-element.75), channel_id=1, source_target_pairs={{0,6},{2,0},{4,2},{6,4},{1,7},{3,1},{5,3},{7,5},{8,14},{10,8},{12,... | collective-permute-start | bytes 196616 | tf_op jit(solution)/shard_map/ppermute | solution.py:29
  11.8 0.8 collective-permute-start.1
  12.6 0.9 collective-permute-start.2
  13.5 1.3 collective-permute-start.3
  14.7 2.8 %collective-permute-done.1 = bf16[128,256]{1,0:T(8,128)(2,1)S(1)} collective-permute-done((bf16[128,256]{1,0:T(8,128)(2,1)S(1)}, bf16[128,256]{1,0:T(8,128)(2,1)S(1)}, u32[]{:S(2)}, u32[]{:S(2)}) %collective-permute-start.1) | collective-permute-done | bytes 65568 | tf_op jit(solution)/shard_map/ppermute | solution.py:29
  17.6 0.7 collective-permute-done.2
  18.2 0.7 pad_maximum_fusion.1
  19.0 0.0 all-gather.5.cloned.1.call-update
  19.0 0.0 reduce-scatter.3.cloned.1.call-start
  19.1 0.7 pad_add_fusion.place
  19.7 6.6 %shard_map.128 = (bf16[4,8,336,256]{3,2,1,0:T(8,128)(2,1)}, bf16[4,8,176,128]{3,2,1,0:T(8,128)(2,1)}, bf16[4,8,176,128]{3,2,1,0:T(8,128)(2,1)}) custom-call(s32[3]{0:T(128)} %pad_add_fusion.place, bf16[256,8192]{1,0:T(8,128)(2,1)} %bitcast.114, bf16[256,512]{1,0:T(8,128)(2,1)} %bitcast.117), custom_call_target="tpu_custom_call" | custom-call | flops 2147483648 | bytes 12582912 | tf_op jit(solution)/shard_map/pallas_call | solution.py:96
  26.3 0.0 reduce-scatter.5.cloned.1.call-start
  26.4 1.4 collective-permute-start.7
  27.8 1.2 collective-permute-start.4
  29.0 1.5 collective-permute-start.5
  30.5 0.1 collective-permute-start.6
  30.6 2.2 %collective-permute-done.4 = bf16[256,256]{1,0:T(8,128)(2,1)S(1)} collective-permute-done((bf16[256,256]{1,0:T(8,128)(2,1)S(1)}, bf16[256,256]{1,0:T(8,128)(2,1)S(1)}, u32[]{:S(2)}, u32[]{:S(2)}) %collective-permute-start.4) | collective-permute-done | bytes 131104 | tf_op jit(solution)/shard_map/ppermute | solution.py:29
  32.9 2.6 %collective-permute-done.5 = bf16[256,256]{1,0:T(8,128)(2,1)S(1)} collective-permute-done((bf16[256,256]{1,0:T(8,128)(2,1)S(1)}, bf16[256,256]{1,0:T(8,128)(2,1)S(1)}, u32[]{:S(2)}, u32[]{:S(2)}) %collective-permute-start.5) | collective-permute-done | bytes 131104 | tf_op jit(solution)/shard_map/ppermute | solution.py:29
  35.5 1.4 collective-permute-done.6
  36.9 0.9 pad_maximum_fusion
  37.8 20.8 %collective-permute-done.7 = bf16[4,8,176,128]{3,2,1,0:T(8,128)(2,1)S(1)} collective-permute-done((bf16[4,8,176,128]{3,2,1,0:T(8,128)(2,1)}, bf16[4,8,176,128]{3,2,1,0:T(8,128)(2,1)S(1)}, u32[]{:S(2)}, u32[]{:S(2)}) %collective-permute-start.7) | collective-permute-done | bytes 1441824 | tf_op jit(solution)/shard_map/ppermute | solution.py:29
  58.6 1.5 add_convert_fusion
  60.1 0.0 all-gather.7.cloned.1.call-start
  60.2 1.3 all-gather.5.cloned.1.call-done
  61.5 0.2 mul.35
  61.7 0.2 sub.17
  61.9 0.2 add.64
  62.2 0.9 fusion
  63.0 0.1 collective-permute-start.10
  63.1 0.6 collective-permute-start.8
  63.8 3.0 %collective-permute-start.9 = (bf16[16,8192]{1,0:T(8,128)(2,1)S(1)}, bf16[16,8192]{1,0:T(8,128)(2,1)S(1)}, u32[]{:S(2)}, u32[]{:S(2)}) collective-permute-start(bf16[16,8192]{1,0:T(8,128)(2,1)S(1)} %fusion), channel_id=1, source_target_pairs={{0,128},{128,0},{1,129},{129,1},{2,130},{130,2},{3,131},{131,3},{4... | collective-permute-start | bytes 786440 | tf_op jit(solution)/shard_map/ppermute | solution.py:29
  66.8 1.2 collective-permute-start.19
  68.0 4.8 %collective-permute-done.10 = bf16[16,8192]{1,0:T(8,128)(2,1)S(1)} collective-permute-done((bf16[16,8192]{1,0:T(8,128)(2,1)S(1)}, bf16[16,8192]{1,0:T(8,128)(2,1)S(1)}, u32[]{:S(2)}, u32[]{:S(2)}) %collective-permute-start.10) | collective-permute-done | bytes 262176 | tf_op jit(solution)/shard_map/ppermute | solution.py:40
  72.7 2.7 %collective-permute-done.9 = bf16[16,8192]{1,0:T(8,128)(2,1)S(1)} collective-permute-done((bf16[16,8192]{1,0:T(8,128)(2,1)S(1)}, bf16[16,8192]{1,0:T(8,128)(2,1)S(1)}, u32[]{:S(2)}, u32[]{:S(2)}) %collective-permute-start.9) | collective-permute-done | bytes 262176 | tf_op jit(solution)/shard_map/ppermute | solution.py:29
  75.5 1.2 multiply_subtract_fusion
  76.7 10.9 %reduce-scatter.3.cloned.1.call-done = bf16[1,8,336,256]{3,2,1,0:T(8,128)(2,1)} async-done(((bf16[4,8,336,256]{3,2,1,0:T(8,128)(2,1)}), bf16[1,8,336,256]{3,2,1,0:T(8,128)(2,1)}) %reduce-scatter.3.cloned.1.call-update) | async-done | bytes 1376272 | tf_op jit(solution)/shard_map/reduce_scatter | solution.py:225
  87.5 0.9 slice_bitcast_fusion.9
  88.5 1.6 %collective-permute-start.11 = (bf16[160,256]{1,0:T(8,128)(2,1)S(1)}, bf16[160,256]{1,0:T(8,128)(2,1)S(1)}, u32[]{:S(2)}, u32[]{:S(2)}) collective-permute-start(bf16[160,256]{1,0:T(8,128)(2,1)S(1)} %get-tuple-element.66), channel_id=1, source_target_pairs={{0,8},{8,16},{16,24},{24,32},{32,40},{40,48},{48,56},{56,0},{1,9},... | collective-permute-start | bytes 245768 | tf_op jit(solution)/shard_map/ppermute | solution.py:29
  90.1 1.0 slice_bitcast_fusion.7
  91.0 1.6 %convert_element_type.87 = f32[8,336,256]{2,1,0:T(8,128)S(1)} convert(bf16[8,336,256]{2,1,0:T(8,128)(2,1)} %bitcast.97) | non-fusion elementwise | flops 688128 | bytes 4128768 | tf_op jit(solution)/shard_map/convert_element_type | solution.py:247
  92.6 1.9 %collective-permute-start.12 = (bf16[176,256]{1,0:T(8,128)(2,1)S(1)}, bf16[176,256]{1,0:T(8,128)(2,1)S(1)}, u32[]{:S(2)}, u32[]{:S(2)}) collective-permute-start(bf16[176,256]{1,0:T(8,128)(2,1)S(1)} %get-tuple-element.67), channel_id=1, source_target_pairs={{0,56},{8,0},{16,8},{24,16},{32,24},{40,32},{48,40},{56,48},{1,57}... | collective-permute-start | bytes 270344 | tf_op jit(solution)/shard_map/ppermute | solution.py:29
  94.5 2.1 %collective-permute-done.11 = bf16[160,256]{1,0:T(8,128)(2,1)S(1)} collective-permute-done((bf16[160,256]{1,0:T(8,128)(2,1)S(1)}, bf16[160,256]{1,0:T(8,128)(2,1)S(1)}, u32[]{:S(2)}, u32[]{:S(2)}) %collective-permute-start.11) | collective-permute-done | bytes 81952 | tf_op jit(solution)/shard_map/ppermute | solution.py:29
  96.6 3.0 %collective-permute-done.12 = bf16[176,256]{1,0:T(8,128)(2,1)S(1)} collective-permute-done((bf16[176,256]{1,0:T(8,128)(2,1)S(1)}, bf16[176,256]{1,0:T(8,128)(2,1)S(1)}, u32[]{:S(2)}, u32[]{:S(2)}) %collective-permute-start.12) | collective-permute-done | bytes 90144 | tf_op jit(solution)/shard_map/ppermute | solution.py:29
  99.7 1.6 %collective-permute-start.13 = (bf16[336,256]{1,0:T(8,128)(2,1)S(1)}, bf16[336,256]{1,0:T(8,128)(2,1)S(1)}, u32[]{:S(2)}, u32[]{:S(2)}) collective-permute-start(bf16[336,256]{1,0:T(8,128)(2,1)S(1)} %pad_maximum_fusion.2), channel_id=1, source_target_pairs={{0,8},{8,16},{16,24},{24,32},{32,40},{40,48},{48,56},{56,0},{1,9},... | collective-permute-start | bytes 516104 | tf_op jit(solution)/shard_map/ppermute | solution.py:29
  101.3 1.7 %collective-permute-start.14 = (bf16[336,256]{1,0:T(8,128)(2,1)S(1)}, bf16[336,256]{1,0:T(8,128)(2,1)S(1)}, u32[]{:S(2)}, u32[]{:S(2)}) collective-permute-start(bf16[336,256]{1,0:T(8,128)(2,1)S(1)} %pad_maximum_fusion.3), channel_id=1, source_target_pairs={{0,56},{8,0},{16,8},{24,16},{32,24},{40,32},{48,40},{56,48},{1,57}... | collective-permute-start | bytes 516104 | tf_op jit(solution)/shard_map/ppermute | solution.py:29
  103.0 8.1 %collective-permute-done.13 = bf16[336,256]{1,0:T(8,128)(2,1)S(1)} collective-permute-done((bf16[336,256]{1,0:T(8,128)(2,1)S(1)}, bf16[336,256]{1,0:T(8,128)(2,1)S(1)}, u32[]{:S(2)}, u32[]{:S(2)}) %collective-permute-start.13) | collective-permute-done | bytes 172064 | tf_op jit(solution)/shard_map/ppermute | solution.py:29
  111.1 0.6 collective-permute-done.14
  111.7 0.1 fusion.6
  111.8 3.3 %collective-permute-start.15 = (bf16[336,256]{1,0:T(8,128)(2,1)S(1)}, bf16[336,256]{1,0:T(8,128)(2,1)S(1)}, u32[]{:S(2)}, u32[]{:S(2)}) collective-permute-start(bf16[336,256]{1,0:T(8,128)(2,1)S(1)} %get-tuple-element.41), channel_id=1, source_target_pairs={{0,8},{8,16},{16,24},{24,32},{32,40},{40,48},{48,56},{56,0},{1,9},... | collective-permute-start | bytes 516104 | tf_op jit(solution)/shard_map/ppermute | solution.py:29
  115.2 7.9 %collective-permute-done.15 = bf16[336,256]{1,0:T(8,128)(2,1)S(1)} collective-permute-done((bf16[336,256]{1,0:T(8,128)(2,1)S(1)}, bf16[336,256]{1,0:T(8,128)(2,1)S(1)}, u32[]{:S(2)}, u32[]{:S(2)}) %collective-permute-start.15) | collective-permute-done | bytes 172064 | tf_op jit(solution)/shard_map/ppermute | solution.py:29
  123.0 2.0 %collective-permute-done.16 = bf16[336,256]{1,0:T(8,128)(2,1)S(1)} collective-permute-done((bf16[336,256]{1,0:T(8,128)(2,1)S(1)}, bf16[336,256]{1,0:T(8,128)(2,1)S(1)}, u32[]{:S(2)}, u32[]{:S(2)}) %collective-permute-start.16) | collective-permute-done | bytes 172064 | tf_op jit(solution)/shard_map/ppermute | solution.py:29
  125.0 0.8 fusion.4
  125.8 1.8 %collective-permute-start.17 = (bf16[336,256]{1,0:T(8,128)(2,1)}, bf16[336,256]{1,0:T(8,128)(2,1)S(1)}, u32[]{:S(2)}, u32[]{:S(2)}) collective-permute-start(bf16[336,256]{1,0:T(8,128)(2,1)} %get-tuple-element.43), channel_id=1, source_target_pairs={{0,8},{8,16},{16,24},{24,32},{32,40},{40,48},{48,56},{56,0},{1,9},... | collective-permute-start | bytes 516104 | tf_op jit(solution)/shard_map/ppermute | solution.py:29
  127.6 1.4 collective-permute-start.18
  129.0 4.3 %all-to-all-start = ((bf16[8,176,128]{2,1,0:T(8,128)(2,1)}), bf16[8,176,128]{2,1,0:T(8,128)(2,1)S(1)}, u32[]{:S(2)}, u32[]{:S(2)}) async-start(bf16[8,176,128]{2,1,0:T(8,128)(2,1)} %bitcast.102), calls=%async_computation.2 | async-start | bytes 720896 | tf_op jit(solution)/shard_map/all_to_all | solution.py:258
  133.3 0.7 copy-done.5
  134.0 0.1 collective-permute-done.18
  134.1 1.0 fusion.11
  135.2 1.5 collective-permute-start.20
  136.7 10.0 %shard_map.129 = (bf16[256,512]{1,0:T(8,128)(2,1)}, bf16[256,8192]{1,0:T(8,128)(2,1)}) custom-call(s32[3]{0:T(128)} %pad_add_fusion.place, bf16[256,8192]{1,0:T(8,128)(2,1)} %bitcast.115, bf16[256,512]{1,0:T(8,128)(2,1)} %bitcast.118, bf16[8,4,256,256]{3,2,1,0:T(8,128)(2,1)} %bitcast.116, bf16[8,4,128,256]{3,2,1,0:T(8,128)(2,1)} %bitcast.14.weight_c, ...), custom_call_target="tpu_custom_call" | custom-call | flops 4294967296 | bytes 16777216 | tf_op jit(solution)/shard_map/pallas_call | solution.py:176
  146.8 0.1 convert_reduce_fusion
  146.9 0.8 copy.15
  (39 shorter events, 0.3 us)
Async XLA Ops:
  8.0 53.5 %all-gather.5.cloned.1.call-start = ((), (), s32[]{:S(2)}) async-start(), calls=%async_computation.5 | async-start | bytes 2359296 | tf_op jit(solution)/shard_map/all_gather | solution.py:222
  8.9 5.8 %collective-permute-start = (bf16[128,256]{1,0:T(8,128)(2,1)S(1)}, bf16[128,256]{1,0:T(8,128)(2,1)S(1)}, u32[]{:S(2)}, u32[]{:S(2)}) collective-permute-start(bf16[128,256]{1,0:T(8,128)(2,1)S(1)} %get-tuple-element.75), channel_id=1, source_target_pairs={{0,6},{2,0},{4,2},{6,4},{1,7},{3,1},{5,3},{7,5},{8,14},{10,8},{12,... | collective-permute-start | bytes 196616 | tf_op jit(solution)/shard_map/ppermute | solution.py:29
  11.8 5.8 %collective-permute-start.1 = (bf16[128,256]{1,0:T(8,128)(2,1)S(1)}, bf16[128,256]{1,0:T(8,128)(2,1)S(1)}, u32[]{:S(2)}, u32[]{:S(2)}) collective-permute-start(bf16[128,256]{1,0:T(8,128)(2,1)S(1)} %get-tuple-element.75), channel_id=1, source_target_pairs={{0,4},{2,6},{4,0},{6,2},{1,5},{3,7},{5,1},{7,3},{8,12},{10,14},{12... | collective-permute-start | bytes 196616 | tf_op jit(solution)/shard_map/ppermute | solution.py:29
  12.6 5.7 %collective-permute-start.2 = (bf16[128,256]{1,0:T(8,128)(2,1)S(1)}, bf16[128,256]{1,0:T(8,128)(2,1)S(1)}, u32[]{:S(2)}, u32[]{:S(2)}) collective-permute-start(bf16[128,256]{1,0:T(8,128)(2,1)S(1)} %get-tuple-element.75), channel_id=1, source_target_pairs={{0,2},{2,4},{4,6},{6,0},{1,3},{3,5},{5,7},{7,1},{8,10},{10,12},{12... | collective-permute-start | bytes 196616 | tf_op jit(solution)/shard_map/ppermute | solution.py:29
  13.5 5.5 %collective-permute-start.3 = (bf16[128,256]{1,0:T(8,128)(2,1)S(1)}, bf16[128,256]{1,0:T(8,128)(2,1)S(1)}, u32[]{:S(2)}, u32[]{:S(2)}) collective-permute-start(bf16[128,256]{1,0:T(8,128)(2,1)S(1)} %get-tuple-element.73), channel_id=1, source_target_pairs={{0,1},{1,0},{2,3},{3,2},{4,5},{5,4},{6,7},{7,6},{8,9},{9,8},{10,11... | collective-permute-start | bytes 196616 | tf_op jit(solution)/shard_map/ppermute | solution.py:29
  19.0 68.5 %reduce-scatter.3.cloned.1.call-start = ((), (), s32[]{:S(2)}) async-start(), calls=%async_computation.3 | async-start | bytes 6881280 | tf_op jit(solution)/shard_map/reduce_scatter | solution.py:225
  26.3 1.5 copy-start.4
  26.3 32.3 %copy-start = (bf16[4,8,176,128]{3,2,1,0:T(8,128)(2,1)S(1)}, bf16[4,8,176,128]{3,2,1,0:T(8,128)(2,1)}, u32[]{:S(2)}) copy-start(bf16[4,8,176,128]{3,2,1,0:T(8,128)(2,1)} %get-tuple-element.32) | copy-start | bytes 4325380
  26.3 102.7 %reduce-scatter.5.cloned.1.call-start = ((), (), s32[]{:S(2)}) async-start(), calls=%async_computation.4 | async-start | bytes 1802240 | tf_op jit(solution)/shard_map/reduce_scatter | solution.py:235
  26.4 32.2 %collective-permute-start.7 = (bf16[4,8,176,128]{3,2,1,0:T(8,128)(2,1)}, bf16[4,8,176,128]{3,2,1,0:T(8,128)(2,1)S(1)}, u32[]{:S(2)}, u32[]{:S(2)}) collective-permute-start(bf16[4,8,176,128]{3,2,1,0:T(8,128)(2,1)} %get-tuple-element.30), channel_id=1, source_target_pairs={{0,1},{1,0},{2,3},{3,2},{4,5},{5,4},{6,7},{7,6},{8,9},{9,8},{10,11... | collective-permute-start | bytes 4325384 | tf_op jit(solution)/shard_map/ppermute | solution.py:29
  27.8 5.0 %collective-permute-start.4 = (bf16[256,256]{1,0:T(8,128)(2,1)S(1)}, bf16[256,256]{1,0:T(8,128)(2,1)S(1)}, u32[]{:S(2)}, u32[]{:S(2)}) collective-permute-start(bf16[256,256]{1,0:T(8,128)(2,1)S(1)} %get-tuple-element.72), channel_id=1, source_target_pairs={{0,6},{2,0},{4,2},{6,4},{1,7},{3,1},{5,3},{7,5},{8,14},{10,8},{12,... | collective-permute-start | bytes 393224 | tf_op jit(solution)/shard_map/ppermute | solution.py:29
  29.0 6.5 %collective-permute-start.5 = (bf16[256,256]{1,0:T(8,128)(2,1)S(1)}, bf16[256,256]{1,0:T(8,128)(2,1)S(1)}, u32[]{:S(2)}, u32[]{:S(2)}) collective-permute-start(bf16[256,256]{1,0:T(8,128)(2,1)S(1)} %get-tuple-element.72), channel_id=1, source_target_pairs={{0,4},{2,6},{4,0},{6,2},{1,5},{3,7},{5,1},{7,3},{8,12},{10,14},{12... | collective-permute-start | bytes 393224 | tf_op jit(solution)/shard_map/ppermute | solution.py:29
  30.5 6.4 %collective-permute-start.6 = (bf16[256,256]{1,0:T(8,128)(2,1)S(1)}, bf16[256,256]{1,0:T(8,128)(2,1)S(1)}, u32[]{:S(2)}, u32[]{:S(2)}) collective-permute-start(bf16[256,256]{1,0:T(8,128)(2,1)S(1)} %get-tuple-element.72), channel_id=1, source_target_pairs={{0,2},{2,4},{4,6},{6,0},{1,3},{3,5},{5,7},{7,1},{8,10},{10,12},{12... | collective-permute-start | bytes 393224 | tf_op jit(solution)/shard_map/ppermute | solution.py:29
  58.6 2.9 %copy-start.6 = (f32[1,16,64]{2,1,0:T(8,128)S(1)}, f32[1,16,64]{2,1,0:T(8,128)}, u32[]{:S(2)}) copy-start(f32[1,16,64]{2,1,0:T(8,128)} %param.15) | copy-start | bytes 12292
  58.6 3.1 %copy-start.7 = (s32[1,16,64]{2,1,0:T(8,128)S(1)}, s32[1,16,64]{2,1,0:T(8,128)}, u32[]{:S(2)}) copy-start(s32[1,16,64]{2,1,0:T(8,128)} %param.13) | copy-start | bytes 12292
  58.6 3.3 %copy-start.8 = (f32[1,16,64]{2,1,0:T(8,128)S(1)}, f32[1,16,64]{2,1,0:T(8,128)}, u32[]{:S(2)}) copy-start(f32[1,16,64]{2,1,0:T(8,128)} %param.14) | copy-start | bytes 12292
  60.1 2.1 %copy-start.1 = (s32[1,16,8192]{2,1,0:T(8,128)S(1)}, s32[1,16,8192]{2,1,0:T(8,128)}, u32[]{:S(2)}) copy-start(s32[1,16,8192]{2,1,0:T(8,128)} %param.12) | copy-start | bytes 1572868
  60.1 15.4 %copy-start.2 = (f32[16,8192]{1,0:T(8,128)S(1)}, f32[16,8192]{1,0:T(8,128)}, u32[]{:S(2)}) copy-start(f32[16,8192]{1,0:T(8,128)} %param.17) | copy-start | bytes 1572868
  60.1 15.4 %copy-start.3 = (f32[16,8192]{1,0:T(8,128)S(1)}, f32[16,8192]{1,0:T(8,128)}, u32[]{:S(2)}) copy-start(f32[16,8192]{1,0:T(8,128)} %param.16) | copy-start | bytes 1572868
  60.1 76.6 %all-gather.7.cloned.1.call-start = ((), (), s32[]{:S(2)}) async-start(), calls=%async_computation.6 | async-start | bytes 4718592 | tf_op jit(solution)/shard_map/all_gather | solution.py:238
  63.0 9.7 %collective-permute-start.10 = (bf16[16,8192]{1,0:T(8,128)(2,1)S(1)}, bf16[16,8192]{1,0:T(8,128)(2,1)S(1)}, u32[]{:S(2)}, u32[]{:S(2)}) collective-permute-start(bf16[16,8192]{1,0:T(8,128)(2,1)S(1)} %fusion), channel_id=1, source_target_pairs={{0,192},{64,128},{128,64},{192,0},{1,193},{65,129},{129,65},{193,1... | collective-permute-start | bytes 786440 | tf_op jit(solution)/shard_map/ppermute | solution.py:40
  63.1 9.6 %collective-permute-start.8 = (bf16[16,8192]{1,0:T(8,128)(2,1)S(1)}, bf16[16,8192]{1,0:T(8,128)(2,1)S(1)}, u32[]{:S(2)}, u32[]{:S(2)}) collective-permute-start(bf16[16,8192]{1,0:T(8,128)(2,1)S(1)} %fusion), channel_id=1, source_target_pairs={{0,64},{64,0},{1,65},{65,1},{2,66},{66,2},{3,67},{67,3},{4,68},{68... | collective-permute-start | bytes 786440 | tf_op jit(solution)/shard_map/ppermute | solution.py:29
  63.8 11.7 %collective-permute-start.9 = (bf16[16,8192]{1,0:T(8,128)(2,1)S(1)}, bf16[16,8192]{1,0:T(8,128)(2,1)S(1)}, u32[]{:S(2)}, u32[]{:S(2)}) collective-permute-start(bf16[16,8192]{1,0:T(8,128)(2,1)S(1)} %fusion), channel_id=1, source_target_pairs={{0,128},{128,0},{1,129},{129,1},{2,130},{130,2},{3,131},{131,3},{4... | collective-permute-start | bytes 786440 | tf_op jit(solution)/shard_map/ppermute | solution.py:29
  66.8 62.2 %collective-permute-start.19 = (bf16[8,4,128,256]{3,2,1,0:T(8,128)(2,1)}, bf16[8,4,128,256]{3,2,1,0:T(8,128)(2,1)}, u32[]{:S(2)}, u32[]{:S(2)}) collective-permute-start(bf16[8,4,128,256]{3,2,1,0:T(8,128)(2,1)} %bitcast.14.weight_c), channel_id=1, source_target_pairs={{0,1},{1,0},{2,3},{3,2},{4,5},{5,4},{6,7},{7,6},{8,9},{9,8},{10,11... | collective-permute-start | bytes 6291464 | tf_op jit(solution)/shard_map/ppermute | solution.py:29
  88.5 8.1 %collective-permute-start.11 = (bf16[160,256]{1,0:T(8,128)(2,1)S(1)}, bf16[160,256]{1,0:T(8,128)(2,1)S(1)}, u32[]{:S(2)}, u32[]{:S(2)}) collective-permute-start(bf16[160,256]{1,0:T(8,128)(2,1)S(1)} %get-tuple-element.66), channel_id=1, source_target_pairs={{0,8},{8,16},{16,24},{24,32},{32,40},{40,48},{48,56},{56,0},{1,9},... | collective-permute-start | bytes 245768 | tf_op jit(solution)/shard_map/ppermute | solution.py:29
  92.6 7.0 %collective-permute-start.12 = (bf16[176,256]{1,0:T(8,128)(2,1)S(1)}, bf16[176,256]{1,0:T(8,128)(2,1)S(1)}, u32[]{:S(2)}, u32[]{:S(2)}) collective-permute-start(bf16[176,256]{1,0:T(8,128)(2,1)S(1)} %get-tuple-element.67), channel_id=1, source_target_pairs={{0,56},{8,0},{16,8},{24,16},{32,24},{40,32},{48,40},{56,48},{1,57}... | collective-permute-start | bytes 270344 | tf_op jit(solution)/shard_map/ppermute | solution.py:29
  99.7 11.5 %collective-permute-start.13 = (bf16[336,256]{1,0:T(8,128)(2,1)S(1)}, bf16[336,256]{1,0:T(8,128)(2,1)S(1)}, u32[]{:S(2)}, u32[]{:S(2)}) collective-permute-start(bf16[336,256]{1,0:T(8,128)(2,1)S(1)} %pad_maximum_fusion.2), channel_id=1, source_target_pairs={{0,8},{8,16},{16,24},{24,32},{32,40},{40,48},{48,56},{56,0},{1,9},... | collective-permute-start | bytes 516104 | tf_op jit(solution)/shard_map/ppermute | solution.py:29
  101.3 10.4 %collective-permute-start.14 = (bf16[336,256]{1,0:T(8,128)(2,1)S(1)}, bf16[336,256]{1,0:T(8,128)(2,1)S(1)}, u32[]{:S(2)}, u32[]{:S(2)}) collective-permute-start(bf16[336,256]{1,0:T(8,128)(2,1)S(1)} %pad_maximum_fusion.3), channel_id=1, source_target_pairs={{0,56},{8,0},{16,8},{24,16},{32,24},{40,32},{48,40},{56,48},{1,57}... | collective-permute-start | bytes 516104 | tf_op jit(solution)/shard_map/ppermute | solution.py:29
  111.8 11.2 %collective-permute-start.15 = (bf16[336,256]{1,0:T(8,128)(2,1)S(1)}, bf16[336,256]{1,0:T(8,128)(2,1)S(1)}, u32[]{:S(2)}, u32[]{:S(2)}) collective-permute-start(bf16[336,256]{1,0:T(8,128)(2,1)S(1)} %get-tuple-element.41), channel_id=1, source_target_pairs={{0,8},{8,16},{16,24},{24,32},{32,40},{40,48},{48,56},{56,0},{1,9},... | collective-permute-start | bytes 516104 | tf_op jit(solution)/shard_map/ppermute | solution.py:29
  115.2 9.8 %collective-permute-start.16 = (bf16[336,256]{1,0:T(8,128)(2,1)S(1)}, bf16[336,256]{1,0:T(8,128)(2,1)S(1)}, u32[]{:S(2)}, u32[]{:S(2)}) collective-permute-start(bf16[336,256]{1,0:T(8,128)(2,1)S(1)} %get-tuple-element.42), channel_id=1, source_target_pairs={{0,56},{8,0},{16,8},{24,16},{32,24},{40,32},{48,40},{56,48},{1,57}... | collective-permute-start | bytes 516104 | tf_op jit(solution)/shard_map/ppermute | solution.py:29
  125.8 7.6 %collective-permute-start.17 = (bf16[336,256]{1,0:T(8,128)(2,1)}, bf16[336,256]{1,0:T(8,128)(2,1)S(1)}, u32[]{:S(2)}, u32[]{:S(2)}) collective-permute-start(bf16[336,256]{1,0:T(8,128)(2,1)} %get-tuple-element.43), channel_id=1, source_target_pairs={{0,8},{8,16},{16,24},{24,32},{32,40},{40,48},{48,56},{56,0},{1,9},... | collective-permute-start | bytes 516104 | tf_op jit(solution)/shard_map/ppermute | solution.py:29
  127.6 6.5 %collective-permute-start.18 = (bf16[336,256]{1,0:T(8,128)(2,1)S(1)}, bf16[336,256]{1,0:T(8,128)(2,1)}, u32[]{:S(2)}, u32[]{:S(2)}) collective-permute-start(bf16[336,256]{1,0:T(8,128)(2,1)S(1)} %get-tuple-element.44), channel_id=1, source_target_pairs={{0,56},{8,0},{16,8},{24,16},{32,24},{40,32},{48,40},{56,48},{1,57}... | collective-permute-start | bytes 516104 | tf_op jit(solution)/shard_map/ppermute | solution.py:29
  129.0 17.8 %all-to-all-start = ((bf16[8,176,128]{2,1,0:T(8,128)(2,1)}), bf16[8,176,128]{2,1,0:T(8,128)(2,1)S(1)}, u32[]{:S(2)}, u32[]{:S(2)}) async-start(bf16[8,176,128]{2,1,0:T(8,128)(2,1)} %bitcast.102), calls=%async_computation.2 | async-start | bytes 720896 | tf_op jit(solution)/shard_map/all_to_all | solution.py:258
  133.3 0.7 copy-start.5
  135.2 11.5 %collective-permute-start.20 = (bf16[336,128]{1,0:T(8,128)(2,1)S(1)}, bf16[336,128]{1,0:T(8,128)(2,1)S(1)}, u32[]{:S(2)}, u32[]{:S(2)}) collective-permute-start(bf16[336,128]{1,0:T(8,128)(2,1)S(1)} %select_convert_fusion), channel_id=1, source_target_pairs={{0,1},{1,0},{2,3},{3,2},{4,5},{5,4},{6,7},{7,6},{8,9},{9,8},{10,11... | collective-permute-start | bytes 258056 | tf_op jit(solution)/shard_map/ppermute | solution.py:29
Sparse Core Ops, SparseCore 0:
  19.1 42.3 all-gather.4
  63.3 65.5 all-gather.6
Sparse Core Ops, SparseCore 1:
  26.4 61.0 reduce-scatter.2
  90.5 27.2 reduce-scatter.4
